TPU v7x, 512 devices: a whole 4x4x16 slice. The times are simulated.
512 devices in a mesh: dp: 16 (over x, y), ctx: 32 (over z, core).
Axes of the slice: x: 4, y: 4, z: 16, core: 2. Of those that a mesh axis runs over, the one named last changes fastest.
Arguments:
- inputs: bfloat16 [16, 4096, 2560], P('dp', 'ctx'), may hold values from -6 to 6
- in_keys: bfloat16 [16, 4096, 128], P('dp', 'ctx'), may hold values from -6 to 6
- output_queries: bfloat16 [16, 4096, 128], P('dp', 'ctx'), may hold values from -0.5 to 0.5
- step_raw: float32 [16, 4096, 40], P('dp', 'ctx'), may hold values from -9 to 18
- decay_log: float32 [40], replicated, may hold values from -12 to 4
- skip_weight: float32 [40], replicated, may hold values from 0.5 to 1.5
- grad_out: bfloat16 [16, 4096, 2560], P('dp', 'ctx')
Outputs:
- grad_inputs: bfloat16 [16, 4096, 2560], P('dp', 'ctx')
- grad_keys: float32 [16, 4096, 128], P('dp', 'ctx')
- grad_queries: float32 [16, 4096, 128], P('dp', 'ctx')
- grad_steps: float32 [16, 4096, 40], P('dp', 'ctx')
- grad_decay: float32 [40], replicated
- grad_skip: float32 [40], replicated
All inputs are finite; a program needn't handle non-finite values.
Results may differ from a plain program's by a relative error of at most 0.0035.
Values sent between devices are 32-bit elements; how exact they have to be, the bound alone decides.
No kernel may reach another device: no remote copies, remote signals or barrier semaphores. Data moves between devices by JAX's collectives and lax.ppermute only.
A program may use at most 128 MiB of HBM per device.

v0:
```python
import jax
import jax.numpy as jnp
from jax import lax
from jax.sharding import PartitionSpec as P

HEAD_BLOCK = 8


HIGHEST_PRECISION = lax.Precision.HIGHEST


def carried_in(part, axis, combine, identity, reverse):
    count = lax.axis_size(axis)
    place = lax.axis_index(axis)
    ahead = count - 1 - place if reverse else place
    gathered = jax.tree.map(lambda a: lax.all_gather(a, axis), part)
    state = jax.tree.map(lambda a, e: jnp.zeros_like(a) + jnp.asarray(e, a.dtype), part, identity)

    def one(step, state):
        source = count - 1 - step if reverse else step
        return combine(
            state, jax.tree.map(lambda a: lax.dynamic_index_in_dim(a, source, 0, False), gathered)
        )

    return lax.fori_loop(0, ahead, one, state)


def combine_states(earlier, later):
    early_decay, early_state = earlier
    late_decay, late_state = later
    return (early_decay * late_decay, early_state * late_decay[:, None, None] + late_state)


def block_summaries(inputs_block, cotangent_block, cumulative, step_block, keys_f, queries_f):
    closing_segment = cumulative[-1]
    weighted = (jnp.exp(closing_segment[None, :] - cumulative) * step_block)[
        :, :, None
    ] * inputs_block
    own_state = jnp.einsum("jhp,jn->hpn", weighted, keys_f, precision=HIGHEST_PRECISION)
    lifted = jnp.exp(cumulative)[:, :, None] * cotangent_block
    own_message = jnp.einsum("ihp,in->hpn", lifted, queries_f, precision=HIGHEST_PRECISION)
    return (jnp.exp(closing_segment), own_state, own_message)


def block_gradients(
    inputs_block,
    cotangent_block,
    inputs_raw,
    cotangent_raw,
    cumulative,
    step_block,
    raw_block,
    rate_block,
    skip_block,
    keys_f,
    queries_f,
    scores,
    causal,
    entering_memory,
    message_in,
):
    closing_segment = cumulative[-1]
    cumulative_t = cumulative.T
    between = cumulative_t[:, :, None] - cumulative_t[:, None, :]
    segment_decay = jnp.exp(jnp.where(causal[None, :, :], between, -jnp.inf))
    products = jnp.einsum(
        "ihp,jhp->hij", cotangent_raw, inputs_raw, preferred_element_type=jnp.float32
    )
    weighted = segment_decay * products
    kernel = segment_decay * scores[None, :, :]
    weighted_scores = weighted * scores[None, :, :]
    tail_decay = jnp.exp(closing_segment[None, :] - cumulative)
    lead_decay = jnp.exp(cumulative)
    message_keys = jnp.einsum("tn,hpn->thp", keys_f, message_in, precision=HIGHEST_PRECISION)
    state_queries = jnp.einsum(
        "tn,hpn->thp", queries_f, entering_memory, precision=HIGHEST_PRECISION
    )
    adjoint_keys = jnp.einsum("hit,ihp->thp", kernel, cotangent_block, precision=HIGHEST_PRECISION)
    adjoint_keys = adjoint_keys + tail_decay[:, :, None] * message_keys
    grad_block = step_block[:, :, None] * adjoint_keys + skip_block[None, :, None] * cotangent_block
    rows_keys = jnp.einsum("th,hit->ti", step_block, weighted, precision=HIGHEST_PRECISION)
    rows_queries = jnp.einsum("htj,jh->tj", weighted, step_block, precision=HIGHEST_PRECISION)
    grad_keys = jnp.dot(rows_keys, queries_f, precision=HIGHEST_PRECISION)
    grad_keys = grad_keys + jnp.einsum(
        "thp,hpn->tn",
        (step_block * tail_decay)[:, :, None] * inputs_block,
        message_in,
        precision=HIGHEST_PRECISION,
    )
    grad_queries = jnp.dot(rows_queries, keys_f, precision=HIGHEST_PRECISION)
    grad_queries = grad_queries + jnp.einsum(
        "thp,hpn->tn",
        lead_decay[:, :, None] * cotangent_block,
        entering_memory,
        precision=HIGHEST_PRECISION,
    )
    inward = lead_decay * jnp.sum(cotangent_block * state_queries, axis=2)
    outward = tail_decay * step_block * jnp.sum(inputs_block * message_keys, axis=2)
    meeting = jnp.exp(closing_segment) * jnp.sum(message_in * entering_memory, axis=(1, 2))
    row_part = jnp.einsum("hij,jh->ih", weighted_scores, step_block, precision=HIGHEST_PRECISION)
    column_part = jnp.sum(weighted_scores, axis=1).T * step_block
    through = row_part - column_part + inward - outward
    through = through.at[-1].add(jnp.sum(outward, axis=0) + meeting)
    grad_cumulative = jnp.cumsum(through[::-1], axis=0)[::-1]
    grad_step = grad_cumulative * rate_block[None, :] + jnp.sum(inputs_block * adjoint_keys, axis=2)
    grad_raw = grad_step * jax.nn.sigmoid(raw_block)
    grad_rate_log = jnp.sum(grad_cumulative * step_block, axis=0) * rate_block
    return (grad_block, grad_keys, grad_queries, grad_raw, grad_rate_log)


def per_device(inputs, in_keys, output_queries, step_raw, decay_log, skip_weight, grad_out):
    row_count = inputs.shape[1]
    head_count = decay_log.shape[0]
    head_width = inputs.shape[2] // head_count
    state_width = in_keys.shape[2]
    inputs_all = inputs[0].reshape(row_count, head_count, head_width)
    cotangent_all = grad_out[0].reshape(row_count, head_count, head_width)
    keys_f = in_keys[0].astype(jnp.float32)
    queries_f = output_queries[0].astype(jnp.float32)
    raw_steps = step_raw[0]
    step_widths = jax.nn.softplus(raw_steps)
    decay_rates = -jnp.exp(decay_log)
    cumulative = jnp.cumsum(step_widths * decay_rates[None, :], axis=0)
    scores = jnp.dot(output_queries[0], in_keys[0].T, preferred_element_type=jnp.float32)
    token_place = jnp.arange(row_count)
    causal = token_place[:, None] >= token_place[None, :]
    skip_part = jnp.einsum(
        "thp,thp->h", cotangent_all, inputs_all, preferred_element_type=jnp.float32
    )
    starts = list(range(0, head_count, HEAD_BLOCK))

    def sequence_pieces(offset):
        stop = offset + HEAD_BLOCK
        return (
            inputs_all[:, offset:stop].astype(jnp.float32),
            cotangent_all[:, offset:stop].astype(jnp.float32),
            cumulative[:, offset:stop],
            step_widths[:, offset:stop],
        )

    results = []
    summaries = [block_summaries(*sequence_pieces(offset), keys_f, queries_f) for offset in starts]
    decays = jnp.concatenate([entry[0] for entry in summaries], axis=0)
    own_states = jnp.concatenate([entry[1] for entry in summaries], axis=0)
    own_messages = jnp.concatenate([entry[2] for entry in summaries], axis=0)
    identity = (
        jnp.ones((head_count,), jnp.float32),
        jnp.zeros((head_count, head_width, state_width), jnp.float32),
    )
    carried = carried_in((decays, own_states), "ctx", combine_states, identity, False)
    returned = carried_in((decays, own_messages), "ctx", combine_states, identity, True)
    for offset in starts:
        stop = offset + HEAD_BLOCK
        entering_memory = carried[1][offset:stop]
        message_in = returned[1][offset:stop]
        finish_stop = offset + HEAD_BLOCK
        inputs_block, cotangent_block, cumulative_block, step_block = sequence_pieces(offset)
        results.append(
            block_gradients(
                inputs_block,
                cotangent_block,
                inputs_all[:, offset:finish_stop],
                cotangent_all[:, offset:finish_stop],
                cumulative_block,
                step_block,
                raw_steps[:, offset:finish_stop],
                decay_rates[offset:finish_stop],
                skip_weight[offset:finish_stop],
                keys_f,
                queries_f,
                scores,
                causal,
                entering_memory,
                message_in,
            )
        )
    grad_inputs = jnp.concatenate([entry[0] for entry in results], axis=1)
    grad_inputs = grad_inputs.reshape(1, row_count, head_count * head_width).astype(jnp.bfloat16)
    grad_keys = results[0][1]
    grad_queries = results[0][2]
    for entry in results[1:]:
        grad_keys = grad_keys + entry[1]
        grad_queries = grad_queries + entry[2]
    grad_steps = jnp.concatenate([entry[3] for entry in results], axis=1)
    rate_part = jnp.concatenate([entry[4] for entry in results], axis=0)
    grad_decay, grad_skip = lax.psum((rate_part, skip_part), ("dp", "ctx"))
    return (
        grad_inputs,
        grad_keys[None],
        grad_queries[None],
        grad_steps[None],
        grad_decay,
        grad_skip,
    )


def solution(mesh):
    placed = (
        P("dp", "ctx", None),
        P("dp", "ctx", None),
        P("dp", "ctx", None),
        P("dp", "ctx", None),
        P(),
        P(),
        P("dp", "ctx", None),
    )
    return jax.shard_map(
        per_device,
        mesh=mesh,
        in_specs=placed,
        out_specs=(
            P("dp", "ctx", None),
            P("dp", "ctx", None),
            P("dp", "ctx", None),
            P("dp", "ctx", None),
            P(),
            P(),
        ),
        check_vma=False,
    )
```

profile of v0, /device:TPU:1, one launch (start us, length us, event | category | flops | bytes accessed | tf_op | source)
XLA Modules:
  0.0 745.5 jit_solution(16705665960690249820)
XLA Ops:
  12.0 1.1 copy-done.8
  13.2 1.3 dynamic-slice.40
  15.5 57.8 %all-reduce = f32[1280]{0:T(1024)S(1)} all-reduce(f32[1280]{0:T(1024)S(1)} %dynamic-update-slice.15), channel_id=2, replica_groups=mesh['dp'=16,'ctx'=32] {'ctx'}, use_global_device_ids=true, to_apply=%add | all-reduce | flops 1280 | bytes 10240
  73.9 179.6 %all-gather.6.cloned.1.call-done = f32[1280,64,128]{2,1,0:T(8,128)} async-done(((f32[40,64,128]{2,1,0:T(8,128)}), f32[1280,64,128]{2,1,0:T(8,128)}) %all-gather.6.cloned.1.call-update) | async-done | bytes 41943056 | tf_op jit(solution)/shard_map/all_gather | solution.py:16
  253.7 49.0 %while.31 = (s32[]{:T(128)}, f32[40,64,128]{2,1,0:T(8,128)S(1)}, s32[]{:T(128)}, f32[32,40]{1,0:T(8,128)S(1)}, f32[32,40,64,128]{3,2,1,0:T(8,128)}, /*index=5*/s32[]{:T(128)}, s32[]{:T(128)}, s32[]{:T(128)}, s32[]{:T(128)}) while((s32[]{:T(128)}, f32[40,64,128]{2,1,0:T(8,128)S(1)}, s32[]{:T(128)}, f32[32,40]{1,0:T(8,128)S(1)}, ...), condition=%wide.region_2.3_spmd, body=%wide.region_1.2_spmd.sunk | while | flops 655366 | bytes 3932787 | solution.py:25
  253.7 1.6 bitcast_add_fusion.4
  255.3 1.6 bitcast_add_fusion.4
  257.0 1.6 bitcast_add_fusion.4
  258.6 1.6 bitcast_add_fusion.4
  260.2 1.6 bitcast_add_fusion.4
  261.8 1.6 bitcast_add_fusion.4
  263.5 1.6 bitcast_add_fusion.4
  265.1 1.6 bitcast_add_fusion.4
  266.7 1.6 bitcast_add_fusion.4
  268.4 1.6 bitcast_add_fusion.4
  270.0 1.6 bitcast_add_fusion.4
  271.6 1.6 bitcast_add_fusion.4
  273.2 1.6 bitcast_add_fusion.4
  274.9 1.6 bitcast_add_fusion.4
  276.5 1.6 bitcast_add_fusion.4
  278.1 1.6 bitcast_add_fusion.4
  279.7 1.6 bitcast_add_fusion.4
  281.4 1.6 bitcast_add_fusion.4
  283.0 1.6 bitcast_add_fusion.4
  284.6 1.6 bitcast_add_fusion.4
  286.2 1.6 bitcast_add_fusion.4
  287.9 1.6 bitcast_add_fusion.4
  289.5 1.6 bitcast_add_fusion.4
  291.1 1.6 bitcast_add_fusion.4
  292.8 1.6 bitcast_add_fusion.4
  294.4 1.6 bitcast_add_fusion.4
  296.0 1.6 bitcast_add_fusion.4
  297.6 1.6 bitcast_add_fusion.4
  299.3 1.6 bitcast_add_fusion.4
  300.9 1.6 bitcast_add_fusion.4
  306.0 1.6 fusion.59
  308.6 1.0 convolution_dynamic-update-slice_fusion.4
  309.5 1.0 convolution_dynamic-update-slice_fusion.3
  310.5 1.0 convolution_dynamic-update-slice_fusion.2
  311.5 1.0 convolution_dynamic-update-slice_fusion.1
  312.5 1.0 convolution_dynamic-update-slice_fusion
  316.9 1.0 fusion
  319.5 1.1 convolution_multiply_fusion.2
  320.6 1.1 convolution_multiply_fusion.3
  325.6 1.2 convolution_bitcast_fusion.23
  326.9 1.2 convolution_bitcast_fusion.22
  328.1 1.2 convolution_bitcast_fusion.21
  329.3 1.2 convolution_bitcast_fusion.20
  330.9 1.1 multiply_reduce_fusion.5
  333.7 1.5 fusion.39
  335.2 1.5 fusion.31
  336.8 202.9 %all-gather.8.cloned.1.call-done = f32[1280,64,128]{2,1,0:T(8,128)} async-done(((f32[40,64,128]{2,1,0:T(8,128)}), f32[1280,64,128]{2,1,0:T(8,128)}) %all-gather.8.cloned.1.call-update) | async-done | bytes 41943056 | tf_op jit(solution)/shard_map/all_gather | solution.py:16
  539.8 2.5 while.32
  540.6 1.6 bitcast_add_fusion.5
  545.9 1.2 convolution_bitcast_fusion.19
  547.1 1.2 convolution_bitcast_fusion.18
  548.3 1.2 convolution_bitcast_fusion.17
  549.6 1.2 convolution_bitcast_fusion.16
  550.8 1.2 convolution_bitcast_fusion.15
  552.8 1.2 multiply_reduce_fusion.3
  554.0 2.0 fusion.37
  562.5 1.0 fusion.60
  563.8 1.1 copy.174
  565.5 169.4 %all-reduce.1 = (f32[40]{0:T(128)}, f32[40]{0:T(128)}) all-reduce(f32[40]{0:T(128)S(1)} %concatenate.34, f32[40]{0:T(128)S(1)} %copy-done.104), channel_id=1, replica_groups=mesh['dp'=16,'ctx'=32] {'dp','ctx'}, use_global_device_ids=true, to_apply=%region_45.46 | all-reduce | flops 80 | bytes 640 | tf_op jit(solution)/shard_map/psum | solution.py:186
  (376 shorter events, 36.9 us)
Async XLA Ops:
  7.2 66.6 %copy-start = (bf16[1,128,128]{2,1,0:T(8,128)(2,1)S(1)}, bf16[1,128,128]{2,1,0:T(8,128)(2,1)}, u32[]{:S(2)}) copy-start(bf16[1,128,128]{2,1,0:T(8,128)(2,1)} %param.22) | copy-start | bytes 98308
  7.2 246.3 %all-gather.6.cloned.1.call-start = ((), (), s32[]{:S(2)}) async-start(), calls=%async_computation | async-start | bytes 43253760 | tf_op jit(solution)/shard_map/all_gather | solution.py:16
  9.8 320.7 %copy-start.54 = (f32[128,8]{0,1:T(8,128)}, f32[128,8]{0,1:T(8,128)S(1)}, u32[]{:S(2)}) copy-start(f32[128,8]{0,1:T(8,128)S(1)} %copy.230) | copy-start | bytes 12292
  9.9 310.7 %copy-start.56 = (f32[128,8]{0,1:T(8,128)}, f32[128,8]{0,1:T(8,128)S(1)}, u32[]{:S(2)}) copy-start(f32[128,8]{0,1:T(8,128)S(1)} %copy.236) | copy-start | bytes 12292
  10.3 309.2 %copy-start.50 = (f32[128,8]{0,1:T(8,128)}, f32[128,8]{0,1:T(8,128)S(1)}, u32[]{:S(2)}) copy-start(f32[128,8]{0,1:T(8,128)S(1)} %copy.237) | copy-start | bytes 12292
  10.4 308.8 %copy-start.52 = (f32[128,8]{0,1:T(8,128)}, f32[128,8]{0,1:T(8,128)S(1)}, u32[]{:S(2)}) copy-start(f32[128,8]{0,1:T(8,128)S(1)} %copy.238) | copy-start | bytes 12292
  11.2 4.0 copy-start.34
  11.2 62.2 %copy-start.19 = (bf16[1,128,2560]{2,1,0:T(8,128)(2,1)S(1)}, bf16[1,128,2560]{2,1,0:T(8,128)(2,1)}, u32[]{:S(2)}) copy-start(bf16[1,128,2560]{2,1,0:T(8,128)(2,1)} %param.21) | copy-start | bytes 1966084
  13.1 526.6 %all-gather.8.cloned.1.call-start = ((), (), s32[]{:S(2)}) async-start(), calls=%async_computation.1 | async-start | bytes 43253760 | tf_op jit(solution)/shard_map/all_gather | solution.py:16
  73.7 257.1 %copy-start.1 = (bf16[1,128,2560]{1,2,0:T(8,128)(2,1)}, bf16[1,128,2560]{1,2,0:T(8,128)(2,1)S(1)}, u32[]{:S(2)}) copy-start(bf16[1,128,2560]{1,2,0:T(8,128)(2,1)S(1)} %copy.153) | copy-start | bytes 1966084
  302.7 3.3 copy-start.81
  307.6 5.8 copy-start.40
  307.7 5.8 copy-start.42
  307.7 5.8 copy-start.44
  307.7 5.8 copy-start.46
  307.7 5.8 copy-start.48
  308.5 22.0 %copy-start.36 = (f32[128,8]{0,1:T(8,128)}, f32[128,8]{0,1:T(8,128)S(1)}, u32[]{:S(2)}) copy-start(f32[128,8]{0,1:T(8,128)S(1)} %get-tuple-element.314) | copy-start | bytes 12292
  310.5 3.7 copy-start.101
  310.5 4.4 copy-start.100
  310.5 5.0 copy-start.99
  310.5 5.7 copy-start.98
  313.4 5.1 copy-start.82
  319.5 11.4 %copy-start.3 = (f32[8,128,128]{2,1,0:T(8,128)}, f32[8,128,128]{2,1,0:T(8,128)S(1)}, u32[]{:S(2)}) copy-start(f32[8,128,128]{2,1,0:T(8,128)S(1)} %convolution_multiply_fusion.1) | copy-start | bytes 1572868
  543.5 4.9 copy-start.35
  544.1 6.7 copy-start.39
  545.0 7.0 copy-start.92
  545.0 7.1 copy-start.45
  545.0 7.1 copy-start.47
  545.0 7.1 copy-start.55
  545.0 7.1 copy-start.61
  545.0 7.1 copy-start.62
  545.0 7.1 copy-start.65
  545.0 7.1 copy-start.66
  545.9 6.3 copy-start.79
  545.9 6.3 copy-start.80
  549.6 6.4 copy-start.90
  549.6 6.5 copy-start.49
  549.6 6.5 copy-start.57
  549.6 6.5 copy-start.70
  549.6 6.5 copy-start.77
  549.6 6.5 copy-start.78
  550.8 6.1 copy-start.6
  552.8 5.1 copy-start.4
  556.9 3.0 copy-start.72
  556.9 3.0 copy-start.75
  556.9 3.6 copy-start.87
  557.0 3.7 copy-start.71
  557.0 3.7 copy-start.73
  557.0 4.3 copy-start.14
  557.0 4.3 copy-start.17
  557.0 4.3 copy-start.86
  557.9 3.5 copy-start.12
  557.9 3.5 copy-start.85
  558.0 3.6 copy-start.10
  558.0 3.6 copy-start.84
  562.5 172.4 %copy-start.31 = (f32[128,128]{1,0:T(8,128)S(1)}, f32[128,128]{1,0:T(8,128)}, u32[]{:S(2)}) copy-start(f32[128,128]{1,0:T(8,128)} %convolution_bitcast_fusion.18) | copy-start | bytes 196612
  562.5 172.6 %copy-start.26 = (f32[128,128]{1,0:T(8,128)S(1)}, f32[128,128]{1,0:T(8,128)}, u32[]{:S(2)}) copy-start(f32[128,128]{1,0:T(8,128)} %convolution_bitcast_fusion.23) | copy-start | bytes 196612
  562.5 172.6 %copy-start.27 = (f32[128,128]{1,0:T(8,128)S(1)}, f32[128,128]{1,0:T(8,128)}, u32[]{:S(2)}) copy-start(f32[128,128]{1,0:T(8,128)} %convolution_add_fusion.9) | copy-start | bytes 196612
  562.5 172.9 %copy-start.30 = (f32[128,128]{1,0:T(8,128)S(1)}, f32[128,128]{1,0:T(8,128)}, u32[]{:S(2)}) copy-start(f32[128,128]{1,0:T(8,128)} %convolution_bitcast_fusion.17) | copy-start | bytes 196612
  563.5 172.0 %copy-start.25 = (f32[128,128]{1,0:T(8,128)S(1)}, f32[128,128]{1,0:T(8,128)}, u32[]{:S(2)}) copy-start(f32[128,128]{1,0:T(8,128)} %convolution_bitcast_fusion.22) | copy-start | bytes 196612
  563.7 172.1 %copy-start.29 = (f32[128,128]{1,0:T(8,128)S(1)}, f32[128,128]{1,0:T(8,128)}, u32[]{:S(2)}) copy-start(f32[128,128]{1,0:T(8,128)} %convolution_bitcast_fusion.16) | copy-start | bytes 196612
  563.7 172.3 %copy-start.24 = (f32[128,128]{1,0:T(8,128)S(1)}, f32[128,128]{1,0:T(8,128)}, u32[]{:S(2)}) copy-start(f32[128,128]{1,0:T(8,128)} %convolution_bitcast_fusion.21) | copy-start | bytes 196612
  563.8 172.5 %copy-start.28 = (f32[128,128]{1,0:T(8,128)S(1)}, f32[128,128]{1,0:T(8,128)}, u32[]{:S(2)}) copy-start(f32[128,128]{1,0:T(8,128)} %convolution_bitcast_fusion.15) | copy-start | bytes 196612
  564.9 172.3 %copy-start.23 = (f32[128,128]{1,0:T(8,128)S(1)}, f32[128,128]{1,0:T(8,128)}, u32[]{:S(2)}) copy-start(f32[128,128]{1,0:T(8,128)} %convolution_bitcast_fusion.20) | copy-start | bytes 196612
  (44 other events, 101.5 us)
Sparse Core Ops, SparseCore 0:
  13.3 240.2 all-gather.5
  313.6 226.0 all-gather.7
where the time goes:
time: 748 us; the launch traced here: 746 us
  waiting for transfers between devices  383 us (51%)
  blocking collectives  227 us (30%)
  other arithmetic  58.7 us (8%)
  matrix products  40.7 us (5%)
  local copies, waits for them, and re-layouts  18.5 us (2%)
  between operations  16.1 us (2%)
    all_gather x2, waiting for transfers between devices, carried_in(): gathered = jax.tree.map(lambda a: lax.all_gather(a, axis), part)  383 us
    psum x1, blocking collectives, per_device(): grad_decay, grad_skip = lax.psum((rate_part, skip_part), ('dp', 'ctx'))  169 us
    unnamed x1, blocking collectives  57.8 us
    add x31, other arithmetic, combine_states(): early_state * late_decay[:, None, None] + late_state  48.9 us
  transfers between devices with their start and end apart: 2, of which 2 were waited for; matrix products, arithmetic and copies ran while one was open for 3% of the time, Pallas kernels for 0%

commit v1 on v0

v1 whole, which is shorter than its diff:
```python
import functools

import jax
import jax.numpy as jnp
from jax import lax
from jax.experimental import pallas as pl
from jax.experimental.pallas import tpu as pltpu
from jax.sharding import PartitionSpec as P

F32 = jnp.float32
BF16 = jnp.bfloat16
HIGHEST = lax.Precision.HIGHEST
LANES = 128
STREAMS = 2
VMEM_LIMIT = 48 * 1024 * 1024


def nn(a, b):
    return lax.dot_general(a, b, (((1,), (0,)), ((), ())), preferred_element_type=F32)


def nt(a, b):
    return lax.dot_general(a, b, (((1,), (1,)), ((), ())), preferred_element_type=F32)


def halves(a):
    high = a.astype(BF16)
    low = (a - high.astype(F32)).astype(BF16)
    return high, low


def iota(shape, dim):
    return lax.broadcasted_iota(jnp.int32, shape, dim)


def spread(values, block, first):
    return jnp.where(first, values[:, 2 * block : 2 * block + 1], values[:, 2 * block + 1 : 2 * block + 2])


def head_terms(raw_ref, decay_ref, wide, heads):
    rows = raw_ref.shape[0]
    wide[...] = jnp.zeros_like(wide)
    wide[0:1, :heads] = decay_ref[...]
    rate = jnp.where(iota((1, LANES), 1) < heads, -jnp.exp(wide[0:1, :]), 0.0)
    wide[0:1, :] = jnp.zeros((1, LANES), F32)
    wide[:, :heads] = raw_ref[...]
    raw = wide[...]
    step = jnp.maximum(raw, 0.0) + jnp.log1p(jnp.exp(-jnp.abs(raw)))
    lower = (iota((rows, rows), 0) >= iota((rows, rows), 1)).astype(F32)
    cumulative = jnp.dot(lower, step * rate, precision=HIGHEST, preferred_element_type=F32)
    return raw, step, rate, cumulative


def summary_kernel(heads, blocks, core_ref, raw_ref, decay_ref, x_ref, g_ref, b_ref, c_ref, *rest):
    keeps, sends, wide = rest[:STREAMS], rest[STREAMS : 2 * STREAMS], rest[2 * STREAMS]
    forward = core_ref[0] == 1
    raw, step, rate, cumulative = head_terms(raw_ref, decay_ref, wide, heads)
    closing = cumulative[-1:, :]
    weight = jnp.exp(closing - cumulative) * step
    lift = jnp.exp(cumulative)
    rows = cumulative.shape[0]
    first = iota((rows, LANES), 1) < LANES // 2
    keys_t = b_ref[...].astype(F32).T.astype(BF16)
    queries_t = c_ref[...].astype(F32).T.astype(BF16)
    keys_t = jnp.concatenate([keys_t, keys_t], axis=1)
    queries_t = jnp.concatenate([queries_t, queries_t], axis=1)
    per = blocks // STREAMS
    for block in range(blocks):
        stream, place = block // per, block % per
        cols = pl.ds(block * LANES, LANES)
        weighted = spread(weight, block, first) * x_ref[:, cols].astype(F32)
        lifted = spread(lift, block, first) * g_ref[:, cols].astype(F32)
        state = nn(keys_t, jnp.concatenate(halves(weighted), axis=0))
        message = nn(queries_t, jnp.concatenate(halves(lifted), axis=0))
        where = pl.ds(place * LANES, LANES)
        keeps[stream][where, :] = jnp.where(forward, state, message)
        sends[stream][where, :] = jnp.where(forward, message, state)
    for stream in range(STREAMS):
        extra = keeps[stream].shape[0] - per * LANES
        logs = [
            spread(closing, stream * per + place, first[:1]) for place in range(per)
        ] + [jnp.zeros((extra - per, LANES), F32)]
        logs = jnp.concatenate(logs, axis=0)
        keeps[stream][pl.ds(per * LANES, extra), :] = logs
        sends[stream][pl.ds(per * LANES, extra), :] = logs


def local_kernel(
    heads,
    blocks,
    raw_ref,
    decay_ref,
    x_ref,
    g_ref,
    b_ref,
    c_ref,
    adjoint_ref,
    keys_ref,
    queries_ref,
    through_ref,
    column_ref,
    step_ref,
    cumulative_ref,
    slope_ref,
    rate_ref,
    skip_ref,
    wide,
    row_t,
):
    raw, step, rate, cumulative = head_terms(raw_ref, decay_ref, wide, heads)
    rows = cumulative.shape[0]
    lane = iota((rows, LANES), 1)
    first = lane < LANES // 2
    causal = iota((rows, rows), 1) >= iota((rows, rows), 0)
    cumulative_t = cumulative.T
    keys = b_ref[...]
    queries = c_ref[...]
    scores_t = jnp.where(causal, nt(keys, queries), 0.0)
    row_t[...] = jnp.zeros_like(row_t)
    gathered = jnp.zeros((rows, rows), F32)
    column_step = jnp.zeros((rows, LANES), F32)
    skip = jnp.zeros((1, LANES), F32)
    lane_one = iota((1, LANES), 1)
    zero = jnp.zeros((rows, LANES), BF16)
    for block in range(blocks):
        cols = pl.ds(block * LANES, LANES)
        x = x_ref[:, cols]
        g = g_ref[:, cols]
        both_x = jnp.concatenate([jnp.where(first, x, zero), jnp.where(first, zero, x)], axis=0)
        both_g = jnp.concatenate([jnp.where(first, g, zero), jnp.where(first, zero, g)], axis=0)
        products = nt(both_x, g)
        highs, lows = [], []
        for half in range(2):
            head = 2 * block + half
            between = cumulative_t[head : head + 1, :] - cumulative[:, head : head + 1]
            decay = jnp.exp(jnp.minimum(between, 0.0))
            high, low = halves(decay * scores_t)
            highs.append(high)
            lows.append(low)
            scaled = decay * products[half * rows : (half + 1) * rows] * step[:, head : head + 1]
            gathered = gathered + scaled
            scored = scaled * scores_t
            row_t[head : head + 1, :] = jnp.sum(scored, axis=0, keepdims=True)
            column_step = jnp.where(lane == head, jnp.sum(scored, axis=1, keepdims=True), column_step)
        adjoint_ref[:, cols] = nn(jnp.concatenate(highs, axis=1), both_g) + nn(
            jnp.concatenate(lows, axis=1), both_g
        )
        met = jnp.sum(x.astype(F32) * g.astype(F32), axis=0, keepdims=True)
        early = jnp.sum(jnp.where(first[:1], met, 0.0), axis=1, keepdims=True)
        late = jnp.sum(jnp.where(first[:1], 0.0, met), axis=1, keepdims=True)
        skip = jnp.where(lane_one == 2 * block, early, skip)
        skip = jnp.where(lane_one == 2 * block + 1, late, skip)
    gathered = jnp.where(causal, gathered, 0.0)
    keys_ref[...] = nn(
        jnp.concatenate(halves(gathered), axis=1), jnp.concatenate([queries, queries], axis=0)
    )
    queries_ref[...] = nn(
        jnp.concatenate(halves(gathered.T), axis=1), jnp.concatenate([keys, keys], axis=0)
    )
    through_ref[...] = row_t[...].T - column_step
    column_ref[...] = column_step / step
    step_ref[...] = step
    cumulative_ref[...] = cumulative
    slope_ref[...] = 1.0 / (1.0 + jnp.exp(-raw))
    rate_ref[...] = rate
    skip_ref[...] = skip


def finish_kernel(
    heads,
    blocks,
    core_ref,
    skip_weight_ref,
    x_ref,
    g_ref,
    b_ref,
    c_ref,
    adjoint_ref,
    keys_in,
    queries_in,
    through_ref,
    column_ref,
    step_ref,
    cumulative_ref,
    slope_ref,
    rate_ref,
    skip_ref,
    *rest,
):
    pairs, before, other = (rest[i * STREAMS : (i + 1) * STREAMS] for i in range(3))
    grad_x, grad_keys, grad_queries, grad_raw, sums, wide = rest[3 * STREAMS :]
    forward = core_ref[0] == 1
    step = step_ref[...]
    cumulative = cumulative_ref[...]
    rate = rate_ref[...]
    rows = cumulative.shape[0]
    wide[...] = jnp.zeros_like(wide)
    wide[0:1, :heads] = skip_weight_ref[...]
    skip_weight = wide[0:1, :]
    closing = cumulative[-1:, :]
    tail = jnp.exp(closing - cumulative)
    lift = jnp.exp(cumulative)
    first = iota((rows, LANES), 1) < LANES // 2
    lane_one = iota((1, LANES), 1)
    keys = jnp.concatenate([b_ref[...], b_ref[...]], axis=1)
    queries = jnp.concatenate([c_ref[...], c_ref[...]], axis=1)
    side = iota((LANES, LANES), 0) // (LANES // 2)
    place_lane = iota((LANES, LANES), 1)
    per = blocks // STREAMS
    from_keys = keys_in[...]
    from_queries = queries_in[...]
    outward_sum = jnp.zeros((rows, LANES), F32)
    inward_sum = jnp.zeros((rows, LANES), F32)
    meeting = jnp.zeros((1, LANES), F32)
    for block in range(blocks):
        stream, place = block // per, block % per
        cols = pl.ds(block * LANES, LANES)
        where = pl.ds(place * LANES, LANES)
        log_row = pairs[stream][pl.ds(per * LANES + place, 1), :]
        mine = pairs[stream][where, :] + jnp.exp(log_row) * before[stream][where, :]
        theirs = other[stream][where, :]
        entering = jnp.where(forward, mine, theirs)
        message = jnp.where(forward, theirs, mine)
        entering_high, entering_low = halves(entering)
        message_high, message_low = halves(message)
        x = x_ref[:, cols].astype(F32)
        g = g_ref[:, cols].astype(F32)
        message_keys = nn(keys, jnp.concatenate([message_high, message_low], axis=0))
        state_queries = nn(queries, jnp.concatenate([entering_high, entering_low], axis=0))
        tail_b = spread(tail, block, first)
        step_b = spread(step, block, first)
        skip_b = spread(skip_weight, block, first[:1])
        weighted_high, weighted_low = halves(tail_b * step_b * x)
        lifted_high, lifted_low = halves(spread(lift, block, first) * g)
        picker = jnp.where(place_lane == side + 2 * block, 1.0, 0.0).astype(BF16)
        picker = jnp.concatenate([picker, picker], axis=0)
        outward_sum = outward_sum + nn(jnp.concatenate(halves(x * message_keys), axis=1), picker)
        inward_sum = inward_sum + nn(jnp.concatenate(halves(g * state_queries), axis=1), picker)
        from_keys = from_keys + (
            nt(
                jnp.concatenate([weighted_high, weighted_low], axis=1),
                jnp.concatenate([message_high, message_high], axis=1),
            )
            + nt(weighted_high, message_low)
        )
        from_queries = from_queries + (
            nt(
                jnp.concatenate([lifted_high, lifted_low], axis=1),
                jnp.concatenate([entering_high, entering_high], axis=1),
            )
            + nt(lifted_high, entering_low)
        )
        met = jnp.sum(entering * message, axis=0, keepdims=True)
        early = jnp.sum(jnp.where(first[:1], met, 0.0), axis=1, keepdims=True)
        late = jnp.sum(jnp.where(first[:1], 0.0, met), axis=1, keepdims=True)
        meeting = jnp.where(lane_one == 2 * block, early, meeting)
        meeting = jnp.where(lane_one == 2 * block + 1, late, meeting)
        grad = step_b * (adjoint_ref[:, cols] + tail_b * message_keys) + skip_b * g
        grad_x[:, cols] = grad.astype(grad_x.dtype)
    grad_keys[...] = from_keys
    grad_queries[...] = from_queries
    inward = lift * inward_sum
    lead = tail * outward_sum
    outward = lead * step
    through = through_ref[...] + inward - outward
    last = jnp.sum(outward, axis=0, keepdims=True) + jnp.exp(closing) * meeting
    through = through + jnp.where(iota((rows, LANES), 0) == rows - 1, last, 0.0)
    upper = (iota((rows, rows), 1) >= iota((rows, rows), 0)).astype(F32)
    grad_cumulative = jnp.dot(upper, through, precision=HIGHEST, preferred_element_type=F32)
    grad_step = grad_cumulative * rate + column_ref[...] + lead
    grad_raw[...] = (grad_step * slope_ref[...])[:, :heads]
    rate_sum = jnp.sum(grad_cumulative * step, axis=0, keepdims=True) * rate
    sums[0:1, :] = jnp.where(lane_one < heads, rate_sum, 0.0)
    sums[1:2, :] = jnp.where(lane_one < heads, skip_ref[...], 0.0)


def chip_moves(moves, chips):
    ahead = [(2 * a + 1, 2 * b + 1) for a, b in moves]
    back = [(2 * (chips - 1 - a), 2 * (chips - 1 - b)) for a, b in moves]
    return ahead + back


ROUNDS = (
    [(z, z + 1) for z in range(0, 16, 2)],
    [(1, 3), (5, 7), (9, 11), (13, 15)],
    [(3, 7), (1, 2)],
    [(7, 11), (3, 5)],
    [(11, 13), (7, 9), (5, 6), (3, 4)],
    [(7, 8), (9, 10), (11, 12), (13, 14)],
)
LAST_CHIP = [(11, 15)]


def open_up(buffer, per):
    state = buffer[: per * LANES].reshape(per, LANES, LANES)
    log = buffer[per * LANES : per * LANES + per].reshape(per, 1, LANES)
    return state, log


def close_up(state, log, rows):
    per = state.shape[0]
    pad = jnp.zeros((rows - per * LANES - per, LANES), F32)
    return jnp.concatenate([state.reshape(per * LANES, LANES), log.reshape(per, LANES), pad], axis=0)


def scan_chips(keeps, pairs, per, swap):
    chips = 16
    rows = keeps[0].shape[0]
    own, before = [], [None] * STREAMS
    for keep, pair in zip(keeps, pairs):
        state, log = open_up(keep, per)
        pair_state, pair_log = open_up(pair, per)
        own.append((state + jnp.exp(log) * pair_state, log + pair_log))
    for turn, moves in enumerate(ROUNDS):
        arrived = []
        for stream in range(STREAMS):
            state, log = own[stream]
            if before[stream] is not None:
                past, past_log = before[stream]
                state, log = state + jnp.exp(log) * past, log + past_log
            if turn < 3:
                packed = close_up(state, log, rows)
                arrived.append([open_up(lax.ppermute(packed, "ctx", chip_moves(moves, chips)), per)])
            else:
                got = [(lax.ppermute(state, "ctx", chip_moves(moves, chips)), None)]
                if turn == 4:
                    got.append((lax.ppermute(state, "ctx", chip_moves(LAST_CHIP, chips)), None))
                arrived.append(got)
        for stream in range(STREAMS):
            for state, log in arrived[stream]:
                if before[stream] is None:
                    before[stream] = (state, log)
                else:
                    past, past_log = before[stream]
                    new_log = past_log if log is None else past_log + log
                    before[stream] = (past + jnp.exp(past_log) * state, new_log)
    flat = [past.reshape(per * LANES, LANES) for past, _ in before]
    return flat, [lax.ppermute(past, "ctx", swap) for past in flat]


def per_device(inputs, in_keys, output_queries, step_raw, decay_log, skip_weight, grad_out):
    rows = inputs.shape[1]
    width = inputs.shape[2]
    heads = decay_log.shape[0]
    blocks = width // LANES
    per = blocks // STREAMS
    extra = (per + 7) // 8 * 8
    count = lax.axis_size("ctx")
    swap = [(i, i ^ 1) for i in range(count)]
    core = lax.rem(lax.axis_index("ctx"), 2).astype(jnp.int32).reshape(1)
    x, g, keys, queries, raw = inputs[0], grad_out[0], in_keys[0], output_queries[0], step_raw[0]
    decay_row = decay_log.reshape(1, heads)
    skip_row = skip_weight.reshape(1, heads)
    whole = pl.BlockSpec(memory_space=pltpu.VMEM)
    scalar = pl.BlockSpec(memory_space=pltpu.SMEM)
    params = pltpu.CompilerParams(vmem_limit_bytes=VMEM_LIMIT)
    tile = jax.ShapeDtypeStruct((rows, LANES), F32)
    line = jax.ShapeDtypeStruct((1, LANES), F32)
    packed = jax.ShapeDtypeStruct((per * LANES + extra, LANES), F32)
    wide = pltpu.VMEM((rows, LANES), F32)

    made = pl.pallas_call(
        functools.partial(summary_kernel, heads, blocks),
        out_shape=[packed] * (2 * STREAMS),
        in_specs=[scalar] + [whole] * 6,
        out_specs=[whole] * (2 * STREAMS),
        scratch_shapes=[wide],
        compiler_params=params,
        cost_estimate=pl.CostEstimate(flops=400_000_000, bytes_accessed=4_000_000, transcendentals=0),
        name="summaries",
    )(core, raw, decay_row, x, g, keys, queries)
    keeps, sends = made[:STREAMS], made[STREAMS:]
    local = pl.pallas_call(
        functools.partial(local_kernel, heads, blocks),
        out_shape=[jax.ShapeDtypeStruct((rows, width), F32)] + [tile] * 7 + [line] * 2,
        in_specs=[whole] * 6,
        out_specs=[whole] * 10,
        scratch_shapes=[wide, pltpu.VMEM((LANES, rows), F32)],
        compiler_params=params,
        cost_estimate=pl.CostEstimate(flops=2_000_000_000, bytes_accessed=4_000_000, transcendentals=0),
        name="within_slab",
    )(raw, decay_row, x, g, keys, queries)
    pairs = [lax.ppermute(send, "ctx", swap) for send in sends]
    before, other = scan_chips(keeps, pairs, per, swap)
    grad_x, grad_keys, grad_queries, grad_raw, sums = pl.pallas_call(
        functools.partial(finish_kernel, heads, blocks),
        out_shape=[
            jax.ShapeDtypeStruct((rows, width), BF16),
            tile,
            tile,
            jax.ShapeDtypeStruct((rows, heads), F32),
            jax.ShapeDtypeStruct((2, LANES), F32),
        ],
        in_specs=[scalar] + [whole] * (15 + 3 * STREAMS),
        out_specs=[whole] * 5,
        scratch_shapes=[wide],
        compiler_params=params,
        cost_estimate=pl.CostEstimate(flops=800_000_000, bytes_accessed=8_000_000, transcendentals=0),
        name="gradients",
    )(core, skip_row, x, g, keys, queries, *local, *pairs, *before, *other)
    line_sum = jnp.concatenate([sums[0, : LANES // 2], sums[1, : LANES // 2]])
    for axis in ("ctx", "dp"):
        size = lax.axis_size(axis)
        shared = jnp.broadcast_to(line_sum[None], (size, LANES))
        line_sum = jnp.sum(lax.all_to_all(shared, axis, 0, 0, tiled=True), axis=0)
    return (
        grad_x[None],
        grad_keys[None],
        grad_queries[None],
        grad_raw[None],
        line_sum[:heads],
        line_sum[LANES // 2 : LANES // 2 + heads],
    )


def solution(mesh):
    placed = P("dp", "ctx", None)
    return jax.shard_map(
        per_device,
        mesh=mesh,
        in_specs=(placed, placed, placed, placed, P(), P(), placed),
        out_specs=(placed, placed, placed, placed, P(), P()),
        check_vma=False,
    )
```

time: 748 us -> 195 us (0.26)
  waiting for transfers between devices: 383 us -> 6.96 us
  blocking collectives: 227 us -> 24.3 us
  starting transfers between devices: 0.08 us -> 95 us
  other arithmetic: 58.7 us -> 16.4 us
  matrix products: 40.7 us -> 0 us
  local copies, waits for them, and re-layouts: 18.5 us -> 34.8 us
  Pallas kernels: 0 us -> 15 us
  between operations: 16.1 us -> 1.12 us
    all_gather x2 -> x0, waiting for transfers between devices: 383 us -> none  [carried_in(): gathered = jax.tree.map(lambda a: lax.all_gather(a, axis), part)]
    psum x1 -> x0, blocking collectives: 169 us -> none  [per_device(): grad_decay, grad_skip = lax.psum((rate_part, skip_part), ('dp', 'ctx'))]
    ppermute x0 -> x18, starting transfers between devices: none -> 88.2 us  [the longest x2 63 us: scan_chips(): return (flat, [lax.ppermute(past, 'ctx', swap) for past in flat])]
    unnamed x1 -> x0, blocking collectives: 57.8 us -> none
    add x36 -> x14, other arithmetic: 49.3 us -> 7.09 us  [the longest x12 6.88 us: scan_chips(): state, log = (state + jnp.exp(log) * past, log + past_log)]
    dot_general x56 -> x0, matrix products: 40.7 us -> none  [the longest x5 6.85 us: block_gradients(): jnp.einsum('hij,jh->ih', weighted_scores, step_block, precision=HIGHEST_P...]
    concatenate x2 -> x6, local copies, waits for them, and re-layouts: 0.16 us -> 25.3 us  [close_up(): jnp.concatenate([state.reshape(per * LANES, LANES), log.reshape(per, LANE...]
    all_to_all x0 -> x1, blocking collectives: none -> 24.3 us  [per_device(): line_sum = jnp.sum(lax.all_to_all(shared, axis, 0, 0, tiled=True), axis=0)]
  transfers between devices with their start and end apart: 2 -> 19, of which waited for: 2 -> 2; matrix products, arithmetic and copies ran while one was open for 3% -> 22% of each run, Pallas kernels for 0% -> 3%
where the time goes in v1:
time: 195 us; the launch traced here: 194 us
  starting transfers between devices  95 us (49%)
  local copies, waits for them, and re-layouts  34.8 us (18%)
  blocking collectives  24.3 us (12%)
  other arithmetic  16.4 us (8%)
  Pallas kernels  15 us (8%)
  waiting for transfers between devices  6.96 us (4%)
    ppermute x2, starting transfers between devices, scan_chips(): return (flat, [lax.ppermute(past, 'ctx', swap) for past in flat])  63 us
    concatenate x6, local copies, waits for them, and re-layouts, close_up(): jnp.concatenate([state.reshape(per * LANES, LANES), log.reshape(per, LANE...  25.3 us
    all_to_all x1, blocking collectives, per_device(): line_sum = jnp.sum(lax.all_to_all(shared, axis, 0, 0, tiled=True), axis=0)  24.3 us
    ppermute x2, starting transfers between devices, per_device(): pairs = [lax.ppermute(send, 'ctx', swap) for send in sends]  10.7 us
    ppermute x6, starting transfers between devices, scan_chips(): lax.ppermute(packed, 'ctx', chip_moves(moves, chips))  8.81 us
    slice x4, other arithmetic, open_up(): state = buffer[:per * LANES].reshape(per, LANES, LANES)  7.68 us
    pallas_call x1, Pallas kernels, per_device(): pl.pallas_call(functools.partial(finish_kernel, heads, blocks), out_shape...  7.21 us
    unnamed x44, local copies, waits for them, and re-layouts  7.04 us
  transfers between devices with their start and end apart: 19, of which 2 were waited for; matrix products, arithmetic and copies ran while one was open for 22% of the time, Pallas kernels for 3%

profile of v1, /device:TPU:1, one launch (start us, length us, event | category | flops | bytes accessed | tf_op | source)
XLA Modules:
  0.0 193.5 jit_solution(375180842106909888)
XLA Ops:
  0.6 0.8 copy.17
  1.5 1.1 copy-done.1
  2.6 1.1 copy-done.3
  3.6 0.8 copy-done.5
  4.4 0.8 copy-done.7
  5.2 0.7 copy-done.10
  5.8 2.1 %summaries.1 = (f32[1296,128]{1,0:T(8,128)S(1)}, f32[1296,128]{1,0:T(8,128)S(1)}, f32[1296,128]{1,0:T(8,128)S(1)}, f32[1296,128]{1,0:T(8,128)S(1)}) custom-call(s32[1]{0:T(128)} %bitcast.core_ref, f32[128,40]{1,0:T(8,128)S(1)} %bitcast.74, f32[1,40]{1,0:T(1,128)S(1)} %bitcast.84, bf16[128,2560]{1,0:T(8,128)(2,1)S(1)} %bitcast.68, ...), custom_call_target="tpu_custom_call" | custom-call | flops 400000000 | bytes 4000000 | tf_op jit(solution)/shard_map/summaries/pallas_call | solution.py:362
  7.9 8.8 %collective-permute-start.1 = (f32[1296,128]{1,0:T(8,128)S(1)}, f32[1296,128]{1,0:T(8,128)S(1)}, u32[]{:S(2)}, u32[]{:S(2)}) collective-permute-start(f32[1296,128]{1,0:T(8,128)S(1)} %get-tuple-element.36), channel_id=1, source_target_pairs={{0,1},{1,0},{2,3},{3,2},{4,5},{5,4},{6,7},{7,6},{8,9},{9,8},{10,11... | collective-permute-start | bytes 1990664 | tf_op jit(solution)/shard_map/ppermute | solution.py:383
  16.7 1.9 collective-permute-start
  18.7 1.2 fusion.16
  19.9 3.3 %concatenate.24 = f32[1296,128]{1,0:T(8,128)} concatenate(f32[1280,128]{1,0:T(8,128)S(1)} %get-tuple-element.81, f32[10,128]{1,0:T(8,128)S(1)} %get-tuple-element.68, f32[6,128]{1,0:T(8,128)S(1)} %broadcast.32), dimensions={0} | concatenate | bytes 1327104 | tf_op jit(solution)/shard_map/concatenate | solution.py:303
  23.2 2.1 %collective-permute-start.9 = (f32[1296,128]{1,0:T(8,128)}, f32[1296,128]{1,0:T(8,128)}, u32[]{:S(2)}, u32[]{:S(2)}) collective-permute-start(f32[1296,128]{1,0:T(8,128)} %concatenate.24), channel_id=1, source_target_pairs={{1,3},{5,7},{9,11},{13,15},{17,19},{21,23},{25,27},{29,31},{30,28}... | collective-permute-start | bytes 1990664 | tf_op jit(solution)/shard_map/ppermute | solution.py:323
  25.4 1.2 fusion.18
  26.6 3.3 %concatenate.21 = f32[1296,128]{1,0:T(8,128)} concatenate(f32[1280,128]{1,0:T(8,128)S(1)} %get-tuple-element.90, f32[10,128]{1,0:T(8,128)S(1)} %get-tuple-element.75, f32[6,128]{1,0:T(8,128)S(1)} %broadcast.32), dimensions={0} | concatenate | bytes 1327104 | tf_op jit(solution)/shard_map/concatenate | solution.py:303
  29.9 1.3 collective-permute-start.2
  31.3 1.2 collective-permute-done.9
  32.4 2.0 %fusion.2 = f32[1280,128]{1,0:T(8,128)} fusion(f32[1280,128]{1,0:T(8,128)S(1)} %get-tuple-element.81, f32[10,128]{1,0:T(8,128)S(1)} %get-tuple-element.67, f32[1296,128]{1,0:T(8,128)} %collective-permute-done.9), kind=kLoop, calls=%fused_computation.6 | loop fusion | flops 327680 | bytes 1971200 | tf_op jit(solution)/shard_map/add | solution.py:320
  34.4 0.7 slice_add_fusion.6
  35.1 4.6 %concatenate.25 = f32[1296,128]{1,0:T(8,128)} concatenate(f32[1280,128]{1,0:T(8,128)} %fusion.2, f32[10,128]{1,0:T(8,128)S(1)} %slice_add_fusion.6, f32[6,128]{1,0:T(8,128)S(1)} %broadcast.32), dimensions={0} | concatenate | bytes 1327104 | tf_op jit(solution)/shard_map/concatenate | solution.py:303
  39.8 1.5 collective-permute-start.10
  41.3 1.0 fusion
  42.3 4.6 %concatenate.22 = f32[1296,128]{1,0:T(8,128)} concatenate(f32[1280,128]{1,0:T(8,128)} %fusion, f32[10,128]{1,0:T(8,128)S(1)} %slice_add_fusion.7, f32[6,128]{1,0:T(8,128)S(1)} %broadcast.32), dimensions={0} | concatenate | bytes 1327104 | tf_op jit(solution)/shard_map/concatenate | solution.py:303
  47.0 1.5 collective-permute-start.3
  48.5 0.7 fusion.12
  49.2 2.8 %fusion.17 = (f32[1280,128]{1,0:T(8,128)}, f32[1280,128]{1,0:T(8,128)}, f32[1280,128]{1,0:T(8,128)}) fusion(f32[1296,128]{1,0:T(8,128)} %collective-permute-done.10, f32[1280,128]{1,0:T(8,128)S(1)} %get-tuple-element.81, f32[10,128]{1,0:T(8,128)S(1)} %get-tuple-element.87, f32[1296,128]{1,0:T(8,128)} %collective-permute-done.9, ...), kind=kLoop, calls=%fused_computation.56 | loop fusion | flops 655360 | bytes 3942400 | tf_op jit(solution)/shard_map/slice | solution.py:295
  52.0 4.7 %concatenate.26 = f32[1296,128]{1,0:T(8,128)} concatenate(f32[1280,128]{1,0:T(8,128)} %get-tuple-element.84, f32[10,128]{1,0:T(8,128)S(1)} %get-tuple-element.86, f32[6,128]{1,0:T(8,128)S(1)} %broadcast.32), dimensions={0} | concatenate | bytes 1327104 | tf_op jit(solution)/shard_map/concatenate | solution.py:303
  56.6 1.5 collective-permute-start.11
  58.1 0.7 fusion.10
  58.8 2.5 %fusion.19 = (f32[1280,128]{1,0:T(8,128)}, f32[1280,128]{1,0:T(8,128)}, f32[1280,128]{1,0:T(8,128)}) fusion(f32[1296,128]{1,0:T(8,128)} %collective-permute-done.3, f32[1280,128]{1,0:T(8,128)S(1)} %get-tuple-element.90, f32[10,128]{1,0:T(8,128)S(1)} %get-tuple-element.96, f32[1296,128]{1,0:T(8,128)S(1)} %collective-permute-done.2, ...), kind=kLoop, calls=%fused_computation.58 | loop fusion | flops 655360 | bytes 3942400 | tf_op jit(solution)/shard_map/slice | solution.py:295
  61.3 4.7 %concatenate.23 = f32[1296,128]{1,0:T(8,128)} concatenate(f32[1280,128]{1,0:T(8,128)} %get-tuple-element.93, f32[10,128]{1,0:T(8,128)S(1)} %get-tuple-element.95, f32[6,128]{1,0:T(8,128)S(1)} %broadcast.32), dimensions={0} | concatenate | bytes 1327104 | tf_op jit(solution)/shard_map/concatenate | solution.py:303
  66.1 0.8 collective-permute-start.4
  66.9 1.1 slice.110
  68.1 0.7 fusion.8
  68.9 0.4 multiply_add_fusion.5
  69.2 0.0 copy-start.13
  69.2 0.8 collective-permute-start.12
  70.1 0.7 fusion.9
  70.9 0.5 multiply_add_fusion.13
  71.4 0.7 collective-permute-start.5
  72.1 0.2 multiply_add_fusion.3
  72.3 0.7 collective-permute-start.13
  73.0 0.7 collective-permute-start.14
  73.7 0.2 multiply_add_fusion.11
  73.8 0.7 collective-permute-start.6
  74.6 0.7 collective-permute-start.7
  75.3 0.3 multiply_add_fusion.1
  75.6 0.7 collective-permute-start.15
  76.3 0.3 multiply_add_fusion.9
  76.6 0.7 collective-permute-start.8
  77.3 0.1 multiply_add_fusion
  77.4 0.0 copy-start.2
  77.5 60.9 %collective-permute-start.17 = (f32[1280,128]{1,0:T(8,128)S(1)}, f32[1280,128]{1,0:T(8,128)S(1)}, u32[]{:S(2)}, u32[]{:S(2)}) collective-permute-start(f32[1280,128]{1,0:T(8,128)S(1)} %bitcast.64), channel_id=1, source_target_pairs={{0,1},{1,0},{2,3},{3,2},{4,5},{5,4},{6,7},{7,6},{8,9},{9,8},{10,11... | collective-permute-start | bytes 1966088 | tf_op jit(solution)/shard_map/ppermute | solution.py:338
  138.4 0.1 multiply_add_fusion.8
  138.5 2.1 %collective-permute-start.16 = (f32[1280,128]{1,0:T(8,128)S(1)}, f32[1280,128]{1,0:T(8,128)S(1)}, u32[]{:S(2)}, u32[]{:S(2)}) collective-permute-start(f32[1280,128]{1,0:T(8,128)S(1)} %bitcast.66), channel_id=1, source_target_pairs={{0,1},{1,0},{2,3},{3,2},{4,5},{5,4},{6,7},{7,6},{8,9},{9,8},{10,11... | collective-permute-start | bytes 1966088 | tf_op jit(solution)/shard_map/ppermute | solution.py:338
  140.7 5.7 %within_slab.1 = (f32[128,2560]{1,0:T(8,128)S(1)}, f32[128,128]{1,0:T(8,128)S(1)}, f32[128,128]{1,0:T(8,128)S(1)}, f32[128,128]{1,0:T(8,128)S(1)}, f32[128,128]{...) custom-call(f32[128,40]{1,0:T(8,128)S(1)} %bitcast.75, ...), custom_call_target="tpu_custom_call" | custom-call | flops 2000000000 | bytes 4000000 | tf_op jit(solution)/shard_map/within_slab/pallas_call | solution.py:373
  146.4 1.1 copy-done
  147.5 7.2 %gradients.1 = (bf16[128,2560]{1,0:T(8,128)(2,1)}, f32[128,128]{1,0:T(8,128)}, f32[128,128]{1,0:T(8,128)}, f32[128,40]{1,0:T(8,128)S(1)}, f32[2,128]{1,0:T(2,128)S(1)}) custom-call(s32[1]{0:T(128)} %bitcast.core_ref, f32[1,40]{1,0:T(1,128)S(1)} %bitcast.83, bf16[128,2560]{1,0:T(8,128)(2,1)S(1)} %bitcast.70, bf16[128,2560]{1,0:T(8,128)(2,1)S(1)} %bitcast.73, ...), custom_call_target="tpu_custom_call" | custom-call | flops 800000000 | bytes 8000000 | tf_op jit(solution)/shard_map/gradients/pallas_call | solution.py:385
  154.7 0.1 pad_maximum_fusion
  154.8 24.3 %all_to_all.12 = f32[32,1,128]{2,1,0:T(1,128)S(1)} all-to-all(f32[32,1,128]{2,1,0:T(1,128)S(1)} %broadcast_in_dim.28), channel_id=1, replica_groups=mesh['dp'=16,'ctx'=32] {'ctx'}, dimensions={0} | all-to-all | bytes 32768 | tf_op jit(solution)/shard_map/all_to_all | solution.py:405
  179.1 0.6 broadcast_in_dim.29
  179.7 6.8 %all-to-all-start.1 = ((f32[16,1,128]{2,1,0:T(1,128)}), f32[16,1,128]{2,1,0:T(1,128)S(1)}, u32[]{:S(2)}, u32[]{:S(2)}) async-start(f32[16,1,128]{2,1,0:T(1,128)} %broadcast_in_dim.29), calls=%async_computation.1 | async-start | bytes 16384 | tf_op jit(solution)/shard_map/all_to_all | solution.py:405
  186.5 0.7 copy.20
  187.2 5.7 %all-to-all-done.1 = f32[16,1,128]{2,1,0:T(1,128)S(1)} async-done(((f32[16,1,128]{2,1,0:T(1,128)}), f32[16,1,128]{2,1,0:T(1,128)S(1)}, u32[]{:S(2)}, u32[]{:S(2)}) %all-to-all-start.1) | async-done | bytes 8224 | tf_op jit(solution)/shard_map/all_to_all | solution.py:405
  192.9 0.6 fusion.20
  (60 shorter events, 0.2 us)
Async XLA Ops:
  1.5 1.1 copy-start.1
  2.6 1.1 copy-start.3
  3.6 0.8 copy-start.5
  4.4 0.8 copy-start.7
  5.2 0.7 copy-start.10
  7.9 10.7 %collective-permute-start.1 = (f32[1296,128]{1,0:T(8,128)S(1)}, f32[1296,128]{1,0:T(8,128)S(1)}, u32[]{:S(2)}, u32[]{:S(2)}) collective-permute-start(f32[1296,128]{1,0:T(8,128)S(1)} %get-tuple-element.36), channel_id=1, source_target_pairs={{0,1},{1,0},{2,3},{3,2},{4,5},{5,4},{6,7},{7,6},{8,9},{9,8},{10,11... | collective-permute-start | bytes 1990664 | tf_op jit(solution)/shard_map/ppermute | solution.py:383
  16.7 8.7 %collective-permute-start = (f32[1296,128]{1,0:T(8,128)S(1)}, f32[1296,128]{1,0:T(8,128)S(1)}, u32[]{:S(2)}, u32[]{:S(2)}) collective-permute-start(f32[1296,128]{1,0:T(8,128)S(1)} %get-tuple-element.35), channel_id=1, source_target_pairs={{0,1},{1,0},{2,3},{3,2},{4,5},{5,4},{6,7},{7,6},{8,9},{9,8},{10,11... | collective-permute-start | bytes 1990664 | tf_op jit(solution)/shard_map/ppermute | solution.py:383
  23.2 9.2 %collective-permute-start.9 = (f32[1296,128]{1,0:T(8,128)}, f32[1296,128]{1,0:T(8,128)}, u32[]{:S(2)}, u32[]{:S(2)}) collective-permute-start(f32[1296,128]{1,0:T(8,128)} %concatenate.24), channel_id=1, source_target_pairs={{1,3},{5,7},{9,11},{13,15},{17,19},{21,23},{25,27},{29,31},{30,28}... | collective-permute-start | bytes 1990664 | tf_op jit(solution)/shard_map/ppermute | solution.py:323
  29.9 11.4 %collective-permute-start.2 = (f32[1296,128]{1,0:T(8,128)}, f32[1296,128]{1,0:T(8,128)S(1)}, u32[]{:S(2)}, u32[]{:S(2)}) collective-permute-start(f32[1296,128]{1,0:T(8,128)} %concatenate.21), channel_id=1, source_target_pairs={{1,3},{5,7},{9,11},{13,15},{17,19},{21,23},{25,27},{29,31},{30,28}... | collective-permute-start | bytes 1990664 | tf_op jit(solution)/shard_map/ppermute | solution.py:323
  39.8 8.7 %collective-permute-start.10 = (f32[1296,128]{1,0:T(8,128)}, f32[1296,128]{1,0:T(8,128)}, u32[]{:S(2)}, u32[]{:S(2)}) collective-permute-start(f32[1296,128]{1,0:T(8,128)} %concatenate.25), channel_id=1, source_target_pairs={{3,7},{11,15},{19,23},{27,31},{28,24},{20,16},{12,8},{4,0},{35,39}... | collective-permute-start | bytes 1990664 | tf_op jit(solution)/shard_map/ppermute | solution.py:323
  41.3 17.6 %copy-start.12 = (f32[1296,128]{1,0:T(8,128)}, f32[1296,128]{1,0:T(8,128)S(1)}, u32[]{:S(2)}) copy-start(f32[1296,128]{1,0:T(8,128)S(1)} %collective-permute-done.2) | copy-start | bytes 1990660
  47.0 11.2 %collective-permute-start.3 = (f32[1296,128]{1,0:T(8,128)}, f32[1296,128]{1,0:T(8,128)}, u32[]{:S(2)}, u32[]{:S(2)}) collective-permute-start(f32[1296,128]{1,0:T(8,128)} %concatenate.22), channel_id=1, source_target_pairs={{3,7},{11,15},{19,23},{27,31},{28,24},{20,16},{12,8},{4,0},{35,39}... | collective-permute-start | bytes 1990664 | tf_op jit(solution)/shard_map/ppermute | solution.py:323
  56.6 10.3 %collective-permute-start.11 = (f32[1296,128]{1,0:T(8,128)}, f32[1296,128]{1,0:T(8,128)}, u32[]{:S(2)}, u32[]{:S(2)}) collective-permute-start(f32[1296,128]{1,0:T(8,128)} %concatenate.26), channel_id=1, source_target_pairs={{7,15},{3,5},{24,16},{28,26},{39,47},{35,37},{56,48},{60,58},{71,7... | collective-permute-start | bytes 1990664 | tf_op jit(solution)/shard_map/ppermute | solution.py:323
  61.3 7.5 %copy-start.15 = (f32[1280,128]{1,0:T(8,128)S(1)}, f32[1280,128]{1,0:T(8,128)}, u32[]{:S(2)}) copy-start(f32[1280,128]{1,0:T(8,128)} %get-tuple-element.80) | copy-start | bytes 1966084
  61.3 7.5 %copy-start.16 = (f32[1280,128]{1,0:T(8,128)S(1)}, f32[1280,128]{1,0:T(8,128)}, u32[]{:S(2)}) copy-start(f32[1280,128]{1,0:T(8,128)} %get-tuple-element.82) | copy-start | bytes 1966084
  66.1 2.7 %copy-start.19 = (f32[1280,128]{1,0:T(8,128)S(1)}, f32[1280,128]{1,0:T(8,128)}, u32[]{:S(2)}) copy-start(f32[1280,128]{1,0:T(8,128)} %get-tuple-element.83) | copy-start | bytes 1966084
  66.1 2.7 %copy-start.20 = (f32[1280,128]{1,0:T(8,128)S(1)}, f32[1280,128]{1,0:T(8,128)}, u32[]{:S(2)}) copy-start(f32[1280,128]{1,0:T(8,128)} %get-tuple-element.85) | copy-start | bytes 1966084
  66.1 4.0 %collective-permute-start.4 = (f32[1296,128]{1,0:T(8,128)}, f32[1296,128]{1,0:T(8,128)S(1)}, u32[]{:S(2)}, u32[]{:S(2)}) collective-permute-start(f32[1296,128]{1,0:T(8,128)} %concatenate.23), channel_id=1, source_target_pairs={{7,15},{3,5},{24,16},{28,26},{39,47},{35,37},{56,48},{60,58},{71,7... | collective-permute-start | bytes 1990664 | tf_op jit(solution)/shard_map/ppermute | solution.py:323
  68.8 2.0 %copy-start.17 = (f32[1280,128]{1,0:T(8,128)S(1)}, f32[1280,128]{1,0:T(8,128)}, u32[]{:S(2)}) copy-start(f32[1280,128]{1,0:T(8,128)} %get-tuple-element.92) | copy-start | bytes 1966084
  68.9 2.0 %copy-start.18 = (f32[1280,128]{1,0:T(8,128)S(1)}, f32[1280,128]{1,0:T(8,128)}, u32[]{:S(2)}) copy-start(f32[1280,128]{1,0:T(8,128)} %get-tuple-element.94) | copy-start | bytes 1966084
  69.2 1.7 copy-start.13
  69.2 1.7 copy-start.14
  69.2 2.8 %collective-permute-start.12 = (f32[10,128,128]{2,1,0:T(8,128)S(1)}, f32[10,128,128]{2,1,0:T(8,128)S(1)}, u32[]{:S(2)}, u32[]{:S(2)}) collective-permute-start(f32[10,128,128]{2,1,0:T(8,128)S(1)} %get-tuple-element.64), channel_id=1, source_target_pairs={{15,23},{7,11},{16,8},{24,20},{47,55},{39,43},{48,40},{56,52},{79,... | collective-permute-start | bytes 1966088 | tf_op jit(solution)/shard_map/ppermute | solution.py:325
  71.4 2.3 %collective-permute-start.5 = (f32[10,128,128]{2,1,0:T(8,128)S(1)}, f32[10,128,128]{2,1,0:T(8,128)S(1)}, u32[]{:S(2)}, u32[]{:S(2)}) collective-permute-start(f32[10,128,128]{2,1,0:T(8,128)S(1)} %get-tuple-element.71), channel_id=1, source_target_pairs={{15,23},{7,11},{16,8},{24,20},{47,55},{39,43},{48,40},{56,52},{79,... | collective-permute-start | bytes 1966088 | tf_op jit(solution)/shard_map/ppermute | solution.py:325
  72.3 3.0 %collective-permute-start.13 = (f32[10,128,128]{2,1,0:T(8,128)S(1)}, f32[10,128,128]{2,1,0:T(8,128)S(1)}, u32[]{:S(2)}, u32[]{:S(2)}) collective-permute-start(f32[10,128,128]{2,1,0:T(8,128)S(1)} %multiply_add_fusion.3), channel_id=1, source_target_pairs={{23,27},{15,19},{11,13},{7,9},{8,4},{16,12},{20,18},{24,22},{55,59... | collective-permute-start | bytes 1966088 | tf_op jit(solution)/shard_map/ppermute | solution.py:325
  73.0 2.3 %collective-permute-start.14 = (f32[10,128,128]{2,1,0:T(8,128)S(1)}, f32[10,128,128]{2,1,0:T(8,128)S(1)}, u32[]{:S(2)}, u32[]{:S(2)}) collective-permute-start(f32[10,128,128]{2,1,0:T(8,128)S(1)} %multiply_add_fusion.3), channel_id=1, source_target_pairs={{23,31},{8,0},{55,63},{40,32},{87,95},{72,64},{119,127},{104,96},{... | collective-permute-start | bytes 1966088 | tf_op jit(solution)/shard_map/ppermute | solution.py:327
  73.8 2.4 %collective-permute-start.6 = (f32[10,128,128]{2,1,0:T(8,128)S(1)}, f32[10,128,128]{2,1,0:T(8,128)S(1)}, u32[]{:S(2)}, u32[]{:S(2)}) collective-permute-start(f32[10,128,128]{2,1,0:T(8,128)S(1)} %multiply_add_fusion.11), channel_id=1, source_target_pairs={{23,27},{15,19},{11,13},{7,9},{8,4},{16,12},{20,18},{24,22},{55,59... | collective-permute-start | bytes 1966088 | tf_op jit(solution)/shard_map/ppermute | solution.py:325
  74.6 1.7 collective-permute-start.7
  75.6 1.8 collective-permute-start.15
  76.6 61.8 %collective-permute-start.8 = (f32[10,128,128]{2,1,0:T(8,128)S(1)}, f32[10,128,128]{2,1,0:T(8,128)S(1)}, u32[]{:S(2)}, u32[]{:S(2)}) collective-permute-start(f32[10,128,128]{2,1,0:T(8,128)S(1)} %get-tuple-element.69), channel_id=1, source_target_pairs={{15,17},{19,21},{23,25},{27,29},{16,14},{12,10},{8,6},{4,2},{47,49... | collective-permute-start | bytes 1966088 | tf_op jit(solution)/shard_map/ppermute | solution.py:325
  77.4 63.2 %copy-start.2 = (bf16[1,128,2560]{2,1,0:T(8,128)(2,1)S(1)}, bf16[1,128,2560]{2,1,0:T(8,128)(2,1)}, u32[]{:S(2)}) copy-start(bf16[1,128,2560]{2,1,0:T(8,128)(2,1)} %param.7) | copy-start | bytes 1966084
  77.5 63.2 %copy-start.4 = (bf16[1,128,2560]{2,1,0:T(8,128)(2,1)S(1)}, bf16[1,128,2560]{2,1,0:T(8,128)(2,1)}, u32[]{:S(2)}) copy-start(bf16[1,128,2560]{2,1,0:T(8,128)(2,1)} %param.13) | copy-start | bytes 1966084
  77.5 63.2 %copy-start.6 = (bf16[1,128,128]{2,1,0:T(8,128)(2,1)S(1)}, bf16[1,128,128]{2,1,0:T(8,128)(2,1)}, u32[]{:S(2)}) copy-start(bf16[1,128,128]{2,1,0:T(8,128)(2,1)} %param.8) | copy-start | bytes 98308
  77.5 63.2 %copy-start.8 = (bf16[1,128,128]{2,1,0:T(8,128)(2,1)S(1)}, bf16[1,128,128]{2,1,0:T(8,128)(2,1)}, u32[]{:S(2)}) copy-start(bf16[1,128,128]{2,1,0:T(8,128)(2,1)} %param.9) | copy-start | bytes 98308
  77.5 63.2 %copy-start.11 = (f32[40]{0:T(128)S(1)}, f32[40]{0:T(128)}, u32[]{:S(2)}) copy-start(f32[40]{0:T(128)} %param.11) | copy-start | bytes 484
  77.5 70.0 %collective-permute-start.17 = (f32[1280,128]{1,0:T(8,128)S(1)}, f32[1280,128]{1,0:T(8,128)S(1)}, u32[]{:S(2)}, u32[]{:S(2)}) collective-permute-start(f32[1280,128]{1,0:T(8,128)S(1)} %bitcast.64), channel_id=1, source_target_pairs={{0,1},{1,0},{2,3},{3,2},{4,5},{5,4},{6,7},{7,6},{8,9},{9,8},{10,11... | collective-permute-start | bytes 1966088 | tf_op jit(solution)/shard_map/ppermute | solution.py:338
  138.5 9.0 %copy-start.9 = (f32[40]{0:T(128)S(1)}, f32[40]{0:T(128)}, u32[]{:S(2)}) copy-start(f32[40]{0:T(128)} %param.12) | copy-start | bytes 484
  138.5 9.0 %collective-permute-start.16 = (f32[1280,128]{1,0:T(8,128)S(1)}, f32[1280,128]{1,0:T(8,128)S(1)}, u32[]{:S(2)}, u32[]{:S(2)}) collective-permute-start(f32[1280,128]{1,0:T(8,128)S(1)} %bitcast.66), channel_id=1, source_target_pairs={{0,1},{1,0},{2,3},{3,2},{4,5},{5,4},{6,7},{7,6},{8,9},{9,8},{10,11... | collective-permute-start | bytes 1966088 | tf_op jit(solution)/shard_map/ppermute | solution.py:338
  146.3 1.1 copy-start
  179.7 13.2 %all-to-all-start.1 = ((f32[16,1,128]{2,1,0:T(1,128)}), f32[16,1,128]{2,1,0:T(1,128)S(1)}, u32[]{:S(2)}, u32[]{:S(2)}) async-start(f32[16,1,128]{2,1,0:T(1,128)} %broadcast_in_dim.29), calls=%async_computation.1 | async-start | bytes 16384 | tf_op jit(solution)/shard_map/all_to_all | solution.py:405

commit v2 on v1

--- a/solution.py
+++ b/solution.py
@@ -12,7 +12,7 @@
 HIGHEST = lax.Precision.HIGHEST
 LANES = 128
 STREAMS = 2
-VMEM_LIMIT = 48 * 1024 * 1024
+VMEM_LIMIT = 20 * 1024 * 1024
 
 
 def nn(a, b):
@@ -38,13 +38,13 @@
 
 
 def head_terms(raw_ref, decay_ref, wide, heads):
-    rows = raw_ref.shape[0]
+    rows = raw_ref.shape[1]
     wide[...] = jnp.zeros_like(wide)
     wide[0:1, :heads] = decay_ref[...]
     rate = jnp.where(iota((1, LANES), 1) < heads, -jnp.exp(wide[0:1, :]), 0.0)
     wide[0:1, :] = jnp.zeros((1, LANES), F32)
-    wide[:, :heads] = raw_ref[...]
-    raw = wide[...]
+    wide[:heads, :] = raw_ref[...]
+    raw = wide[...].T
     step = jnp.maximum(raw, 0.0) + jnp.log1p(jnp.exp(-jnp.abs(raw)))
     lower = (iota((rows, rows), 0) >= iota((rows, rows), 1)).astype(F32)
     cumulative = jnp.dot(lower, step * rate, precision=HIGHEST, preferred_element_type=F32)
@@ -166,35 +166,19 @@
     skip_ref[...] = skip
 
 
-def finish_kernel(
-    heads,
-    blocks,
-    core_ref,
-    skip_weight_ref,
-    x_ref,
-    g_ref,
-    b_ref,
-    c_ref,
-    adjoint_ref,
-    keys_in,
-    queries_in,
-    through_ref,
-    column_ref,
-    step_ref,
-    cumulative_ref,
-    slope_ref,
-    rate_ref,
-    skip_ref,
-    *rest,
-):
-    pairs, before, other = (rest[i * STREAMS : (i + 1) * STREAMS] for i in range(3))
-    grad_x, grad_keys, grad_queries, grad_raw, sums, wide = rest[3 * STREAMS :]
+def gradient_kernel(heads, blocks, stream, core_ref, skip_weight_ref, x_ref, g_ref, b_ref, c_ref, *rest):
+    fixed, rest = rest[:9], rest[9:]
+    (adjoint_ref, through_ref, column_ref, step_ref, cumulative_ref, slope_ref, rate_ref, skip_ref, pair_ref) = fixed
+    before_ref, other_ref, rest = rest[0], rest[1], rest[2:]
+    given = 2 if stream == 0 else 6
+    taken, rest = rest[:given], rest[given:]
+    final = stream == STREAMS - 1
     forward = core_ref[0] == 1
     step = step_ref[...]
     cumulative = cumulative_ref[...]
-    rate = rate_ref[...]
     rows = cumulative.shape[0]
-    wide[...] = jnp.zeros_like(wide)
+    wide = rest[-1]
+    wide[0:1, :] = jnp.zeros((1, LANES), F32)
     wide[0:1, :heads] = skip_weight_ref[...]
     skip_weight = wide[0:1, :]
     closing = cumulative[-1:, :]
@@ -207,18 +191,27 @@
     side = iota((LANES, LANES), 0) // (LANES // 2)
     place_lane = iota((LANES, LANES), 1)
     per = blocks // STREAMS
-    from_keys = keys_in[...]
-    from_queries = queries_in[...]
-    outward_sum = jnp.zeros((rows, LANES), F32)
-    inward_sum = jnp.zeros((rows, LANES), F32)
-    meeting = jnp.zeros((1, LANES), F32)
-    for block in range(blocks):
-        stream, place = block // per, block % per
+    from_keys = taken[0][...]
+    from_queries = taken[1][...]
+    if stream == 0:
+        outward_sum = jnp.zeros((rows, LANES), F32)
+        inward_sum = jnp.zeros((rows, LANES), F32)
+        meeting = jnp.zeros((1, LANES), F32)
+    else:
+        outward_sum = taken[2][...]
+        inward_sum = taken[3][...]
+        meeting = taken[4][...]
+    grad_x = rest[0]
+    if stream > 0:
+        ready = pl.ds(0, stream * per * LANES)
+        grad_x[:, ready] = taken[5][:, ready]
+    for place in range(per):
+        block = stream * per + place
         cols = pl.ds(block * LANES, LANES)
         where = pl.ds(place * LANES, LANES)
-        log_row = pairs[stream][pl.ds(per * LANES + place, 1), :]
-        mine = pairs[stream][where, :] + jnp.exp(log_row) * before[stream][where, :]
-        theirs = other[stream][where, :]
+        log_row = pair_ref[pl.ds(per * LANES + place, 1), :]
+        mine = pair_ref[where, :] + jnp.exp(log_row) * before_ref[where, :]
+        theirs = other_ref[where, :]
         entering = jnp.where(forward, mine, theirs)
         message = jnp.where(forward, theirs, mine)
         entering_high, entering_low = halves(entering)
@@ -257,8 +250,15 @@
         meeting = jnp.where(lane_one == 2 * block + 1, late, meeting)
         grad = step_b * (adjoint_ref[:, cols] + tail_b * message_keys) + skip_b * g
         grad_x[:, cols] = grad.astype(grad_x.dtype)
-    grad_keys[...] = from_keys
-    grad_queries[...] = from_queries
+    rest[1][...] = from_keys
+    rest[2][...] = from_queries
+    if not final:
+        rest[3][...] = outward_sum
+        rest[4][...] = inward_sum
+        rest[5][...] = meeting
+        return
+    grad_raw, sums = rest[3], rest[4]
+    rate = rate_ref[...]
     inward = lift * inward_sum
     lead = tail * outward_sum
     outward = lead * step
@@ -268,10 +268,37 @@
     upper = (iota((rows, rows), 1) >= iota((rows, rows), 0)).astype(F32)
     grad_cumulative = jnp.dot(upper, through, precision=HIGHEST, preferred_element_type=F32)
     grad_step = grad_cumulative * rate + column_ref[...] + lead
-    grad_raw[...] = (grad_step * slope_ref[...])[:, :heads]
+    grad_raw[...] = (grad_step * slope_ref[...]).T[:heads, :]
     rate_sum = jnp.sum(grad_cumulative * step, axis=0, keepdims=True) * rate
     sums[0:1, :] = jnp.where(lane_one < heads, rate_sum, 0.0)
     sums[1:2, :] = jnp.where(lane_one < heads, skip_ref[...], 0.0)
+
+
+def combine_kernel(per, has_before, wants_send, *refs):
+    refs = list(refs)
+    own = refs.pop(0) if wants_send else None
+    past = refs.pop(0) if has_before else None
+    arrived = refs.pop(0)
+    new_past = refs.pop(0) if has_before else None
+    send = refs.pop(0) if wants_send else None
+    tail = pl.ds(per * LANES, arrived.shape[0] - per * LANES)
+    past_log = past[tail, :] if has_before else None
+    new_log = arrived[tail, :] + past_log if has_before else arrived[tail, :]
+    if has_before:
+        new_past[tail, :] = new_log
+        past_decay = jnp.exp(past_log)
+    if wants_send:
+        own_log = own[tail, :]
+        own_decay = jnp.exp(own_log)
+        send[tail, :] = own_log + new_log
+    for place in range(per):
+        where = pl.ds(place * LANES, LANES)
+        state = arrived[where, :]
+        if has_before:
+            state = past[where, :] + past_decay[place : place + 1, :] * state
+            new_past[where, :] = state
+        if wants_send:
+            send[where, :] = own[where, :] + own_decay[place : place + 1, :] * state
 
 
 def chip_moves(moves, chips):
@@ -282,60 +309,55 @@
 
 ROUNDS = (
     [(z, z + 1) for z in range(0, 16, 2)],
-    [(1, 3), (5, 7), (9, 11), (13, 15)],
+    [(1, 3), (5, 7), (9, 11)],
     [(3, 7), (1, 2)],
     [(7, 11), (3, 5)],
     [(11, 13), (7, 9), (5, 6), (3, 4)],
     [(7, 8), (9, 10), (11, 12), (13, 14)],
 )
-LAST_CHIP = [(11, 15)]
-
-
-def open_up(buffer, per):
-    state = buffer[: per * LANES].reshape(per, LANES, LANES)
-    log = buffer[per * LANES : per * LANES + per].reshape(per, 1, LANES)
-    return state, log
-
-
-def close_up(state, log, rows):
-    per = state.shape[0]
-    pad = jnp.zeros((rows - per * LANES - per, LANES), F32)
-    return jnp.concatenate([state.reshape(per * LANES, LANES), log.reshape(per, LANES), pad], axis=0)
-
-
-def scan_chips(keeps, pairs, per, swap):
+LAST_CHIP = [(13, 15)]
+
+
+def combine(per, own, past, arrived):
+    shape = jax.ShapeDtypeStruct(arrived.shape, F32)
+    operands = [a for a in (own, past, arrived) if a is not None]
+    whole = pl.BlockSpec(memory_space=pltpu.VMEM)
+    outs = (past is not None) + (own is not None)
+    results = list(
+        pl.pallas_call(
+            functools.partial(combine_kernel, per, past is not None, own is not None),
+            out_shape=[shape] * outs,
+            in_specs=[whole] * len(operands),
+            out_specs=[whole] * outs,
+            compiler_params=pltpu.CompilerParams(vmem_limit_bytes=8 * 1024 * 1024),
+            cost_estimate=pl.CostEstimate(flops=1_000_000, bytes_accessed=1_000_000, transcendentals=0),
+            name="combine",
+        )(*operands)
+    )
+    new_past = results.pop(0) if past is not None else arrived
+    return new_past, (results.pop(0) if own is not None else None)
+
+
+def scan_chips(keeps, pairs, per, swap, beside):
     chips = 16
-    rows = keeps[0].shape[0]
-    own, before = [], [None] * STREAMS
-    for keep, pair in zip(keeps, pairs):
-        state, log = open_up(keep, per)
-        pair_state, pair_log = open_up(pair, per)
-        own.append((state + jnp.exp(log) * pair_state, log + pair_log))
+    own = [combine(per, keep, None, pair)[1] for keep, pair in zip(keeps, pairs)]
+    send, past = list(own), [None] * STREAMS
     for turn, moves in enumerate(ROUNDS):
         arrived = []
         for stream in range(STREAMS):
-            state, log = own[stream]
-            if before[stream] is not None:
-                past, past_log = before[stream]
-                state, log = state + jnp.exp(log) * past, log + past_log
-            if turn < 3:
-                packed = close_up(state, log, rows)
-                arrived.append([open_up(lax.ppermute(packed, "ctx", chip_moves(moves, chips)), per)])
-            else:
-                got = [(lax.ppermute(state, "ctx", chip_moves(moves, chips)), None)]
-                if turn == 4:
-                    got.append((lax.ppermute(state, "ctx", chip_moves(LAST_CHIP, chips)), None))
-                arrived.append(got)
+            got = [lax.ppermute(send[stream], "ctx", chip_moves(moves, chips))]
+            if turn == 5:
+                got.append(lax.ppermute(send[stream], "ctx", chip_moves(LAST_CHIP, chips)))
+            arrived.append(got)
+        if turn == 0:
+            extra = beside(own)
+            arrived[-1], extra = lax.optimization_barrier((arrived[-1], extra))
         for stream in range(STREAMS):
-            for state, log in arrived[stream]:
-                if before[stream] is None:
-                    before[stream] = (state, log)
-                else:
-                    past, past_log = before[stream]
-                    new_log = past_log if log is None else past_log + log
-                    before[stream] = (past + jnp.exp(past_log) * state, new_log)
-    flat = [past.reshape(per * LANES, LANES) for past, _ in before]
-    return flat, [lax.ppermute(past, "ctx", swap) for past in flat]
+            for index, block in enumerate(arrived[stream]):
+                target = own[stream] if index == 0 and turn < 5 else None
+                past[stream], new_send = combine(per, target, past[stream], block)
+                send[stream] = new_send if new_send is not None else send[stream]
+    return past, [lax.ppermute(a, "ctx", swap) for a in past], extra
 
 
 def per_device(inputs, in_keys, output_queries, step_raw, decay_log, skip_weight, grad_out):
@@ -348,7 +370,8 @@
     count = lax.axis_size("ctx")
     swap = [(i, i ^ 1) for i in range(count)]
     core = lax.rem(lax.axis_index("ctx"), 2).astype(jnp.int32).reshape(1)
-    x, g, keys, queries, raw = inputs[0], grad_out[0], in_keys[0], output_queries[0], step_raw[0]
+    x, g, keys, queries = inputs[0], grad_out[0], in_keys[0], output_queries[0]
+    raw_t = jnp.swapaxes(step_raw[0], 0, 1)
     decay_row = decay_log.reshape(1, heads)
     skip_row = skip_weight.reshape(1, heads)
     whole = pl.BlockSpec(memory_space=pltpu.VMEM)
@@ -359,45 +382,64 @@
     packed = jax.ShapeDtypeStruct((per * LANES + extra, LANES), F32)
     wide = pltpu.VMEM((rows, LANES), F32)
 
+    def fetched(a):
+        return pl.BlockSpec(a.shape, lambda i: (0, 0))
+
+    operands = (raw_t, decay_row, x, g, keys, queries)
     made = pl.pallas_call(
         functools.partial(summary_kernel, heads, blocks),
+        grid=(1,),
         out_shape=[packed] * (2 * STREAMS),
-        in_specs=[scalar] + [whole] * 6,
+        in_specs=[scalar] + [fetched(a) for a in operands],
         out_specs=[whole] * (2 * STREAMS),
         scratch_shapes=[wide],
         compiler_params=params,
         cost_estimate=pl.CostEstimate(flops=400_000_000, bytes_accessed=4_000_000, transcendentals=0),
         name="summaries",
-    )(core, raw, decay_row, x, g, keys, queries)
+    )(core, *operands)
     keeps, sends = made[:STREAMS], made[STREAMS:]
-    local = pl.pallas_call(
-        functools.partial(local_kernel, heads, blocks),
-        out_shape=[jax.ShapeDtypeStruct((rows, width), F32)] + [tile] * 7 + [line] * 2,
-        in_specs=[whole] * 6,
-        out_specs=[whole] * 10,
-        scratch_shapes=[wide, pltpu.VMEM((LANES, rows), F32)],
-        compiler_params=params,
-        cost_estimate=pl.CostEstimate(flops=2_000_000_000, bytes_accessed=4_000_000, transcendentals=0),
-        name="within_slab",
-    )(raw, decay_row, x, g, keys, queries)
+
+    def within_slab(after):
+        held, _ = lax.optimization_barrier((operands, after))
+        return pl.pallas_call(
+            functools.partial(local_kernel, heads, blocks),
+            out_shape=[jax.ShapeDtypeStruct((rows, width), F32)] + [tile] * 7 + [line] * 2,
+            in_specs=[whole] * 6,
+            out_specs=[whole] * 10,
+            scratch_shapes=[wide, pltpu.VMEM((LANES, rows), F32)],
+            compiler_params=params,
+            cost_estimate=pl.CostEstimate(flops=2_000_000_000, bytes_accessed=4_000_000, transcendentals=0),
+            name="within_slab",
+        )(*held)
+
     pairs = [lax.ppermute(send, "ctx", swap) for send in sends]
-    before, other = scan_chips(keeps, pairs, per, swap)
-    grad_x, grad_keys, grad_queries, grad_raw, sums = pl.pallas_call(
-        functools.partial(finish_kernel, heads, blocks),
-        out_shape=[
-            jax.ShapeDtypeStruct((rows, width), BF16),
-            tile,
-            tile,
-            jax.ShapeDtypeStruct((rows, heads), F32),
-            jax.ShapeDtypeStruct((2, LANES), F32),
-        ],
-        in_specs=[scalar] + [whole] * (15 + 3 * STREAMS),
-        out_specs=[whole] * 5,
-        scratch_shapes=[wide],
-        compiler_params=params,
-        cost_estimate=pl.CostEstimate(flops=800_000_000, bytes_accessed=8_000_000, transcendentals=0),
-        name="gradients",
-    )(core, skip_row, x, g, keys, queries, *local, *pairs, *before, *other)
+    before, other, local = scan_chips(keeps, pairs, per, swap, within_slab)
+    adjoint, keys_part, queries_part, *terms = local
+    full = jax.ShapeDtypeStruct((rows, width), BF16)
+    carried = [keys_part, queries_part]
+    for stream in range(STREAMS):
+        final = stream == STREAMS - 1
+        shapes = [full, tile, tile]
+        if final:
+            shapes += [jax.ShapeDtypeStruct((heads, rows), F32), jax.ShapeDtypeStruct((2, LANES), F32)]
+        else:
+            shapes += [tile, tile, line]
+        given = [core, skip_row, x, g, keys, queries, adjoint, *terms]
+        given += [pairs[stream], before[stream], other[stream], *carried]
+        done = pl.pallas_call(
+            functools.partial(gradient_kernel, heads, blocks, stream),
+            out_shape=shapes,
+            in_specs=[scalar] + [whole] * (len(given) - 1),
+            out_specs=[whole] * len(shapes),
+            scratch_shapes=[pltpu.VMEM((8, LANES), F32)],
+            compiler_params=params,
+            cost_estimate=pl.CostEstimate(flops=800_000_000, bytes_accessed=8_000_000, transcendentals=0),
+            name="gradients",
+        )(*given)
+        if final:
+            grad_x, grad_keys, grad_queries, grad_raw_t, sums = done
+        else:
+            carried = [*done[1:], done[0]]
     line_sum = jnp.concatenate([sums[0, : LANES // 2], sums[1, : LANES // 2]])
     for axis in ("ctx", "dp"):
         size = lax.axis_size(axis)
@@ -407,7 +449,7 @@
         grad_x[None],
         grad_keys[None],
         grad_queries[None],
-        grad_raw[None],
+        jnp.swapaxes(grad_raw_t, 0, 1)[None],
         line_sum[:heads],
         line_sum[LANES // 2 : LANES // 2 + heads],
     )

time: 195 us -> 168 us (0.86)
  local copies, waits for them, and re-layouts: 34.8 us -> 5.7 us
  other arithmetic: 16.4 us -> 0.11 us
  starting transfers between devices: 95 us -> 110 us
  blocking collectives: 24.3 us -> 27.5 us
    concatenate x6 -> x0, local copies, waits for them, and re-layouts: 25.3 us -> none  [close_up(): jnp.concatenate([state.reshape(per * LANES, LANES), log.reshape(per, LANE...]
    ppermute x16, starting transfers between devices: 77.5 us -> 99.2 us  [the longest x2 88.1 us: scan_chips(): return (past, [lax.ppermute(a, 'ctx', swap) for a in past], extra)]
    slice x4 -> x0, other arithmetic: 7.68 us -> none  [open_up(): state = buffer[:per * LANES].reshape(per, LANES, LANES)]
    add x14 -> x0, other arithmetic: 7.09 us -> none  [the longest x12 6.88 us: scan_chips(): state, log = (state + jnp.exp(log) * past, log + past_log)]
    all_to_all x1 -> x0, starting transfers between devices: 6.76 us -> none  [per_device(): line_sum = jnp.sum(lax.all_to_all(shared, axis, 0, 0, tiled=True), axis=0)]
    all_to_all x1 -> x0, waiting for transfers between devices: 5.73 us -> none  [per_device(): line_sum = jnp.sum(lax.all_to_all(shared, axis, 0, 0, tiled=True), axis=0)]
    ppermute x16, waiting for transfers between devices: 1.23 us -> 6.13 us  [the longest x12 6.12 us: scan_chips(): got = [lax.ppermute(send[stream], 'ctx', chip_moves(moves, chips))]]
    all_to_all x1 -> x2, blocking collectives: 24.3 us -> 27.5 us  [per_device(): line_sum = jnp.sum(lax.all_to_all(shared, axis, 0, 0, tiled=True), axis=0)]
  transfers between devices with their start and end apart: 19 -> 18, of which waited for: 2 -> 3; matrix products, arithmetic and copies ran while one was open for 22% -> 0% of each run, Pallas kernels for 3% -> 6%
where the time goes in v2:
time: 168 us; the launch traced here: 167 us
  starting transfers between devices  110 us (65%)
  blocking collectives  27.5 us (16%)
  Pallas kernels  15.8 us (9%)
  waiting for transfers between devices  6.75 us (4%)
  local copies, waits for them, and re-layouts  5.7 us (3%)
    ppermute x2, starting transfers between devices, scan_chips(): return (past, [lax.ppermute(a, 'ctx', swap) for a in past], extra)  88.1 us
    all_to_all x2, blocking collectives, per_device(): line_sum = jnp.sum(lax.all_to_all(shared, axis, 0, 0, tiled=True), axis=0)  27.5 us
    ppermute x2, starting transfers between devices, per_device(): pairs = [lax.ppermute(send, 'ctx', swap) for send in sends]  10.7 us
    ppermute x12, starting transfers between devices, scan_chips(): got = [lax.ppermute(send[stream], 'ctx', chip_moves(moves, chips))]  9.69 us
    pallas_call x2, Pallas kernels, per_device(): pl.pallas_call(functools.partial(gradient_kernel, heads, blocks, stream),...  6.2 us
    ppermute x12, waiting for transfers between devices, scan_chips(): got = [lax.ppermute(send[stream], 'ctx', chip_moves(moves, chips))]  6.12 us
    pallas_call x1, Pallas kernels, within_slab(): pl.pallas_call(functools.partial(local_kernel, heads, blocks), out_shape=...  5.72 us
    unnamed x20, local copies, waits for them, and re-layouts  5.09 us
  transfers between devices with their start and end apart: 18, of which 3 were waited for; matrix products, arithmetic and copies ran while one was open for 0% of the time, Pallas kernels for 6%

profile of v2, /device:TPU:1, one launch (start us, length us, event | category | flops | bytes accessed | tf_op | source)
XLA Modules:
  0.0 166.8 jit_solution(3455299334941514368)
XLA Ops:
  0.6 0.0 copy-start
  0.6 1.1 copy-done
  1.7 1.1 copy-done.2
  2.8 0.8 copy-done.4
  3.6 0.8 copy-done.6
  4.3 0.7 copy-done.8
  5.1 0.7 copy-done.9
  5.7 2.1 %summaries.1 = (f32[1296,128]{1,0:T(8,128)S(1)}, f32[1296,128]{1,0:T(8,128)S(1)}, f32[1296,128]{1,0:T(8,128)S(1)}, f32[1296,128]{1,0:T(8,128)S(1)}) custom-call(s32[1]{0:T(128)} %bitcast.core_ref, f32[40,128]{1,0:T(8,128)S(1)} %bitcast.40, f32[1,40]{1,0:T(1,128)S(1)} %bitcast.42, bf16[128,2560]{1,0:T(8,128)(2,1)S(1)} %bitcast.22, ...), custom_call_target="tpu_custom_call" | custom-call | flops 400000000 | bytes 4000000 | tf_op jit(solution)/shard_map/summaries/pallas_call | solution.py:389
  7.9 8.8 %collective-permute-start.2 = (f32[1296,128]{1,0:T(8,128)S(1)}, f32[1296,128]{1,0:T(8,128)S(1)}, u32[]{:S(2)}, u32[]{:S(2)}) collective-permute-start(f32[1296,128]{1,0:T(8,128)S(1)} %get-tuple-element.67), channel_id=1, source_target_pairs={{0,1},{1,0},{2,3},{3,2},{4,5},{5,4},{6,7},{7,6},{8,9},{9,8},{10,11... | collective-permute-start | bytes 1990664 | tf_op jit(solution)/shard_map/ppermute | solution.py:415
  16.7 1.9 %collective-permute-start = (f32[1296,128]{1,0:T(8,128)S(1)}, f32[1296,128]{1,0:T(8,128)S(1)}, u32[]{:S(2)}, u32[]{:S(2)}) collective-permute-start(f32[1296,128]{1,0:T(8,128)S(1)} %get-tuple-element.65), channel_id=1, source_target_pairs={{0,1},{1,0},{2,3},{3,2},{4,5},{5,4},{6,7},{7,6},{8,9},{9,8},{10,11... | collective-permute-start | bytes 1990664 | tf_op jit(solution)/shard_map/ppermute | solution.py:415
  18.6 0.1 combine.17.refs_0_
  18.7 1.3 collective-permute-start.10
  20.0 0.6 collective-permute-done.refs_1_.rest_8_
  20.7 0.1 combine.16.refs_0_
  20.8 1.3 collective-permute-start.1
  22.1 5.5 %collective-permute-done.10.refs_1_ = f32[1296,128]{1,0:T(8,128)S(1)} collective-permute-done((f32[1296,128]{1,0:T(8,128)S(1)}, f32[1296,128]{1,0:T(8,128)S(1)}, u32[]{:S(2)}, u32[]{:S(2)}) %collective-permute-start.10) | collective-permute-done | bytes 663584 | tf_op jit(solution)/shard_map/ppermute | solution.py:348
  27.6 0.1 combine.25
  27.7 0.7 collective-permute-start.11
  28.4 5.7 %within_slab.1 = (f32[128,2560]{1,0:T(8,128)S(1)}, f32[128,128]{1,0:T(8,128)S(1)}, f32[128,128]{1,0:T(8,128)S(1)}, f32[128,128]{1,0:T(8,128)S(1)}, f32[128,128]{...) custom-call(f32[40,128]{1,0:T(8,128)S(1)} %bitcast.41, ...), custom_call_target="tpu_custom_call" | custom-call | flops 2000000000 | bytes 4000000 | tf_op jit(solution)/shard_map/within_slab/pallas_call | solution.py:404
  34.1 0.6 collective-permute-done.1.refs_1_
  34.7 0.1 combine.18
  34.8 0.7 collective-permute-start.3
  35.5 0.0 collective-permute-done.11.refs_2_
  35.5 0.1 combine.26
  35.6 0.7 collective-permute-start.12
  36.4 0.0 collective-permute-done.3.refs_2_
  36.4 0.1 combine.19
  36.5 0.7 collective-permute-start.4
  37.2 0.0 collective-permute-done.12.refs_2_
  37.2 0.1 combine.27
  37.3 0.7 collective-permute-start.13
  38.1 0.0 collective-permute-done.4.refs_2_
  38.1 0.1 combine.20
  38.2 0.7 collective-permute-start.5
  38.9 0.0 collective-permute-done.13.refs_2_
  38.9 0.1 combine.28
  39.1 0.7 collective-permute-start.14
  39.8 0.0 collective-permute-done.5.refs_2_
  39.8 0.1 combine.21
  39.9 0.7 collective-permute-start.6
  40.6 0.0 collective-permute-done.14.refs_2_
  40.6 0.1 combine.29
  40.8 0.7 collective-permute-start.15
  41.5 0.7 collective-permute-start.16
  42.2 0.1 combine.22
  42.3 0.7 collective-permute-start.7
  43.1 0.7 collective-permute-start.8
  43.8 0.0 collective-permute-done.15.refs_1_
  43.8 0.1 combine.30.refs_0_
  43.9 0.1 combine.31.rest_9_
  44.0 73.0 %collective-permute-start.17 = (f32[1296,128]{1,0:T(8,128)S(1)}, f32[1296,128]{1,0:T(8,128)S(1)}, u32[]{:S(2)}, u32[]{:S(2)}) collective-permute-start(f32[1296,128]{1,0:T(8,128)S(1)} %combine.31.rest_9_), channel_id=1, source_target_pairs={{0,1},{1,0},{2,3},{3,2},{4,5},{5,4},{6,7},{7,6},{8,9},{9,8},{10,11... | collective-permute-start | bytes 1990664 | tf_op jit(solution)/shard_map/ppermute | solution.py:360
  116.9 0.1 combine.23.refs_0_
  117.0 0.0 copy-start.1
  117.0 0.0 copy-start.3
  117.1 0.0 copy-start.5
  117.1 0.0 copy-start.7
  117.1 0.1 combine.24.rest_9_
  117.2 15.1 %collective-permute-start.9 = (f32[1296,128]{1,0:T(8,128)S(1)}, f32[1296,128]{1,0:T(8,128)S(1)}, u32[]{:S(2)}, u32[]{:S(2)}) collective-permute-start(f32[1296,128]{1,0:T(8,128)S(1)} %combine.24.rest_9_), channel_id=1, source_target_pairs={{0,1},{1,0},{2,3},{3,2},{4,5},{5,4},{6,7},{7,6},{8,9},{9,8},{10,11... | collective-permute-start | bytes 1990664 | tf_op jit(solution)/shard_map/ppermute | solution.py:360
  132.3 2.6 %gradients.2 = (bf16[128,2560]{1,0:T(8,128)(2,1)S(1)}, f32[128,128]{1,0:T(8,128)S(1)}, f32[128,128]{1,0:T(8,128)S(1)}, f32[128,128]{1,0:T(8,128)S(1)}, f32[128,128]{1,0:T(8,128)S(1)}, /*index=5*/f32[1,128]{1,0:T(1,128)S(1)}) custom-call(s32[1]{0:T(128)} %bitcast.core_ref, f32[1,40]{1,0:T(1,128)S(1)} %bitcast.38, bf16[128,2560]{1,0:T(8,128)(2,1)S(1)} %bitcast.24, ...), custom_call_target="tpu_custom_call" | custom-call | flops 800000000 | bytes 8000000 | tf_op jit(solution)/shard_map/gradients/pallas_call | solution.py:429
  134.9 3.6 %gradients.3 = (bf16[128,2560]{1,0:T(8,128)(2,1)}, f32[128,128]{1,0:T(8,128)}, f32[128,128]{1,0:T(8,128)}, f32[40,128]{1,0:T(8,128)}, f32[2,128]{1,0:T(2,128)S(1)}) custom-call(s32[1]{0:T(128)} %bitcast.core_ref, f32[1,40]{1,0:T(1,128)S(1)} %bitcast.39, bf16[128,2560]{1,0:T(8,128)(2,1)S(1)} %bitcast.25, bf16[128,2560]{1,0:T(8,128)(2,1)S(1)} %bitcast.29, ...), custom_call_target="tpu_custom_call" | custom-call | flops 800000000 | bytes 8000000 | tf_op jit(solution)/shard_map/gradients/pallas_call | solution.py:429
  138.6 0.1 pad_maximum_fusion
  138.6 14.5 %all_to_all.12 = f32[32,1,128]{2,1,0:T(1,128)S(1)} all-to-all(f32[32,1,128]{2,1,0:T(1,128)S(1)} %broadcast_in_dim.28), channel_id=1, replica_groups=mesh['dp'=16,'ctx'=32] {'ctx'}, dimensions={0} | all-to-all | bytes 32768 | tf_op jit(solution)/shard_map/all_to_all | solution.py:447
  153.2 13.0 %all_to_all.13 = f32[16,1,128]{2,1,0:T(1,128)S(1)} all-to-all(f32[16,1,128]{2,1,0:T(1,128)S(1)} %broadcast_in_dim.29), channel_id=1, replica_groups=mesh['dp'=16,'ctx'=32] {'dp'}, dimensions={0} | all-to-all | bytes 16384 | tf_op jit(solution)/shard_map/all_to_all | solution.py:447
  166.2 0.6 fusion
  (21 shorter events, 0.1 us)
Async XLA Ops:
  0.6 1.1 copy-start
  1.7 1.1 copy-start.2
  2.8 0.8 copy-start.4
  3.6 0.8 copy-start.6
  4.3 0.7 copy-start.8
  5.1 0.7 copy-start.9
  7.9 10.7 %collective-permute-start.2 = (f32[1296,128]{1,0:T(8,128)S(1)}, f32[1296,128]{1,0:T(8,128)S(1)}, u32[]{:S(2)}, u32[]{:S(2)}) collective-permute-start(f32[1296,128]{1,0:T(8,128)S(1)} %get-tuple-element.67), channel_id=1, source_target_pairs={{0,1},{1,0},{2,3},{3,2},{4,5},{5,4},{6,7},{7,6},{8,9},{9,8},{10,11... | collective-permute-start | bytes 1990664 | tf_op jit(solution)/shard_map/ppermute | solution.py:415
  16.7 4.0 %collective-permute-start = (f32[1296,128]{1,0:T(8,128)S(1)}, f32[1296,128]{1,0:T(8,128)S(1)}, u32[]{:S(2)}, u32[]{:S(2)}) collective-permute-start(f32[1296,128]{1,0:T(8,128)S(1)} %get-tuple-element.65), channel_id=1, source_target_pairs={{0,1},{1,0},{2,3},{3,2},{4,5},{5,4},{6,7},{7,6},{8,9},{9,8},{10,11... | collective-permute-start | bytes 1990664 | tf_op jit(solution)/shard_map/ppermute | solution.py:415
  18.7 8.9 %collective-permute-start.10 = (f32[1296,128]{1,0:T(8,128)S(1)}, f32[1296,128]{1,0:T(8,128)S(1)}, u32[]{:S(2)}, u32[]{:S(2)}) collective-permute-start(f32[1296,128]{1,0:T(8,128)S(1)} %combine.17.refs_0_), channel_id=1, source_target_pairs={{1,3},{5,7},{9,11},{13,15},{17,19},{21,23},{25,27},{29,31},{30,28}... | collective-permute-start | bytes 1990664 | tf_op jit(solution)/shard_map/ppermute | solution.py:348
  20.8 13.9 %collective-permute-start.1 = (f32[1296,128]{1,0:T(8,128)S(1)}, f32[1296,128]{1,0:T(8,128)S(1)}, u32[]{:S(2)}, u32[]{:S(2)}) collective-permute-start(f32[1296,128]{1,0:T(8,128)S(1)} %combine.16.refs_0_), channel_id=1, source_target_pairs={{1,3},{5,7},{9,11},{13,15},{17,19},{21,23},{25,27},{29,31},{30,28}... | collective-permute-start | bytes 1990664 | tf_op jit(solution)/shard_map/ppermute | solution.py:348
  27.7 7.8 %collective-permute-start.11 = (f32[1296,128]{1,0:T(8,128)S(1)}, f32[1296,128]{1,0:T(8,128)S(1)}, u32[]{:S(2)}, u32[]{:S(2)}) collective-permute-start(f32[1296,128]{1,0:T(8,128)S(1)} %combine.25), channel_id=1, source_target_pairs={{3,7},{11,15},{19,23},{28,24},{20,16},{12,8},{35,39},{43,47},{51,5... | collective-permute-start | bytes 1990664 | tf_op jit(solution)/shard_map/ppermute | solution.py:348
  34.8 1.6 collective-permute-start.3
  35.6 1.6 collective-permute-start.12
  36.5 1.6 collective-permute-start.4
  37.3 1.6 collective-permute-start.13
  38.2 1.6 collective-permute-start.5
  39.1 1.6 collective-permute-start.14
  39.9 2.3 %collective-permute-start.6 = (f32[1296,128]{1,0:T(8,128)S(1)}, f32[1296,128]{1,0:T(8,128)S(1)}, u32[]{:S(2)}, u32[]{:S(2)}) collective-permute-start(f32[1296,128]{1,0:T(8,128)S(1)} %get-tuple-element.98), channel_id=1, source_target_pairs={{23,27},{15,19},{11,13},{7,9},{8,4},{16,12},{20,18},{24,22},{55,59... | collective-permute-start | bytes 1990664 | tf_op jit(solution)/shard_map/ppermute | solution.py:348
  40.8 3.0 %collective-permute-start.15 = (f32[1296,128]{1,0:T(8,128)S(1)}, f32[1296,128]{1,0:T(8,128)S(1)}, u32[]{:S(2)}, u32[]{:S(2)}) collective-permute-start(f32[1296,128]{1,0:T(8,128)S(1)} %get-tuple-element.108), channel_id=1, source_target_pairs={{15,17},{19,21},{23,25},{27,29},{16,14},{12,10},{8,6},{4,2},{47,49... | collective-permute-start | bytes 1990664 | tf_op jit(solution)/shard_map/ppermute | solution.py:348
  41.5 2.4 %collective-permute-start.16 = (f32[1296,128]{1,0:T(8,128)S(1)}, f32[1296,128]{1,0:T(8,128)S(1)}, u32[]{:S(2)}, u32[]{:S(2)}) collective-permute-start(f32[1296,128]{1,0:T(8,128)S(1)} %get-tuple-element.108), channel_id=1, source_target_pairs={{27,31},{4,0},{59,63},{36,32},{91,95},{68,64},{123,127},{100,96},{... | collective-permute-start | bytes 1990664 | tf_op jit(solution)/shard_map/ppermute | solution.py:350
  42.3 74.6 %collective-permute-start.7 = (f32[1296,128]{1,0:T(8,128)S(1)}, f32[1296,128]{1,0:T(8,128)S(1)}, u32[]{:S(2)}, u32[]{:S(2)}) collective-permute-start(f32[1296,128]{1,0:T(8,128)S(1)} %get-tuple-element.100), channel_id=1, source_target_pairs={{15,17},{19,21},{23,25},{27,29},{16,14},{12,10},{8,6},{4,2},{47,49... | collective-permute-start | bytes 1990664 | tf_op jit(solution)/shard_map/ppermute | solution.py:348
  43.1 74.0 %collective-permute-start.8 = (f32[1296,128]{1,0:T(8,128)S(1)}, f32[1296,128]{1,0:T(8,128)S(1)}, u32[]{:S(2)}, u32[]{:S(2)}) collective-permute-start(f32[1296,128]{1,0:T(8,128)S(1)} %get-tuple-element.100), channel_id=1, source_target_pairs={{27,31},{4,0},{59,63},{36,32},{91,95},{68,64},{123,127},{100,96},{... | collective-permute-start | bytes 1990664 | tf_op jit(solution)/shard_map/ppermute | solution.py:350
  44.0 88.3 %collective-permute-start.17 = (f32[1296,128]{1,0:T(8,128)S(1)}, f32[1296,128]{1,0:T(8,128)S(1)}, u32[]{:S(2)}, u32[]{:S(2)}) collective-permute-start(f32[1296,128]{1,0:T(8,128)S(1)} %combine.31.rest_9_), channel_id=1, source_target_pairs={{0,1},{1,0},{2,3},{3,2},{4,5},{5,4},{6,7},{7,6},{8,9},{9,8},{10,11... | collective-permute-start | bytes 1990664 | tf_op jit(solution)/shard_map/ppermute | solution.py:360
  117.0 15.3 %copy-start.1 = (bf16[1,128,2560]{2,1,0:T(8,128)(2,1)S(1)}, bf16[1,128,2560]{2,1,0:T(8,128)(2,1)}, u32[]{:S(2)}) copy-start(bf16[1,128,2560]{2,1,0:T(8,128)(2,1)} %param.7) | copy-start | bytes 1966084
  117.0 15.3 %copy-start.3 = (bf16[1,128,2560]{2,1,0:T(8,128)(2,1)S(1)}, bf16[1,128,2560]{2,1,0:T(8,128)(2,1)}, u32[]{:S(2)}) copy-start(bf16[1,128,2560]{2,1,0:T(8,128)(2,1)} %param.13) | copy-start | bytes 1966084
  117.1 15.3 %copy-start.5 = (bf16[1,128,128]{2,1,0:T(8,128)(2,1)S(1)}, bf16[1,128,128]{2,1,0:T(8,128)(2,1)}, u32[]{:S(2)}) copy-start(bf16[1,128,128]{2,1,0:T(8,128)(2,1)} %param.8) | copy-start | bytes 98308
  117.1 15.3 %copy-start.7 = (f32[40]{0:T(128)S(1)}, f32[40]{0:T(128)}, u32[]{:S(2)}) copy-start(f32[40]{0:T(128)} %param.12) | copy-start | bytes 484
  117.2 17.8 %collective-permute-start.9 = (f32[1296,128]{1,0:T(8,128)S(1)}, f32[1296,128]{1,0:T(8,128)S(1)}, u32[]{:S(2)}, u32[]{:S(2)}) collective-permute-start(f32[1296,128]{1,0:T(8,128)S(1)} %combine.24.rest_9_), channel_id=1, source_target_pairs={{0,1},{1,0},{2,3},{3,2},{4,5},{5,4},{6,7},{7,6},{8,9},{9,8},{10,11... | collective-permute-start | bytes 1990664 | tf_op jit(solution)/shard_map/ppermute | solution.py:360

commit v3 on v2

--- a/solution.py
+++ b/solution.py
@@ -11,7 +11,7 @@
 BF16 = jnp.bfloat16
 HIGHEST = lax.Precision.HIGHEST
 LANES = 128
-STREAMS = 2
+STREAMS = 4
 VMEM_LIMIT = 20 * 1024 * 1024
 
 
@@ -51,8 +51,16 @@
     return raw, step, rate, cumulative
 
 
-def summary_kernel(heads, blocks, core_ref, raw_ref, decay_ref, x_ref, g_ref, b_ref, c_ref, *rest):
-    keeps, sends, wide = rest[:STREAMS], rest[STREAMS : 2 * STREAMS], rest[2 * STREAMS]
+def summary_kernel(heads, blocks, core_ref, *refs):
+    far, refs = refs[:6], refs[6:]
+    keeps, sends, near = refs[:STREAMS], refs[STREAMS], refs[STREAMS + 1 : STREAMS + 7]
+    wide, arrivals = refs[STREAMS + 7], refs[STREAMS + 8]
+    copies = [pltpu.make_async_copy(a, b, arrivals.at[i]) for i, (a, b) in enumerate(zip(far, near))]
+    for copy in copies:
+        copy.start()
+    for copy in copies:
+        copy.wait()
+    raw_ref, decay_ref, x_ref, g_ref, b_ref, c_ref = near
     forward = core_ref[0] == 1
     raw, step, rate, cumulative = head_terms(raw_ref, decay_ref, wide, heads)
     closing = cumulative[-1:, :]
@@ -65,6 +73,7 @@
     keys_t = jnp.concatenate([keys_t, keys_t], axis=1)
     queries_t = jnp.concatenate([queries_t, queries_t], axis=1)
     per = blocks // STREAMS
+    packed_rows = keeps[0].shape[0]
     for block in range(blocks):
         stream, place = block // per, block % per
         cols = pl.ds(block * LANES, LANES)
@@ -72,17 +81,16 @@
         lifted = spread(lift, block, first) * g_ref[:, cols].astype(F32)
         state = nn(keys_t, jnp.concatenate(halves(weighted), axis=0))
         message = nn(queries_t, jnp.concatenate(halves(lifted), axis=0))
-        where = pl.ds(place * LANES, LANES)
-        keeps[stream][where, :] = jnp.where(forward, state, message)
-        sends[stream][where, :] = jnp.where(forward, message, state)
+        keeps[stream][pl.ds(place * LANES, LANES), :] = jnp.where(forward, state, message)
+        sends[pl.ds(stream * packed_rows + place * LANES, LANES), :] = jnp.where(forward, message, state)
     for stream in range(STREAMS):
-        extra = keeps[stream].shape[0] - per * LANES
+        extra = packed_rows - per * LANES
         logs = [
             spread(closing, stream * per + place, first[:1]) for place in range(per)
         ] + [jnp.zeros((extra - per, LANES), F32)]
         logs = jnp.concatenate(logs, axis=0)
         keeps[stream][pl.ds(per * LANES, extra), :] = logs
-        sends[stream][pl.ds(per * LANES, extra), :] = logs
+        sends[pl.ds(stream * packed_rows + per * LANES, extra), :] = logs
 
 
 def local_kernel(
@@ -202,6 +210,7 @@
         inward_sum = taken[3][...]
         meeting = taken[4][...]
     grad_x = rest[0]
+    base = stream * before_ref.shape[0]
     if stream > 0:
         ready = pl.ds(0, stream * per * LANES)
         grad_x[:, ready] = taken[5][:, ready]
@@ -209,8 +218,8 @@
         block = stream * per + place
         cols = pl.ds(block * LANES, LANES)
         where = pl.ds(place * LANES, LANES)
-        log_row = pair_ref[pl.ds(per * LANES + place, 1), :]
-        mine = pair_ref[where, :] + jnp.exp(log_row) * before_ref[where, :]
+        log_row = pair_ref[pl.ds(base + per * LANES + place, 1), :]
+        mine = pair_ref[pl.ds(base + place * LANES, LANES), :] + jnp.exp(log_row) * before_ref[where, :]
         theirs = other_ref[where, :]
         entering = jnp.where(forward, mine, theirs)
         message = jnp.where(forward, theirs, mine)
@@ -270,20 +279,23 @@
     grad_step = grad_cumulative * rate + column_ref[...] + lead
     grad_raw[...] = (grad_step * slope_ref[...]).T[:heads, :]
     rate_sum = jnp.sum(grad_cumulative * step, axis=0, keepdims=True) * rate
-    sums[0:1, :] = jnp.where(lane_one < heads, rate_sum, 0.0)
-    sums[1:2, :] = jnp.where(lane_one < heads, skip_ref[...], 0.0)
-
-
-def combine_kernel(per, has_before, wants_send, *refs):
+    wide[0:1, :] = jnp.where(lane_one < heads, rate_sum, 0.0)
+    wide[0:1, LANES // 2 :] = skip_ref[:, : LANES // 2]
+    sums[...] = jnp.broadcast_to(wide[0:1, :], sums.shape)
+
+
+def combine_kernel(per, base, has_before, wants_send, *refs):
     refs = list(refs)
     own = refs.pop(0) if wants_send else None
     past = refs.pop(0) if has_before else None
     arrived = refs.pop(0)
     new_past = refs.pop(0) if has_before else None
     send = refs.pop(0) if wants_send else None
-    tail = pl.ds(per * LANES, arrived.shape[0] - per * LANES)
+    extra = (per + 7) // 8 * 8
+    tail = pl.ds(per * LANES, extra)
     past_log = past[tail, :] if has_before else None
-    new_log = arrived[tail, :] + past_log if has_before else arrived[tail, :]
+    new_log = arrived[pl.ds(base + per * LANES, extra), :]
+    new_log = new_log + past_log if has_before else new_log
     if has_before:
         new_past[tail, :] = new_log
         past_decay = jnp.exp(past_log)
@@ -293,7 +305,7 @@
         send[tail, :] = own_log + new_log
     for place in range(per):
         where = pl.ds(place * LANES, LANES)
-        state = arrived[where, :]
+        state = arrived[pl.ds(base + place * LANES, LANES), :]
         if has_before:
             state = past[where, :] + past_decay[place : place + 1, :] * state
             new_past[where, :] = state
@@ -318,14 +330,15 @@
 LAST_CHIP = [(13, 15)]
 
 
-def combine(per, own, past, arrived):
-    shape = jax.ShapeDtypeStruct(arrived.shape, F32)
+def combine(per, own, past, arrived, base=0):
+    rows = per * LANES + (per + 7) // 8 * 8
+    shape = jax.ShapeDtypeStruct((rows, LANES), F32)
     operands = [a for a in (own, past, arrived) if a is not None]
     whole = pl.BlockSpec(memory_space=pltpu.VMEM)
     outs = (past is not None) + (own is not None)
     results = list(
         pl.pallas_call(
-            functools.partial(combine_kernel, per, past is not None, own is not None),
+            functools.partial(combine_kernel, per, base, past is not None, own is not None),
             out_shape=[shape] * outs,
             in_specs=[whole] * len(operands),
             out_specs=[whole] * outs,
@@ -338,26 +351,33 @@
     return new_past, (results.pop(0) if own is not None else None)
 
 
-def scan_chips(keeps, pairs, per, swap, beside):
+def scan_chips(keeps, pair, per, swap, within, gradients):
     chips = 16
-    own = [combine(per, keep, None, pair)[1] for keep, pair in zip(keeps, pairs)]
+    rows = keeps[0].shape[0]
+    own = [combine(per, keep, None, pair, i * rows)[1] for i, keep in enumerate(keeps)]
     send, past = list(own), [None] * STREAMS
+    final = len(ROUNDS) - 1
     for turn, moves in enumerate(ROUNDS):
         arrived = []
         for stream in range(STREAMS):
             got = [lax.ppermute(send[stream], "ctx", chip_moves(moves, chips))]
-            if turn == 5:
+            if turn == final:
                 got.append(lax.ppermute(send[stream], "ctx", chip_moves(LAST_CHIP, chips)))
             arrived.append(got)
-        if turn == 0:
-            extra = beside(own)
-            arrived[-1], extra = lax.optimization_barrier((arrived[-1], extra))
+        if turn == final:
+            local = within(send[-1])
+            carried = None
         for stream in range(STREAMS):
-            for index, block in enumerate(arrived[stream]):
-                target = own[stream] if index == 0 and turn < 5 else None
+            if turn == final and stream == STREAMS - 1 and stream > 0:
+                arrived[stream], carried = lax.optimization_barrier((arrived[stream], carried))
+            for block in arrived[stream]:
+                target = own[stream] if turn < final else None
                 past[stream], new_send = combine(per, target, past[stream], block)
                 send[stream] = new_send if new_send is not None else send[stream]
-    return past, [lax.ppermute(a, "ctx", swap) for a in past], extra
+            if turn == final:
+                other = lax.ppermute(past[stream], "ctx", swap)
+                carried = gradients(stream, local, past[stream], other, carried)
+    return carried
 
 
 def per_device(inputs, in_keys, output_queries, step_raw, decay_log, skip_weight, grad_out):
@@ -382,22 +402,20 @@
     packed = jax.ShapeDtypeStruct((per * LANES + extra, LANES), F32)
     wide = pltpu.VMEM((rows, LANES), F32)
 
-    def fetched(a):
-        return pl.BlockSpec(a.shape, lambda i: (0, 0))
-
     operands = (raw_t, decay_row, x, g, keys, queries)
+    far = pl.BlockSpec(memory_space=pltpu.HBM)
     made = pl.pallas_call(
         functools.partial(summary_kernel, heads, blocks),
-        grid=(1,),
-        out_shape=[packed] * (2 * STREAMS),
-        in_specs=[scalar] + [fetched(a) for a in operands],
-        out_specs=[whole] * (2 * STREAMS),
-        scratch_shapes=[wide],
+        out_shape=[packed] * STREAMS + [jax.ShapeDtypeStruct((STREAMS * packed.shape[0], LANES), F32)],
+        in_specs=[scalar] + [far] * 6,
+        out_specs=[whole] * (STREAMS + 1),
+        scratch_shapes=[pltpu.VMEM(a.shape, a.dtype) for a in operands]
+        + [wide, pltpu.SemaphoreType.DMA((6,))],
         compiler_params=params,
         cost_estimate=pl.CostEstimate(flops=400_000_000, bytes_accessed=4_000_000, transcendentals=0),
         name="summaries",
     )(core, *operands)
-    keeps, sends = made[:STREAMS], made[STREAMS:]
+    keeps, sends = made[:STREAMS], made[STREAMS]
 
     def within_slab(after):
         held, _ = lax.optimization_barrier((operands, after))
@@ -412,21 +430,19 @@
             name="within_slab",
         )(*held)
 
-    pairs = [lax.ppermute(send, "ctx", swap) for send in sends]
-    before, other, local = scan_chips(keeps, pairs, per, swap, within_slab)
-    adjoint, keys_part, queries_part, *terms = local
     full = jax.ShapeDtypeStruct((rows, width), BF16)
-    carried = [keys_part, queries_part]
-    for stream in range(STREAMS):
+
+    def gradients(stream, local, before, other, carried):
         final = stream == STREAMS - 1
         shapes = [full, tile, tile]
         if final:
-            shapes += [jax.ShapeDtypeStruct((heads, rows), F32), jax.ShapeDtypeStruct((2, LANES), F32)]
+            shapes += [jax.ShapeDtypeStruct((heads, rows), F32), jax.ShapeDtypeStruct((count, LANES), F32)]
         else:
             shapes += [tile, tile, line]
-        given = [core, skip_row, x, g, keys, queries, adjoint, *terms]
-        given += [pairs[stream], before[stream], other[stream], *carried]
-        done = pl.pallas_call(
+        adjoint, keys_part, queries_part, *terms = local
+        carried = [keys_part, queries_part] if carried is None else [*carried[1:], carried[0]]
+        given = [core, skip_row, x, g, keys, queries, adjoint, *terms, pair, before, other, *carried]
+        return pl.pallas_call(
             functools.partial(gradient_kernel, heads, blocks, stream),
             out_shape=shapes,
             in_specs=[scalar] + [whole] * (len(given) - 1),
@@ -436,15 +452,14 @@
             cost_estimate=pl.CostEstimate(flops=800_000_000, bytes_accessed=8_000_000, transcendentals=0),
             name="gradients",
         )(*given)
-        if final:
-            grad_x, grad_keys, grad_queries, grad_raw_t, sums = done
-        else:
-            carried = [*done[1:], done[0]]
-    line_sum = jnp.concatenate([sums[0, : LANES // 2], sums[1, : LANES // 2]])
-    for axis in ("ctx", "dp"):
-        size = lax.axis_size(axis)
-        shared = jnp.broadcast_to(line_sum[None], (size, LANES))
-        line_sum = jnp.sum(lax.all_to_all(shared, axis, 0, 0, tiled=True), axis=0)
+
+    pair = lax.ppermute(sends, "ctx", swap)
+    done = scan_chips(keeps, pair, per, swap, within_slab, gradients)
+    grad_x, grad_keys, grad_queries, grad_raw_t, shared = done
+    shared = lax.all_to_all(shared, "ctx", 0, 0, tiled=True)
+    line_sum = jnp.sum(shared, axis=0)
+    shared = jnp.broadcast_to(line_sum[None], (lax.axis_size("dp"), LANES))
+    line_sum = jnp.sum(lax.all_to_all(shared, "dp", 0, 0, tiled=True), axis=0)
     return (
         grad_x[None],
         grad_keys[None],

time: 168 us -> 165 us (0.982)
  starting transfers between devices: 110 us -> 89.5 us
  blocking collectives: 27.5 us -> 39.8 us
  waiting for transfers between devices: 6.75 us -> 10.2 us
    ppermute x4 -> x5, starting transfers between devices: 98.8 us -> 64.3 us  [the longest x4 55.5 us: scan_chips(): other = lax.ppermute(past[stream], 'ctx', swap)]
    ppermute x12 -> x24, starting transfers between devices: 9.69 us -> 22.5 us  [scan_chips(): got = [lax.ppermute(send[stream], 'ctx', chip_moves(moves, chips))]]
    all_to_all x2, blocking collectives: 27.5 us -> 39.8 us  [the longest x1 26.9 us: per_device(): shared = lax.all_to_all(shared, 'ctx', 0, 0, tiled=True)]
    ppermute x4 -> x5, waiting for transfers between devices: 0.63 us -> 4.27 us  [the longest x1 2.66 us: per_device(): pair = lax.ppermute(sends, 'ctx', swap)]
    pallas_call x19 -> x37, Pallas kernels: 10.1 us -> 11.1 us  [the longest x4 6.5 us: gradients(): pl.pallas_call(functools.partial(gradient_kernel, heads, blocks, stream),...]
    ppermute x12 -> x24, waiting for transfers between devices: 6.12 us -> 5.89 us  [scan_chips(): got = [lax.ppermute(send[stream], 'ctx', chip_moves(moves, chips))]]
    unnamed x20 -> x22, local copies, waits for them, and re-layouts: 5.09 us -> 5.1 us
  transfers between devices with their start and end apart: 18 -> 33, of which waited for: 3 -> 5; matrix products, arithmetic and copies ran while one was open for 0% -> 0% of each run, Pallas kernels for 6% -> 7%
where the time goes in v3:
time: 165 us; the launch traced here: 163 us
  starting transfers between devices  89.5 us (54%)
  blocking collectives  39.8 us (24%)
  Pallas kernels  16.8 us (10%)
  waiting for transfers between devices  10.2 us (6%)
  local copies, waits for them, and re-layouts  5.69 us (3%)
    ppermute x4, starting transfers between devices, scan_chips(): other = lax.ppermute(past[stream], 'ctx', swap)  55.5 us
    all_to_all x1, blocking collectives, per_device(): shared = lax.all_to_all(shared, 'ctx', 0, 0, tiled=True)  26.9 us
    ppermute x24, starting transfers between devices, scan_chips(): got = [lax.ppermute(send[stream], 'ctx', chip_moves(moves, chips))]  22.5 us
    all_to_all x1, blocking collectives, per_device(): line_sum = jnp.sum(lax.all_to_all(shared, 'dp', 0, 0, tiled=True), axis=0)  13 us
    ppermute x1, starting transfers between devices, per_device(): pair = lax.ppermute(sends, 'ctx', swap)  8.79 us
    pallas_call x4, Pallas kernels, gradients(): pl.pallas_call(functools.partial(gradient_kernel, heads, blocks, stream),...  6.5 us
    ppermute x24, waiting for transfers between devices, scan_chips(): got = [lax.ppermute(send[stream], 'ctx', chip_moves(moves, chips))]  5.89 us
    pallas_call x1, Pallas kernels, within_slab(): pl.pallas_call(functools.partial(local_kernel, heads, blocks), out_shape=...  5.72 us
  transfers between devices with their start and end apart: 33, of which 5 were waited for; matrix products, arithmetic and copies ran while one was open for 0% of the time, Pallas kernels for 7%

profile of v3, /device:TPU:1, one launch (start us, length us, event | category | flops | bytes accessed | tf_op | source)
XLA Modules:
  0.0 163.5 jit_solution(8679491830372237089)
XLA Ops:
  0.6 1.1 copy-done
  1.7 1.1 copy-done.2
  2.8 0.8 copy-done.4
  3.6 0.8 copy-done.6
  4.3 0.7 copy-done.9
  5.1 0.7 copy-done.10
  5.7 2.7 %summaries.1 = (f32[648,128]{1,0:T(8,128)S(1)}, f32[648,128]{1,0:T(8,128)S(1)}, f32[648,128]{1,0:T(8,128)S(1)}, f32[648,128]{1,0:T(8,128)S(1)}, f32[2592,128]{1,0:T(8,128)S(1)}) custom-call(s32[1]{0:T(128)} %bitcast.core_ref, f32[40,128]{1,0:T(8,128)S(1)} %bitcast.49, f32[1,40]{1,0:T(1,128)S(1)} %bitcast.51, bf16[128,2560]{1,0:T(8,128)(2,1)S(1)} %bitcast.20, ...), custom_call_target="tpu_custom_call" | custom-call | flops 400000000 | bytes 4000000 | tf_op jit(solution)/shard_map/summaries/pallas_call | solution.py:407
  8.4 8.8 %collective-permute-start = (f32[2592,128]{1,0:T(8,128)S(1)}, f32[2592,128]{1,0:T(8,128)S(1)}, u32[]{:S(2)}, u32[]{:S(2)}) collective-permute-start(f32[2592,128]{1,0:T(8,128)S(1)} %get-tuple-element.91), channel_id=1, source_target_pairs={{0,1},{1,0},{2,3},{3,2},{4,5},{5,4},{6,7},{7,6},{8,9},{9,8},{10,11... | collective-permute-start | bytes 3981320 | tf_op jit(solution)/shard_map/ppermute | solution.py:456
  17.2 2.7 %collective-permute-done.refs_1_.rest_8_ = f32[2592,128]{1,0:T(8,128)S(1)} collective-permute-done((f32[2592,128]{1,0:T(8,128)S(1)}, f32[2592,128]{1,0:T(8,128)S(1)}, u32[]{:S(2)}, u32[]{:S(2)}) %collective-permute-start) | collective-permute-done | bytes 1327136 | tf_op jit(solution)/shard_map/ppermute | solution.py:456
  19.9 1.3 collective-permute-start.24
  21.3 1.3 collective-permute-start.16
  22.7 1.3 collective-permute-start.8
  24.0 1.3 collective-permute-done.24.refs_1_
  25.3 0.7 collective-permute-start.25
  26.0 2.8 %collective-permute-done.16.refs_1_ = f32[648,128]{1,0:T(8,128)S(1)} collective-permute-done((f32[648,128]{1,0:T(8,128)S(1)}, f32[648,128]{1,0:T(8,128)S(1)}, u32[]{:S(2)}, u32[]{:S(2)}) %collective-permute-start.16) | collective-permute-done | bytes 331808 | tf_op jit(solution)/shard_map/ppermute | solution.py:363
  28.9 0.7 collective-permute-start.17
  29.6 4.9 %collective-permute-start.1 = (f32[648,128]{1,0:T(8,128)S(1)}, f32[648,128]{1,0:T(8,128)S(1)}, u32[]{:S(2)}, u32[]{:S(2)}) collective-permute-start(f32[648,128]{1,0:T(8,128)S(1)} %combine.32.refs_0_), channel_id=1, source_target_pairs={{1,3},{5,7},{9,11},{13,15},{17,19},{21,23},{25,27},{29,31},{30,28}... | collective-permute-start | bytes 995336 | tf_op jit(solution)/shard_map/ppermute | solution.py:363
  34.6 0.7 collective-permute-start.9
  35.3 0.1 combine.56
  35.4 0.7 collective-permute-start.26
  36.1 0.1 combine.48
  36.2 0.7 collective-permute-start.18
  36.9 1.7 %collective-permute-done.1.refs_1_ = f32[648,128]{1,0:T(8,128)S(1)} collective-permute-done((f32[648,128]{1,0:T(8,128)S(1)}, f32[648,128]{1,0:T(8,128)S(1)}, u32[]{:S(2)}, u32[]{:S(2)}) %collective-permute-start.1) | collective-permute-done | bytes 331808 | tf_op jit(solution)/shard_map/ppermute | solution.py:363
  38.6 0.7 collective-permute-start.2
  39.3 0.1 combine.40
  39.4 0.7 collective-permute-start.10
  40.1 0.1 combine.57
  40.2 0.7 collective-permute-start.27
  41.0 0.7 collective-permute-start.19
  41.7 0.1 combine.34
  41.7 0.7 collective-permute-start.3
  42.4 0.1 combine.41
  42.5 0.7 collective-permute-start.11
  43.2 0.1 combine.58
  43.3 0.7 collective-permute-start.28
  44.0 0.1 combine.50
  44.1 0.7 collective-permute-start.20
  44.8 0.7 collective-permute-start.4
  45.5 0.1 combine.42
  45.6 0.7 collective-permute-start.12
  46.4 0.7 collective-permute-start.29
  47.1 0.7 collective-permute-start.30
  47.9 0.7 collective-permute-start.21
  48.6 0.7 collective-permute-start.22
  49.2 0.1 combine.36
  49.3 0.7 collective-permute-start.5
  50.0 0.1 combine.43
  50.1 0.7 collective-permute-start.13
  50.8 0.7 collective-permute-start.14
  51.6 42.1 %collective-permute-start.31 = (f32[648,128]{1,0:T(8,128)S(1)}, f32[648,128]{1,0:T(8,128)S(1)}, u32[]{:S(2)}, u32[]{:S(2)}) collective-permute-start(f32[648,128]{1,0:T(8,128)S(1)} %combine.61.rest_9_), channel_id=1, source_target_pairs={{0,1},{1,0},{2,3},{3,2},{4,5},{5,4},{6,7},{7,6},{8,9},{9,8},{10,11... | collective-permute-start | bytes 995336 | tf_op jit(solution)/shard_map/ppermute | solution.py:378
  93.9 5.6 %collective-permute-start.23 = (f32[648,128]{1,0:T(8,128)S(1)}, f32[648,128]{1,0:T(8,128)S(1)}, u32[]{:S(2)}, u32[]{:S(2)}) collective-permute-start(f32[648,128]{1,0:T(8,128)S(1)} %combine.53.rest_9_), channel_id=1, source_target_pairs={{0,1},{1,0},{2,3},{3,2},{4,5},{5,4},{6,7},{7,6},{8,9},{9,8},{10,11... | collective-permute-start | bytes 995336 | tf_op jit(solution)/shard_map/ppermute | solution.py:378
  99.6 0.7 collective-permute-start.6
  100.3 0.7 collective-permute-start.7
  101.2 5.8 %collective-permute-start.15 = (f32[648,128]{1,0:T(8,128)S(1)}, f32[648,128]{1,0:T(8,128)S(1)}, u32[]{:S(2)}, u32[]{:S(2)}) collective-permute-start(f32[648,128]{1,0:T(8,128)S(1)} %combine.45.rest_9_), channel_id=1, source_target_pairs={{0,1},{1,0},{2,3},{3,2},{4,5},{5,4},{6,7},{7,6},{8,9},{9,8},{10,11... | collective-permute-start | bytes 995336 | tf_op jit(solution)/shard_map/ppermute | solution.py:378
  107.0 5.7 %within_slab.1 = (f32[128,2560]{1,0:T(8,128)S(1)}, f32[128,128]{1,0:T(8,128)S(1)}, f32[128,128]{1,0:T(8,128)S(1)}, f32[128,128]{1,0:T(8,128)S(1)}, f32[128,128]{...) custom-call(f32[40,128]{1,0:T(8,128)S(1)} %bitcast.50, ...), custom_call_target="tpu_custom_call" | custom-call | flops 2000000000 | bytes 4000000 | tf_op jit(solution)/shard_map/within_slab/pallas_call | solution.py:422
  112.8 1.4 gradients.4
  114.1 1.4 gradients.5
  115.5 1.4 gradients.6
  117.0 1.9 %collective-permute-start.32 = (f32[648,128]{1,0:T(8,128)S(1)}, f32[648,128]{1,0:T(8,128)S(1)}, u32[]{:S(2)}, u32[]{:S(2)}) collective-permute-start(f32[648,128]{1,0:T(8,128)S(1)} %combine.63.rest_9_), channel_id=1, source_target_pairs={{0,1},{1,0},{2,3},{3,2},{4,5},{5,4},{6,7},{7,6},{8,9},{9,8},{10,11... | collective-permute-start | bytes 995336 | tf_op jit(solution)/shard_map/ppermute | solution.py:378
  119.0 1.6 collective-permute-done.32.rest_10_
  120.6 2.4 %gradients.7 = (bf16[128,2560]{1,0:T(8,128)(2,1)}, f32[128,128]{1,0:T(8,128)}, f32[128,128]{1,0:T(8,128)}, f32[40,128]{1,0:T(8,128)}, f32[32,128]{1,0:T(8,128)S(1)}) custom-call(s32[1]{0:T(128)} %bitcast.core_ref, f32[1,40]{1,0:T(1,128)S(1)} %bitcast.48, bf16[128,2560]{1,0:T(8,128)(2,1)S(1)} %bitcast.25, bf16[128,2560]{1,0:T(8,128)(2,1)S(1)} %bitcast.31, ...), custom_call_target="tpu_custom_call" | custom-call | flops 800000000 | bytes 8000000 | tf_op jit(solution)/shard_map/gradients/pallas_call | solution.py:445
  123.0 26.9 %all_to_all.15 = f32[32,1,128]{2,1,0:T(1,128)S(1)} all-to-all(f32[32,1,128]{2,1,0:T(1,128)S(1)} %bitcast.44), channel_id=1, replica_groups=mesh['dp'=16,'ctx'=32] {'ctx'}, dimensions={0} | all-to-all | bytes 32768 | tf_op jit(solution)/shard_map/all_to_all | solution.py:459
  149.9 13.0 %all_to_all.16 = f32[16,1,128]{2,1,0:T(1,128)S(1)} all-to-all(f32[16,1,128]{2,1,0:T(1,128)S(1)} %broadcast_in_dim.22), channel_id=1, replica_groups=mesh['dp'=16,'ctx'=32] {'dp'}, dimensions={0} | all-to-all | bytes 16384 | tf_op jit(solution)/shard_map/all_to_all | solution.py:462
  162.9 0.6 fusion
  (68 shorter events, 1.3 us)
Async XLA Ops:
  0.6 1.1 copy-start
  1.7 1.1 copy-start.2
  2.8 0.8 copy-start.4
  3.6 0.8 copy-start.6
  4.3 0.7 copy-start.9
  5.1 0.7 copy-start.10
  8.4 11.5 %collective-permute-start = (f32[2592,128]{1,0:T(8,128)S(1)}, f32[2592,128]{1,0:T(8,128)S(1)}, u32[]{:S(2)}, u32[]{:S(2)}) collective-permute-start(f32[2592,128]{1,0:T(8,128)S(1)} %get-tuple-element.91), channel_id=1, source_target_pairs={{0,1},{1,0},{2,3},{3,2},{4,5},{5,4},{6,7},{7,6},{8,9},{9,8},{10,11... | collective-permute-start | bytes 3981320 | tf_op jit(solution)/shard_map/ppermute | solution.py:456
  19.9 5.3 %collective-permute-start.24 = (f32[648,128]{1,0:T(8,128)S(1)}, f32[648,128]{1,0:T(8,128)S(1)}, u32[]{:S(2)}, u32[]{:S(2)}) collective-permute-start(f32[648,128]{1,0:T(8,128)S(1)} %combine.54.refs_0_), channel_id=1, source_target_pairs={{1,3},{5,7},{9,11},{13,15},{17,19},{21,23},{25,27},{29,31},{30,28}... | collective-permute-start | bytes 995336 | tf_op jit(solution)/shard_map/ppermute | solution.py:363
  21.3 7.5 %collective-permute-start.16 = (f32[648,128]{1,0:T(8,128)S(1)}, f32[648,128]{1,0:T(8,128)S(1)}, u32[]{:S(2)}, u32[]{:S(2)}) collective-permute-start(f32[648,128]{1,0:T(8,128)S(1)} %combine.46.refs_0_), channel_id=1, source_target_pairs={{1,3},{5,7},{9,11},{13,15},{17,19},{21,23},{25,27},{29,31},{30,28}... | collective-permute-start | bytes 995336 | tf_op jit(solution)/shard_map/ppermute | solution.py:363
  22.7 11.9 %collective-permute-start.8 = (f32[648,128]{1,0:T(8,128)S(1)}, f32[648,128]{1,0:T(8,128)S(1)}, u32[]{:S(2)}, u32[]{:S(2)}) collective-permute-start(f32[648,128]{1,0:T(8,128)S(1)} %combine.38.refs_0_), channel_id=1, source_target_pairs={{1,3},{5,7},{9,11},{13,15},{17,19},{21,23},{25,27},{29,31},{30,28}... | collective-permute-start | bytes 995336 | tf_op jit(solution)/shard_map/ppermute | solution.py:363
  25.3 10.0 %collective-permute-start.25 = (f32[648,128]{1,0:T(8,128)S(1)}, f32[648,128]{1,0:T(8,128)S(1)}, u32[]{:S(2)}, u32[]{:S(2)}) collective-permute-start(f32[648,128]{1,0:T(8,128)S(1)} %combine.55), channel_id=1, source_target_pairs={{3,7},{11,15},{19,23},{28,24},{20,16},{12,8},{35,39},{43,47},{51,5... | collective-permute-start | bytes 995336 | tf_op jit(solution)/shard_map/ppermute | solution.py:363
  28.9 7.2 %collective-permute-start.17 = (f32[648,128]{1,0:T(8,128)S(1)}, f32[648,128]{1,0:T(8,128)S(1)}, u32[]{:S(2)}, u32[]{:S(2)}) collective-permute-start(f32[648,128]{1,0:T(8,128)S(1)} %combine.47), channel_id=1, source_target_pairs={{3,7},{11,15},{19,23},{28,24},{20,16},{12,8},{35,39},{43,47},{51,5... | collective-permute-start | bytes 995336 | tf_op jit(solution)/shard_map/ppermute | solution.py:363
  29.6 9.0 %collective-permute-start.1 = (f32[648,128]{1,0:T(8,128)S(1)}, f32[648,128]{1,0:T(8,128)S(1)}, u32[]{:S(2)}, u32[]{:S(2)}) collective-permute-start(f32[648,128]{1,0:T(8,128)S(1)} %combine.32.refs_0_), channel_id=1, source_target_pairs={{1,3},{5,7},{9,11},{13,15},{17,19},{21,23},{25,27},{29,31},{30,28}... | collective-permute-start | bytes 995336 | tf_op jit(solution)/shard_map/ppermute | solution.py:363
  34.6 4.7 %collective-permute-start.9 = (f32[648,128]{1,0:T(8,128)S(1)}, f32[648,128]{1,0:T(8,128)S(1)}, u32[]{:S(2)}, u32[]{:S(2)}) collective-permute-start(f32[648,128]{1,0:T(8,128)S(1)} %combine.39), channel_id=1, source_target_pairs={{3,7},{11,15},{19,23},{28,24},{20,16},{12,8},{35,39},{43,47},{51,5... | collective-permute-start | bytes 995336 | tf_op jit(solution)/shard_map/ppermute | solution.py:363
  35.4 4.7 %collective-permute-start.26 = (f32[648,128]{1,0:T(8,128)S(1)}, f32[648,128]{1,0:T(8,128)S(1)}, u32[]{:S(2)}, u32[]{:S(2)}) collective-permute-start(f32[648,128]{1,0:T(8,128)S(1)} %get-tuple-element.134), channel_id=1, source_target_pairs={{7,15},{3,5},{24,16},{28,26},{39,47},{35,37},{56,48},{60,58},{71,7... | collective-permute-start | bytes 995336 | tf_op jit(solution)/shard_map/ppermute | solution.py:363
  36.2 4.7 %collective-permute-start.18 = (f32[648,128]{1,0:T(8,128)S(1)}, f32[648,128]{1,0:T(8,128)S(1)}, u32[]{:S(2)}, u32[]{:S(2)}) collective-permute-start(f32[648,128]{1,0:T(8,128)S(1)} %get-tuple-element.125), channel_id=1, source_target_pairs={{7,15},{3,5},{24,16},{28,26},{39,47},{35,37},{56,48},{60,58},{71,7... | collective-permute-start | bytes 995336 | tf_op jit(solution)/shard_map/ppermute | solution.py:363
  38.6 3.0 %collective-permute-start.2 = (f32[648,128]{1,0:T(8,128)S(1)}, f32[648,128]{1,0:T(8,128)S(1)}, u32[]{:S(2)}, u32[]{:S(2)}) collective-permute-start(f32[648,128]{1,0:T(8,128)S(1)} %combine.33), channel_id=1, source_target_pairs={{3,7},{11,15},{19,23},{28,24},{20,16},{12,8},{35,39},{43,47},{51,5... | collective-permute-start | bytes 995336 | tf_op jit(solution)/shard_map/ppermute | solution.py:363
  39.4 3.0 %collective-permute-start.10 = (f32[648,128]{1,0:T(8,128)S(1)}, f32[648,128]{1,0:T(8,128)S(1)}, u32[]{:S(2)}, u32[]{:S(2)}) collective-permute-start(f32[648,128]{1,0:T(8,128)S(1)} %get-tuple-element.116), channel_id=1, source_target_pairs={{7,15},{3,5},{24,16},{28,26},{39,47},{35,37},{56,48},{60,58},{71,7... | collective-permute-start | bytes 995336 | tf_op jit(solution)/shard_map/ppermute | solution.py:363
  40.2 3.0 %collective-permute-start.27 = (f32[648,128]{1,0:T(8,128)S(1)}, f32[648,128]{1,0:T(8,128)S(1)}, u32[]{:S(2)}, u32[]{:S(2)}) collective-permute-start(f32[648,128]{1,0:T(8,128)S(1)} %get-tuple-element.136), channel_id=1, source_target_pairs={{15,23},{7,11},{16,8},{24,20},{47,55},{39,43},{48,40},{56,52},{79,... | collective-permute-start | bytes 995336 | tf_op jit(solution)/shard_map/ppermute | solution.py:363
  41.0 3.0 %collective-permute-start.19 = (f32[648,128]{1,0:T(8,128)S(1)}, f32[648,128]{1,0:T(8,128)S(1)}, u32[]{:S(2)}, u32[]{:S(2)}) collective-permute-start(f32[648,128]{1,0:T(8,128)S(1)} %get-tuple-element.127), channel_id=1, source_target_pairs={{15,23},{7,11},{16,8},{24,20},{47,55},{39,43},{48,40},{56,52},{79,... | collective-permute-start | bytes 995336 | tf_op jit(solution)/shard_map/ppermute | solution.py:363
  41.7 3.0 %collective-permute-start.3 = (f32[648,128]{1,0:T(8,128)S(1)}, f32[648,128]{1,0:T(8,128)S(1)}, u32[]{:S(2)}, u32[]{:S(2)}) collective-permute-start(f32[648,128]{1,0:T(8,128)S(1)} %get-tuple-element.93), channel_id=1, source_target_pairs={{7,15},{3,5},{24,16},{28,26},{39,47},{35,37},{56,48},{60,58},{71,7... | collective-permute-start | bytes 995336 | tf_op jit(solution)/shard_map/ppermute | solution.py:363
  42.5 3.0 %collective-permute-start.11 = (f32[648,128]{1,0:T(8,128)S(1)}, f32[648,128]{1,0:T(8,128)S(1)}, u32[]{:S(2)}, u32[]{:S(2)}) collective-permute-start(f32[648,128]{1,0:T(8,128)S(1)} %get-tuple-element.118), channel_id=1, source_target_pairs={{15,23},{7,11},{16,8},{24,20},{47,55},{39,43},{48,40},{56,52},{79,... | collective-permute-start | bytes 995336 | tf_op jit(solution)/shard_map/ppermute | solution.py:363
  43.3 3.0 %collective-permute-start.28 = (f32[648,128]{1,0:T(8,128)S(1)}, f32[648,128]{1,0:T(8,128)S(1)}, u32[]{:S(2)}, u32[]{:S(2)}) collective-permute-start(f32[648,128]{1,0:T(8,128)S(1)} %get-tuple-element.138), channel_id=1, source_target_pairs={{23,27},{15,19},{11,13},{7,9},{8,4},{16,12},{20,18},{24,22},{55,59... | collective-permute-start | bytes 995336 | tf_op jit(solution)/shard_map/ppermute | solution.py:363
  44.1 3.7 %collective-permute-start.20 = (f32[648,128]{1,0:T(8,128)S(1)}, f32[648,128]{1,0:T(8,128)S(1)}, u32[]{:S(2)}, u32[]{:S(2)}) collective-permute-start(f32[648,128]{1,0:T(8,128)S(1)} %get-tuple-element.129), channel_id=1, source_target_pairs={{23,27},{15,19},{11,13},{7,9},{8,4},{16,12},{20,18},{24,22},{55,59... | collective-permute-start | bytes 995336 | tf_op jit(solution)/shard_map/ppermute | solution.py:363
  44.8 3.7 %collective-permute-start.4 = (f32[648,128]{1,0:T(8,128)S(1)}, f32[648,128]{1,0:T(8,128)S(1)}, u32[]{:S(2)}, u32[]{:S(2)}) collective-permute-start(f32[648,128]{1,0:T(8,128)S(1)} %get-tuple-element.95), channel_id=1, source_target_pairs={{15,23},{7,11},{16,8},{24,20},{47,55},{39,43},{48,40},{56,52},{79,... | collective-permute-start | bytes 995336 | tf_op jit(solution)/shard_map/ppermute | solution.py:363
  45.6 3.7 %collective-permute-start.12 = (f32[648,128]{1,0:T(8,128)S(1)}, f32[648,128]{1,0:T(8,128)S(1)}, u32[]{:S(2)}, u32[]{:S(2)}) collective-permute-start(f32[648,128]{1,0:T(8,128)S(1)} %get-tuple-element.120), channel_id=1, source_target_pairs={{23,27},{15,19},{11,13},{7,9},{8,4},{16,12},{20,18},{24,22},{55,59... | collective-permute-start | bytes 995336 | tf_op jit(solution)/shard_map/ppermute | solution.py:363
  46.4 3.7 %collective-permute-start.29 = (f32[648,128]{1,0:T(8,128)S(1)}, f32[648,128]{1,0:T(8,128)S(1)}, u32[]{:S(2)}, u32[]{:S(2)}) collective-permute-start(f32[648,128]{1,0:T(8,128)S(1)} %get-tuple-element.140), channel_id=1, source_target_pairs={{15,17},{19,21},{23,25},{27,29},{16,14},{12,10},{8,6},{4,2},{47,49... | collective-permute-start | bytes 995336 | tf_op jit(solution)/shard_map/ppermute | solution.py:363
  47.1 3.7 %collective-permute-start.30 = (f32[648,128]{1,0:T(8,128)S(1)}, f32[648,128]{1,0:T(8,128)S(1)}, u32[]{:S(2)}, u32[]{:S(2)}) collective-permute-start(f32[648,128]{1,0:T(8,128)S(1)} %get-tuple-element.140), channel_id=1, source_target_pairs={{27,31},{4,0},{59,63},{36,32},{91,95},{68,64},{123,127},{100,96},{... | collective-permute-start | bytes 995336 | tf_op jit(solution)/shard_map/ppermute | solution.py:365
  47.9 3.7 %collective-permute-start.21 = (f32[648,128]{1,0:T(8,128)S(1)}, f32[648,128]{1,0:T(8,128)S(1)}, u32[]{:S(2)}, u32[]{:S(2)}) collective-permute-start(f32[648,128]{1,0:T(8,128)S(1)} %get-tuple-element.131), channel_id=1, source_target_pairs={{15,17},{19,21},{23,25},{27,29},{16,14},{12,10},{8,6},{4,2},{47,49... | collective-permute-start | bytes 995336 | tf_op jit(solution)/shard_map/ppermute | solution.py:363
  48.6 45.3 %collective-permute-start.22 = (f32[648,128]{1,0:T(8,128)S(1)}, f32[648,128]{1,0:T(8,128)S(1)}, u32[]{:S(2)}, u32[]{:S(2)}) collective-permute-start(f32[648,128]{1,0:T(8,128)S(1)} %get-tuple-element.131), channel_id=1, source_target_pairs={{27,31},{4,0},{59,63},{36,32},{91,95},{68,64},{123,127},{100,96},{... | collective-permute-start | bytes 995336 | tf_op jit(solution)/shard_map/ppermute | solution.py:365
  49.3 50.2 %collective-permute-start.5 = (f32[648,128]{1,0:T(8,128)S(1)}, f32[648,128]{1,0:T(8,128)S(1)}, u32[]{:S(2)}, u32[]{:S(2)}) collective-permute-start(f32[648,128]{1,0:T(8,128)S(1)} %get-tuple-element.97), channel_id=1, source_target_pairs={{23,27},{15,19},{11,13},{7,9},{8,4},{16,12},{20,18},{24,22},{55,59... | collective-permute-start | bytes 995336 | tf_op jit(solution)/shard_map/ppermute | solution.py:363
  50.1 50.2 %collective-permute-start.13 = (f32[648,128]{1,0:T(8,128)S(1)}, f32[648,128]{1,0:T(8,128)S(1)}, u32[]{:S(2)}, u32[]{:S(2)}) collective-permute-start(f32[648,128]{1,0:T(8,128)S(1)} %get-tuple-element.122), channel_id=1, source_target_pairs={{15,17},{19,21},{23,25},{27,29},{16,14},{12,10},{8,6},{4,2},{47,49... | collective-permute-start | bytes 995336 | tf_op jit(solution)/shard_map/ppermute | solution.py:363
  50.8 50.3 %collective-permute-start.14 = (f32[648,128]{1,0:T(8,128)S(1)}, f32[648,128]{1,0:T(8,128)S(1)}, u32[]{:S(2)}, u32[]{:S(2)}) collective-permute-start(f32[648,128]{1,0:T(8,128)S(1)} %get-tuple-element.122), channel_id=1, source_target_pairs={{27,31},{4,0},{59,63},{36,32},{91,95},{68,64},{123,127},{100,96},{... | collective-permute-start | bytes 995336 | tf_op jit(solution)/shard_map/ppermute | solution.py:365
  51.6 61.1 %collective-permute-start.31 = (f32[648,128]{1,0:T(8,128)S(1)}, f32[648,128]{1,0:T(8,128)S(1)}, u32[]{:S(2)}, u32[]{:S(2)}) collective-permute-start(f32[648,128]{1,0:T(8,128)S(1)} %combine.61.rest_9_), channel_id=1, source_target_pairs={{0,1},{1,0},{2,3},{3,2},{4,5},{5,4},{6,7},{7,6},{8,9},{9,8},{10,11... | collective-permute-start | bytes 995336 | tf_op jit(solution)/shard_map/ppermute | solution.py:378
  93.9 20.3 %collective-permute-start.23 = (f32[648,128]{1,0:T(8,128)S(1)}, f32[648,128]{1,0:T(8,128)S(1)}, u32[]{:S(2)}, u32[]{:S(2)}) collective-permute-start(f32[648,128]{1,0:T(8,128)S(1)} %combine.53.rest_9_), channel_id=1, source_target_pairs={{0,1},{1,0},{2,3},{3,2},{4,5},{5,4},{6,7},{7,6},{8,9},{9,8},{10,11... | collective-permute-start | bytes 995336 | tf_op jit(solution)/shard_map/ppermute | solution.py:378
  99.5 7.5 %copy-start.5 = (bf16[1,128,128]{2,1,0:T(8,128)(2,1)S(1)}, bf16[1,128,128]{2,1,0:T(8,128)(2,1)}, u32[]{:S(2)}) copy-start(bf16[1,128,128]{2,1,0:T(8,128)(2,1)} %param.8) | copy-start | bytes 98308
  99.5 7.4 %copy-start.7 = (bf16[1,128,128]{2,1,0:T(8,128)(2,1)S(1)}, bf16[1,128,128]{2,1,0:T(8,128)(2,1)}, u32[]{:S(2)}) copy-start(bf16[1,128,128]{2,1,0:T(8,128)(2,1)} %param.9) | copy-start | bytes 98308
  99.6 17.3 %collective-permute-start.6 = (f32[648,128]{1,0:T(8,128)S(1)}, f32[648,128]{1,0:T(8,128)S(1)}, u32[]{:S(2)}, u32[]{:S(2)}) collective-permute-start(f32[648,128]{1,0:T(8,128)S(1)} %get-tuple-element.98), channel_id=1, source_target_pairs={{15,17},{19,21},{23,25},{27,29},{16,14},{12,10},{8,6},{4,2},{47,49... | collective-permute-start | bytes 995336 | tf_op jit(solution)/shard_map/ppermute | solution.py:363
  100.3 16.6 %collective-permute-start.7 = (f32[648,128]{1,0:T(8,128)S(1)}, f32[648,128]{1,0:T(8,128)S(1)}, u32[]{:S(2)}, u32[]{:S(2)}) collective-permute-start(f32[648,128]{1,0:T(8,128)S(1)} %get-tuple-element.98), channel_id=1, source_target_pairs={{27,31},{4,0},{59,63},{36,32},{91,95},{68,64},{123,127},{100,96},{... | collective-permute-start | bytes 995336 | tf_op jit(solution)/shard_map/ppermute | solution.py:365
  101.1 11.6 %copy-start.1 = (bf16[1,128,2560]{2,1,0:T(8,128)(2,1)S(1)}, bf16[1,128,2560]{2,1,0:T(8,128)(2,1)}, u32[]{:S(2)}) copy-start(bf16[1,128,2560]{2,1,0:T(8,128)(2,1)} %param.7) | copy-start | bytes 1966084
  101.1 11.6 %copy-start.3 = (bf16[1,128,2560]{2,1,0:T(8,128)(2,1)S(1)}, bf16[1,128,2560]{2,1,0:T(8,128)(2,1)}, u32[]{:S(2)}) copy-start(bf16[1,128,2560]{2,1,0:T(8,128)(2,1)} %param.13) | copy-start | bytes 1966084
  101.2 11.6 %copy-start.8 = (f32[40]{0:T(128)S(1)}, f32[40]{0:T(128)}, u32[]{:S(2)}) copy-start(f32[40]{0:T(128)} %param.12) | copy-start | bytes 484
  101.2 14.3 %collective-permute-start.15 = (f32[648,128]{1,0:T(8,128)S(1)}, f32[648,128]{1,0:T(8,128)S(1)}, u32[]{:S(2)}, u32[]{:S(2)}) collective-permute-start(f32[648,128]{1,0:T(8,128)S(1)} %combine.45.rest_9_), channel_id=1, source_target_pairs={{0,1},{1,0},{2,3},{3,2},{4,5},{5,4},{6,7},{7,6},{8,9},{9,8},{10,11... | collective-permute-start | bytes 995336 | tf_op jit(solution)/shard_map/ppermute | solution.py:378
  117.0 3.5 %collective-permute-start.32 = (f32[648,128]{1,0:T(8,128)S(1)}, f32[648,128]{1,0:T(8,128)S(1)}, u32[]{:S(2)}, u32[]{:S(2)}) collective-permute-start(f32[648,128]{1,0:T(8,128)S(1)} %combine.63.rest_9_), channel_id=1, source_target_pairs={{0,1},{1,0},{2,3},{3,2},{4,5},{5,4},{6,7},{7,6},{8,9},{9,8},{10,11... | collective-permute-start | bytes 995336 | tf_op jit(solution)/shard_map/ppermute | solution.py:378

commit v4 on v3

--- a/solution.py
+++ b/solution.py
@@ -11,7 +11,12 @@
 BF16 = jnp.bfloat16
 HIGHEST = lax.Precision.HIGHEST
 LANES = 128
-STREAMS = 4
+SIZES = (5, 5, 5, 5)
+STREAMS = len(SIZES)
+STARTS = tuple(sum(SIZES[:i]) for i in range(STREAMS))
+LOG_ROWS = 8
+ROWS = tuple(size * LANES + LOG_ROWS for size in SIZES)
+BASES = tuple(sum(ROWS[:i]) for i in range(STREAMS))
 VMEM_LIMIT = 20 * 1024 * 1024
 
 
@@ -72,50 +77,35 @@
     queries_t = c_ref[...].astype(F32).T.astype(BF16)
     keys_t = jnp.concatenate([keys_t, keys_t], axis=1)
     queries_t = jnp.concatenate([queries_t, queries_t], axis=1)
-    per = blocks // STREAMS
-    packed_rows = keeps[0].shape[0]
-    for block in range(blocks):
-        stream, place = block // per, block % per
+    for stream, place in [(i, j) for i in range(STREAMS) for j in range(SIZES[i])]:
+        block = STARTS[stream] + place
         cols = pl.ds(block * LANES, LANES)
         weighted = spread(weight, block, first) * x_ref[:, cols].astype(F32)
         lifted = spread(lift, block, first) * g_ref[:, cols].astype(F32)
         state = nn(keys_t, jnp.concatenate(halves(weighted), axis=0))
         message = nn(queries_t, jnp.concatenate(halves(lifted), axis=0))
         keeps[stream][pl.ds(place * LANES, LANES), :] = jnp.where(forward, state, message)
-        sends[pl.ds(stream * packed_rows + place * LANES, LANES), :] = jnp.where(forward, message, state)
+        sends[pl.ds(BASES[stream] + place * LANES, LANES), :] = jnp.where(forward, message, state)
     for stream in range(STREAMS):
-        extra = packed_rows - per * LANES
-        logs = [
-            spread(closing, stream * per + place, first[:1]) for place in range(per)
-        ] + [jnp.zeros((extra - per, LANES), F32)]
-        logs = jnp.concatenate(logs, axis=0)
-        keeps[stream][pl.ds(per * LANES, extra), :] = logs
-        sends[pl.ds(stream * packed_rows + per * LANES, extra), :] = logs
-
-
-def local_kernel(
-    heads,
-    blocks,
-    raw_ref,
-    decay_ref,
-    x_ref,
-    g_ref,
-    b_ref,
-    c_ref,
-    adjoint_ref,
-    keys_ref,
-    queries_ref,
-    through_ref,
-    column_ref,
-    step_ref,
-    cumulative_ref,
-    slope_ref,
-    rate_ref,
-    skip_ref,
-    wide,
-    row_t,
-):
-    raw, step, rate, cumulative = head_terms(raw_ref, decay_ref, wide, heads)
+        size = SIZES[stream]
+        logs = [spread(closing, STARTS[stream] + place, first[:1]) for place in range(size)]
+        logs = jnp.concatenate(logs + [jnp.zeros((LOG_ROWS - size, LANES), F32)], axis=0)
+        keeps[stream][pl.ds(size * LANES, LOG_ROWS), :] = logs
+        sends[pl.ds(BASES[stream] + size * LANES, LOG_ROWS), :] = logs
+
+
+def local_kernel(heads, blocks, part, *refs):
+    start, stop = (0, SIZES[0]) if part == 0 else (SIZES[0], blocks)
+    if part == 0:
+        raw_ref, decay_ref, x_ref, g_ref, b_ref, c_ref = refs[:6]
+        outs, (wide, row_t) = refs[6:15], refs[15:]
+        raw, step, rate, cumulative = head_terms(raw_ref, decay_ref, wide, heads)
+    else:
+        x_ref, g_ref, b_ref, c_ref = refs[:4]
+        gathered_in, row_in, column_in, skip_in, step_ref, cumulative_ref = refs[4:10]
+        outs, (row_t,) = refs[10:16], refs[16:]
+        step = step_ref[...]
+        cumulative = cumulative_ref[...]
     rows = cumulative.shape[0]
     lane = iota((rows, LANES), 1)
     first = lane < LANES // 2
@@ -124,13 +114,20 @@
     keys = b_ref[...]
     queries = c_ref[...]
     scores_t = jnp.where(causal, nt(keys, queries), 0.0)
-    row_t[...] = jnp.zeros_like(row_t)
-    gathered = jnp.zeros((rows, rows), F32)
-    column_step = jnp.zeros((rows, LANES), F32)
-    skip = jnp.zeros((1, LANES), F32)
     lane_one = iota((1, LANES), 1)
     zero = jnp.zeros((rows, LANES), BF16)
-    for block in range(blocks):
+    if part == 0:
+        row_t[...] = jnp.zeros_like(row_t)
+        gathered = jnp.zeros((rows, rows), F32)
+        column_step = jnp.zeros((rows, LANES), F32)
+        skip = jnp.zeros((1, LANES), F32)
+    else:
+        row_t[...] = row_in[...]
+        gathered = gathered_in[...]
+        column_step = column_in[...]
+        skip = skip_in[...]
+    for block in range(start, stop):
+        place = block - start
         cols = pl.ds(block * LANES, LANES)
         x = x_ref[:, cols]
         g = g_ref[:, cols]
@@ -138,19 +135,19 @@
         both_g = jnp.concatenate([jnp.where(first, g, zero), jnp.where(first, zero, g)], axis=0)
         products = nt(both_x, g)
         highs, lows = [], []
-        for half in range(2):
-            head = 2 * block + half
+        for side in range(2):
+            head = 2 * block + side
             between = cumulative_t[head : head + 1, :] - cumulative[:, head : head + 1]
             decay = jnp.exp(jnp.minimum(between, 0.0))
             high, low = halves(decay * scores_t)
             highs.append(high)
             lows.append(low)
-            scaled = decay * products[half * rows : (half + 1) * rows] * step[:, head : head + 1]
+            scaled = decay * products[side * rows : (side + 1) * rows] * step[:, head : head + 1]
             gathered = gathered + scaled
             scored = scaled * scores_t
             row_t[head : head + 1, :] = jnp.sum(scored, axis=0, keepdims=True)
             column_step = jnp.where(lane == head, jnp.sum(scored, axis=1, keepdims=True), column_step)
-        adjoint_ref[:, cols] = nn(jnp.concatenate(highs, axis=1), both_g) + nn(
+        outs[0][:, pl.ds(place * LANES, LANES)] = nn(jnp.concatenate(highs, axis=1), both_g) + nn(
             jnp.concatenate(lows, axis=1), both_g
         )
         met = jnp.sum(x.astype(F32) * g.astype(F32), axis=0, keepdims=True)
@@ -158,20 +155,19 @@
         late = jnp.sum(jnp.where(first[:1], 0.0, met), axis=1, keepdims=True)
         skip = jnp.where(lane_one == 2 * block, early, skip)
         skip = jnp.where(lane_one == 2 * block + 1, late, skip)
-    gathered = jnp.where(causal, gathered, 0.0)
-    keys_ref[...] = nn(
-        jnp.concatenate(halves(gathered), axis=1), jnp.concatenate([queries, queries], axis=0)
-    )
-    queries_ref[...] = nn(
-        jnp.concatenate(halves(gathered.T), axis=1), jnp.concatenate([keys, keys], axis=0)
-    )
-    through_ref[...] = row_t[...].T - column_step
-    column_ref[...] = column_step / step
-    step_ref[...] = step
-    cumulative_ref[...] = cumulative
-    slope_ref[...] = 1.0 / (1.0 + jnp.exp(-raw))
-    rate_ref[...] = rate
-    skip_ref[...] = skip
+    if part == 0:
+        values = (gathered, row_t[...], column_step, skip, step, cumulative, 1.0 / (1.0 + jnp.exp(-raw)), rate)
+    else:
+        gathered = jnp.where(causal, gathered, 0.0)
+        values = (
+            nn(jnp.concatenate(halves(gathered), axis=1), jnp.concatenate([queries, queries], axis=0)),
+            nn(jnp.concatenate(halves(gathered.T), axis=1), jnp.concatenate([keys, keys], axis=0)),
+            row_t[...].T - column_step,
+            column_step / step,
+            skip,
+        )
+    for out, value in zip(outs[1:], values):
+        out[...] = value
 
 
 def gradient_kernel(heads, blocks, stream, core_ref, skip_weight_ref, x_ref, g_ref, b_ref, c_ref, *rest):
@@ -198,7 +194,6 @@
     queries = jnp.concatenate([c_ref[...], c_ref[...]], axis=1)
     side = iota((LANES, LANES), 0) // (LANES // 2)
     place_lane = iota((LANES, LANES), 1)
-    per = blocks // STREAMS
     from_keys = taken[0][...]
     from_queries = taken[1][...]
     if stream == 0:
@@ -210,15 +205,15 @@
         inward_sum = taken[3][...]
         meeting = taken[4][...]
     grad_x = rest[0]
-    base = stream * before_ref.shape[0]
+    base, size, start = BASES[stream], SIZES[stream], STARTS[stream]
     if stream > 0:
-        ready = pl.ds(0, stream * per * LANES)
+        ready = pl.ds(0, start * LANES)
         grad_x[:, ready] = taken[5][:, ready]
-    for place in range(per):
-        block = stream * per + place
+    for place in range(size):
+        block = start + place
         cols = pl.ds(block * LANES, LANES)
         where = pl.ds(place * LANES, LANES)
-        log_row = pair_ref[pl.ds(base + per * LANES + place, 1), :]
+        log_row = pair_ref[pl.ds(base + size * LANES + place, 1), :]
         mine = pair_ref[pl.ds(base + place * LANES, LANES), :] + jnp.exp(log_row) * before_ref[where, :]
         theirs = other_ref[where, :]
         entering = jnp.where(forward, mine, theirs)
@@ -257,7 +252,8 @@
         late = jnp.sum(jnp.where(first[:1], 0.0, met), axis=1, keepdims=True)
         meeting = jnp.where(lane_one == 2 * block, early, meeting)
         meeting = jnp.where(lane_one == 2 * block + 1, late, meeting)
-        grad = step_b * (adjoint_ref[:, cols] + tail_b * message_keys) + skip_b * g
+        near = pl.ds((block if stream == 0 else block - SIZES[0]) * LANES, LANES)
+        grad = step_b * (adjoint_ref[:, near] + tail_b * message_keys) + skip_b * g
         grad_x[:, cols] = grad.astype(grad_x.dtype)
     rest[1][...] = from_keys
     rest[2][...] = from_queries
@@ -284,18 +280,16 @@
     sums[...] = jnp.broadcast_to(wide[0:1, :], sums.shape)
 
 
-def combine_kernel(per, base, has_before, wants_send, *refs):
+def combine_kernel(size, has_before, wants_send, *refs):
     refs = list(refs)
     own = refs.pop(0) if wants_send else None
     past = refs.pop(0) if has_before else None
     arrived = refs.pop(0)
     new_past = refs.pop(0) if has_before else None
     send = refs.pop(0) if wants_send else None
-    extra = (per + 7) // 8 * 8
-    tail = pl.ds(per * LANES, extra)
+    tail = pl.ds(size * LANES, LOG_ROWS)
     past_log = past[tail, :] if has_before else None
-    new_log = arrived[pl.ds(base + per * LANES, extra), :]
-    new_log = new_log + past_log if has_before else new_log
+    new_log = arrived[tail, :] + past_log if has_before else arrived[tail, :]
     if has_before:
         new_past[tail, :] = new_log
         past_decay = jnp.exp(past_log)
@@ -303,9 +297,9 @@
         own_log = own[tail, :]
         own_decay = jnp.exp(own_log)
         send[tail, :] = own_log + new_log
-    for place in range(per):
+    for place in range(size):
         where = pl.ds(place * LANES, LANES)
-        state = arrived[pl.ds(base + place * LANES, LANES), :]
+        state = arrived[where, :]
         if has_before:
             state = past[where, :] + past_decay[place : place + 1, :] * state
             new_past[where, :] = state
@@ -330,15 +324,14 @@
 LAST_CHIP = [(13, 15)]
 
 
-def combine(per, own, past, arrived, base=0):
-    rows = per * LANES + (per + 7) // 8 * 8
-    shape = jax.ShapeDtypeStruct((rows, LANES), F32)
+def combine(size, own, past, arrived):
+    shape = jax.ShapeDtypeStruct(arrived.shape, F32)
     operands = [a for a in (own, past, arrived) if a is not None]
     whole = pl.BlockSpec(memory_space=pltpu.VMEM)
     outs = (past is not None) + (own is not None)
     results = list(
         pl.pallas_call(
-            functools.partial(combine_kernel, per, base, past is not None, own is not None),
+            functools.partial(combine_kernel, size, past is not None, own is not None),
             out_shape=[shape] * outs,
             in_specs=[whole] * len(operands),
             out_specs=[whole] * outs,
@@ -351,12 +344,33 @@
     return new_past, (results.pop(0) if own is not None else None)
 
 
-def scan_chips(keeps, pair, per, swap, within, gradients):
+def first_kernel(*refs):
+    keeps, pair, owns = refs[:STREAMS], refs[STREAMS], refs[STREAMS + 1 :]
+    for keep, own, base, size in zip(keeps, owns, BASES, SIZES):
+        tail = pl.ds(size * LANES, LOG_ROWS)
+        log = keep[tail, :]
+        decay = jnp.exp(log)
+        own[tail, :] = log + pair[pl.ds(base + size * LANES, LOG_ROWS), :]
+        for place in range(size):
+            where = pl.ds(place * LANES, LANES)
+            own[where, :] = keep[where, :] + decay[place : place + 1, :] * pair[pl.ds(base + place * LANES, LANES), :]
+
+
+def scan_chips(keeps, pair, swap, within, gradients):
     chips = 16
-    rows = keeps[0].shape[0]
-    own = [combine(per, keep, None, pair, i * rows)[1] for i, keep in enumerate(keeps)]
+    whole = pl.BlockSpec(memory_space=pltpu.VMEM)
+    own = pl.pallas_call(
+        first_kernel,
+        out_shape=[jax.ShapeDtypeStruct(keep.shape, F32) for keep in keeps],
+        in_specs=[whole] * (STREAMS + 1),
+        out_specs=[whole] * STREAMS,
+        compiler_params=pltpu.CompilerParams(vmem_limit_bytes=8 * 1024 * 1024),
+        cost_estimate=pl.CostEstimate(flops=1_000_000, bytes_accessed=4_000_000, transcendentals=0),
+        name="pair_up",
+    )(*keeps, pair)
     send, past = list(own), [None] * STREAMS
     final = len(ROUNDS) - 1
+    carried = None
     for turn, moves in enumerate(ROUNDS):
         arrived = []
         for stream in range(STREAMS):
@@ -364,15 +378,18 @@
             if turn == final:
                 got.append(lax.ppermute(send[stream], "ctx", chip_moves(LAST_CHIP, chips)))
             arrived.append(got)
-        if turn == final:
-            local = within(send[-1])
-            carried = None
+        if turn == 0:
+            local = within(own[-1])
+            arrived[0], local = lax.optimization_barrier((arrived[0], local))
+        if turn > 0:
+            arrived[0], _ = lax.optimization_barrier((arrived[0], previous))
+        previous = arrived[-1]
         for stream in range(STREAMS):
             if turn == final and stream == STREAMS - 1 and stream > 0:
                 arrived[stream], carried = lax.optimization_barrier((arrived[stream], carried))
             for block in arrived[stream]:
                 target = own[stream] if turn < final else None
-                past[stream], new_send = combine(per, target, past[stream], block)
+                past[stream], new_send = combine(SIZES[stream], target, past[stream], block)
                 send[stream] = new_send if new_send is not None else send[stream]
             if turn == final:
                 other = lax.ppermute(past[stream], "ctx", swap)
@@ -385,8 +402,6 @@
     width = inputs.shape[2]
     heads = decay_log.shape[0]
     blocks = width // LANES
-    per = blocks // STREAMS
-    extra = (per + 7) // 8 * 8
     count = lax.axis_size("ctx")
     swap = [(i, i ^ 1) for i in range(count)]
     core = lax.rem(lax.axis_index("ctx"), 2).astype(jnp.int32).reshape(1)
@@ -399,14 +414,14 @@
     params = pltpu.CompilerParams(vmem_limit_bytes=VMEM_LIMIT)
     tile = jax.ShapeDtypeStruct((rows, LANES), F32)
     line = jax.ShapeDtypeStruct((1, LANES), F32)
-    packed = jax.ShapeDtypeStruct((per * LANES + extra, LANES), F32)
+    packed = [jax.ShapeDtypeStruct((count_rows, LANES), F32) for count_rows in (*ROWS, sum(ROWS))]
     wide = pltpu.VMEM((rows, LANES), F32)
 
     operands = (raw_t, decay_row, x, g, keys, queries)
     far = pl.BlockSpec(memory_space=pltpu.HBM)
     made = pl.pallas_call(
         functools.partial(summary_kernel, heads, blocks),
-        out_shape=[packed] * STREAMS + [jax.ShapeDtypeStruct((STREAMS * packed.shape[0], LANES), F32)],
+        out_shape=packed,
         in_specs=[scalar] + [far] * 6,
         out_specs=[whole] * (STREAMS + 1),
         scratch_shapes=[pltpu.VMEM(a.shape, a.dtype) for a in operands]
@@ -417,18 +432,30 @@
     )(core, *operands)
     keeps, sends = made[:STREAMS], made[STREAMS]
 
-    def within_slab(after):
-        held, _ = lax.optimization_barrier((operands, after))
+    parts = [jax.ShapeDtypeStruct((rows, n * LANES), F32) for n in (SIZES[0], blocks - SIZES[0])]
+    row_scratch = pltpu.VMEM((LANES, rows), F32)
+
+    def local_part(part, held, out_shape, scratch):
         return pl.pallas_call(
-            functools.partial(local_kernel, heads, blocks),
-            out_shape=[jax.ShapeDtypeStruct((rows, width), F32)] + [tile] * 7 + [line] * 2,
-            in_specs=[whole] * 6,
-            out_specs=[whole] * 10,
-            scratch_shapes=[wide, pltpu.VMEM((LANES, rows), F32)],
+            functools.partial(local_kernel, heads, blocks, part),
+            out_shape=out_shape,
+            in_specs=[whole] * len(held),
+            out_specs=[whole] * len(out_shape),
+            scratch_shapes=scratch,
             compiler_params=params,
-            cost_estimate=pl.CostEstimate(flops=2_000_000_000, bytes_accessed=4_000_000, transcendentals=0),
+            cost_estimate=pl.CostEstimate(flops=1_000_000_000, bytes_accessed=3_000_000, transcendentals=0),
             name="within_slab",
         )(*held)
+
+    held, keeps = lax.optimization_barrier((operands, keeps))
+    pair = lax.ppermute(sends, "ctx", swap)
+    early = local_part(0, held, [parts[0]] + [tile] * 3 + [line] + [tile] * 3 + [line], [wide, row_scratch])
+    pair, early = lax.optimization_barrier((pair, early))
+
+    def within_slab(after):
+        again, _ = lax.optimization_barrier(((*operands[2:], *early[1:7]), after))
+        late = local_part(1, again, [parts[1]] + [tile] * 4 + [line], [row_scratch])
+        return [early[0], late[0], *late[1:5], *early[5:9], late[5]]
 
     full = jax.ShapeDtypeStruct((rows, width), BF16)
 
@@ -439,7 +466,8 @@
             shapes += [jax.ShapeDtypeStruct((heads, rows), F32), jax.ShapeDtypeStruct((count, LANES), F32)]
         else:
             shapes += [tile, tile, line]
-        adjoint, keys_part, queries_part, *terms = local
+        adjoint = local[0] if stream == 0 else local[1]
+        keys_part, queries_part, *terms = local[2:]
         carried = [keys_part, queries_part] if carried is None else [*carried[1:], carried[0]]
         given = [core, skip_row, x, g, keys, queries, adjoint, *terms, pair, before, other, *carried]
         return pl.pallas_call(
@@ -453,8 +481,7 @@
             name="gradients",
         )(*given)
 
-    pair = lax.ppermute(sends, "ctx", swap)
-    done = scan_chips(keeps, pair, per, swap, within_slab, gradients)
+    done = scan_chips(keeps, pair, swap, within_slab, gradients)
     grad_x, grad_keys, grad_queries, grad_raw_t, shared = done
     shared = lax.all_to_all(shared, "ctx", 0, 0, tiled=True)
     line_sum = jnp.sum(shared, axis=0)

time: 165 us -> 167 us (1.012)
  starting transfers between devices: 89.5 us -> 104 us
  blocking collectives: 39.8 us -> 31.3 us
  waiting for transfers between devices: 10.2 us -> 7.61 us
    ppermute x4, starting transfers between devices: 55.5 us -> 73 us  [scan_chips(): other = lax.ppermute(past[stream], 'ctx', swap)]
    all_to_all x1, blocking collectives: 26.9 us -> 18.3 us  [per_device(): shared = lax.all_to_all(shared, 'ctx', 0, 0, tiled=True)]
    ppermute x24, starting transfers between devices: 22.5 us -> 19 us  [scan_chips(): got = [lax.ppermute(send[stream], 'ctx', chip_moves(moves, chips))]]
    pallas_call x33 -> x31, Pallas kernels: 7.61 us -> 7.41 us  [the longest x2 5.56 us: local_part(): pl.pallas_call(functools.partial(local_kernel, heads, blocks, part), out_...]
  transfers between devices with their start and end apart: 33 -> 33, of which waited for: 5 -> 4; matrix products, arithmetic and copies ran while one was open for 0% -> 0% of each run, Pallas kernels for 7% -> 7%
where the time goes in v4:
time: 167 us; the launch traced here: 166 us
  starting transfers between devices  104 us (62%)
  blocking collectives  31.3 us (19%)
  Pallas kernels  16.6 us (10%)
  waiting for transfers between devices  7.61 us (5%)
  local copies, waits for them, and re-layouts  5.68 us (3%)
    ppermute x4, starting transfers between devices, scan_chips(): other = lax.ppermute(past[stream], 'ctx', swap)  73 us
    ppermute x24, starting transfers between devices, scan_chips(): got = [lax.ppermute(send[stream], 'ctx', chip_moves(moves, chips))]  19 us
    all_to_all x1, blocking collectives, per_device(): shared = lax.all_to_all(shared, 'ctx', 0, 0, tiled=True)  18.3 us
    all_to_all x1, blocking collectives, per_device(): line_sum = jnp.sum(lax.all_to_all(shared, 'dp', 0, 0, tiled=True), axis=0)  13 us
    ppermute x1, starting transfers between devices, per_device(): pair = lax.ppermute(sends, 'ctx', swap)  8.79 us
    pallas_call x4, Pallas kernels, gradients(): pl.pallas_call(functools.partial(gradient_kernel, heads, blocks, stream),...  6.48 us
    pallas_call x2, Pallas kernels, local_part(): pl.pallas_call(functools.partial(local_kernel, heads, blocks, part), out_...  5.56 us
    ppermute x24, waiting for transfers between devices, scan_chips(): got = [lax.ppermute(send[stream], 'ctx', chip_moves(moves, chips))]  5.11 us
  transfers between devices with their start and end apart: 33, of which 4 were waited for; matrix products, arithmetic and copies ran while one was open for 0% of the time, Pallas kernels for 7%

profile of v4, /device:TPU:1, one launch (start us, length us, event | category | flops | bytes accessed | tf_op | source)
XLA Modules:
  0.0 166.3 jit_solution(5471113954958299102)
XLA Ops:
  0.6 1.1 copy-done
  1.7 1.1 copy-done.2
  2.8 0.8 copy-done.4
  3.6 0.8 copy-done.6
  4.3 0.7 copy-done.9
  5.1 0.7 copy-done.10
  5.7 2.7 %summaries.1 = (f32[648,128]{1,0:T(8,128)S(1)}, f32[648,128]{1,0:T(8,128)S(1)}, f32[648,128]{1,0:T(8,128)S(1)}, f32[648,128]{1,0:T(8,128)S(1)}, f32[2592,128]{1,0:T(8,128)S(1)}) custom-call(s32[1]{0:T(128)} %bitcast.core_ref, f32[40,128]{1,0:T(8,128)S(1)} %bitcast.53, f32[1,40]{1,0:T(1,128)S(1)} %bitcast.55, bf16[128,2560]{1,0:T(8,128)(2,1)S(1)} %bitcast.20, ...), custom_call_target="tpu_custom_call" | custom-call | flops 400000000 | bytes 4000000 | tf_op jit(solution)/shard_map/summaries/pallas_call | solution.py:422
  8.4 8.8 %collective-permute-start = (f32[2592,128]{1,0:T(8,128)S(1)}, f32[2592,128]{1,0:T(8,128)S(1)}, u32[]{:S(2)}, u32[]{:S(2)}) collective-permute-start(f32[2592,128]{1,0:T(8,128)S(1)} %get-tuple-element.149), channel_id=1, source_target_pairs={{0,1},{1,0},{2,3},{3,2},{4,5},{5,4},{6,7},{7,6},{8,9},{9,8},{10,11... | collective-permute-start | bytes 3981320 | tf_op jit(solution)/shard_map/ppermute | solution.py:451
  17.2 1.4 within_slab.2
  18.6 1.2 collective-permute-done.refs_4_.rest_8_
  19.9 0.2 pair_up.1
  20.1 1.4 collective-permute-start.1
  21.5 1.3 collective-permute-start.2
  22.8 1.3 collective-permute-start.17
  24.1 1.3 collective-permute-start.9
  25.5 4.2 %within_slab.3 = (f32[128,1920]{1,0:T(8,128)S(1)}, f32[128,128]{1,0:T(8,128)S(1)}, f32[128,128]{1,0:T(8,128)S(1)}, f32[128,128]{1,0:T(8,128)S(1)}, f32[128,128]{1,0:T(8,128)S(1)}, /*index=5*/f32[1,128]{1,0:T(1,128)S(1)}) custom-call(bf16[128,2560]{1,0:T(8,128)(2,1)S(1)} %bitcast.22, bf16[128,2560]{1,0:T(8,128)(2,1)S(1)} %bitcast.29, ...), custom_call_target="tpu_custom_call" | custom-call | flops 1000000000 | bytes 3000000 | tf_op jit(solution)/shard_map/within_slab/pallas_call | solution.py:439
  29.7 0.7 collective-permute-start.25
  30.4 2.2 %collective-permute-done.17.refs_1_ = f32[648,128]{1,0:T(8,128)S(1)} collective-permute-done((f32[648,128]{1,0:T(8,128)S(1)}, f32[648,128]{1,0:T(8,128)S(1)}, u32[]{:S(2)}, u32[]{:S(2)}) %collective-permute-start.17) | collective-permute-done | bytes 331808 | tf_op jit(solution)/shard_map/ppermute | solution.py:377
  32.7 0.7 collective-permute-start.18
  33.4 2.8 %collective-permute-done.9.refs_1_ = f32[648,128]{1,0:T(8,128)S(1)} collective-permute-done((f32[648,128]{1,0:T(8,128)S(1)}, f32[648,128]{1,0:T(8,128)S(1)}, u32[]{:S(2)}, u32[]{:S(2)}) %collective-permute-start.9) | collective-permute-done | bytes 331808 | tf_op jit(solution)/shard_map/ppermute | solution.py:377
  36.3 0.7 collective-permute-start.10
  37.0 0.7 collective-permute-start.3
  37.8 0.7 collective-permute-start.26
  38.5 0.1 combine.41
  38.6 0.7 collective-permute-start.19
  39.3 0.1 combine.34
  39.3 0.7 collective-permute-start.11
  40.0 0.1 combine.29
  40.1 0.7 collective-permute-start.4
  40.8 0.1 combine.49
  40.9 0.7 collective-permute-start.27
  41.6 0.1 combine.42
  41.7 0.7 collective-permute-start.20
  42.4 0.7 collective-permute-start.12
  43.2 0.7 collective-permute-start.5
  44.0 0.7 collective-permute-start.28
  44.7 0.7 collective-permute-start.21
  45.4 0.1 combine.36
  45.5 0.7 collective-permute-start.13
  46.2 0.1 combine.31
  46.3 0.7 collective-permute-start.6
  47.0 0.1 combine.51
  47.1 0.7 collective-permute-start.29
  47.8 0.7 collective-permute-start.30
  48.5 0.1 combine.44
  48.6 0.7 collective-permute-start.22
  49.3 0.7 collective-permute-start.23
  49.9 0.1 combine.37
  50.0 0.7 collective-permute-start.14
  50.7 0.7 collective-permute-start.15
  51.5 52.3 %collective-permute-start.31 = (f32[648,128]{1,0:T(8,128)S(1)}, f32[648,128]{1,0:T(8,128)S(1)}, u32[]{:S(2)}, u32[]{:S(2)}) collective-permute-start(f32[648,128]{1,0:T(8,128)S(1)} %combine.53.rest_9_), channel_id=1, source_target_pairs={{0,1},{1,0},{2,3},{3,2},{4,5},{5,4},{6,7},{7,6},{8,9},{9,8},{10,11... | collective-permute-start | bytes 995336 | tf_op jit(solution)/shard_map/ppermute | solution.py:395
  104.0 6.9 %collective-permute-start.24 = (f32[648,128]{1,0:T(8,128)S(1)}, f32[648,128]{1,0:T(8,128)S(1)}, u32[]{:S(2)}, u32[]{:S(2)}) collective-permute-start(f32[648,128]{1,0:T(8,128)S(1)} %combine.46.rest_9_), channel_id=1, source_target_pairs={{0,1},{1,0},{2,3},{3,2},{4,5},{5,4},{6,7},{7,6},{8,9},{9,8},{10,11... | collective-permute-start | bytes 995336 | tf_op jit(solution)/shard_map/ppermute | solution.py:395
  111.0 7.0 %collective-permute-start.16 = (f32[648,128]{1,0:T(8,128)S(1)}, f32[648,128]{1,0:T(8,128)S(1)}, u32[]{:S(2)}, u32[]{:S(2)}) collective-permute-start(f32[648,128]{1,0:T(8,128)S(1)} %combine.39.rest_9_), channel_id=1, source_target_pairs={{0,1},{1,0},{2,3},{3,2},{4,5},{5,4},{6,7},{7,6},{8,9},{9,8},{10,11... | collective-permute-start | bytes 995336 | tf_op jit(solution)/shard_map/ppermute | solution.py:395
  118.1 0.7 collective-permute-start.7
  118.8 0.9 collective-permute-start.8
  119.7 1.4 gradients.4
  121.0 1.4 gradients.5
  122.4 1.4 gradients.6
  123.9 6.8 %collective-permute-start.32 = (f32[648,128]{1,0:T(8,128)S(1)}, f32[648,128]{1,0:T(8,128)S(1)}, u32[]{:S(2)}, u32[]{:S(2)}) collective-permute-start(f32[648,128]{1,0:T(8,128)S(1)} %combine.55.rest_9_), channel_id=1, source_target_pairs={{0,1},{1,0},{2,3},{3,2},{4,5},{5,4},{6,7},{7,6},{8,9},{9,8},{10,11... | collective-permute-start | bytes 995336 | tf_op jit(solution)/shard_map/ppermute | solution.py:395
  130.7 1.2 collective-permute-done.32.rest_10_
  132.0 2.4 %gradients.7 = (bf16[128,2560]{1,0:T(8,128)(2,1)}, f32[128,128]{1,0:T(8,128)}, f32[128,128]{1,0:T(8,128)}, f32[40,128]{1,0:T(8,128)}, f32[32,128]{1,0:T(8,128)S(1)}) custom-call(s32[1]{0:T(128)} %bitcast.core_ref, f32[1,40]{1,0:T(1,128)S(1)} %bitcast.52, bf16[128,2560]{1,0:T(8,128)(2,1)S(1)} %bitcast.26, bf16[128,2560]{1,0:T(8,128)(2,1)S(1)} %bitcast.33, ...), custom_call_target="tpu_custom_call" | custom-call | flops 800000000 | bytes 8000000 | tf_op jit(solution)/shard_map/gradients/pallas_call | solution.py:473
  134.3 18.3 %all_to_all.15 = f32[32,1,128]{2,1,0:T(1,128)S(1)} all-to-all(f32[32,1,128]{2,1,0:T(1,128)S(1)} %bitcast.48), channel_id=1, replica_groups=mesh['dp'=16,'ctx'=32] {'ctx'}, dimensions={0} | all-to-all | bytes 32768 | tf_op jit(solution)/shard_map/all_to_all | solution.py:486
  152.7 13.0 %all_to_all.16 = f32[16,1,128]{2,1,0:T(1,128)S(1)} all-to-all(f32[16,1,128]{2,1,0:T(1,128)S(1)} %broadcast_in_dim.22), channel_id=1, replica_groups=mesh['dp'=16,'ctx'=32] {'dp'}, dimensions={0} | all-to-all | bytes 16384 | tf_op jit(solution)/shard_map/all_to_all | solution.py:489
  165.7 0.6 fusion
  (66 shorter events, 1.1 us)
Async XLA Ops:
  0.6 1.1 copy-start
  1.7 1.1 copy-start.2
  2.8 0.8 copy-start.4
  3.6 0.8 copy-start.6
  4.3 0.7 copy-start.9
  5.1 0.7 copy-start.10
  8.4 11.5 %collective-permute-start = (f32[2592,128]{1,0:T(8,128)S(1)}, f32[2592,128]{1,0:T(8,128)S(1)}, u32[]{:S(2)}, u32[]{:S(2)}) collective-permute-start(f32[2592,128]{1,0:T(8,128)S(1)} %get-tuple-element.149), channel_id=1, source_target_pairs={{0,1},{1,0},{2,3},{3,2},{4,5},{5,4},{6,7},{7,6},{8,9},{9,8},{10,11... | collective-permute-start | bytes 3981320 | tf_op jit(solution)/shard_map/ppermute | solution.py:451
  19.9 5.6 %copy-start.1 = (bf16[1,128,2560]{2,1,0:T(8,128)(2,1)S(1)}, bf16[1,128,2560]{2,1,0:T(8,128)(2,1)}, u32[]{:S(2)}) copy-start(bf16[1,128,2560]{2,1,0:T(8,128)(2,1)} %param.7) | copy-start | bytes 1966084
  19.9 5.6 %copy-start.3 = (bf16[1,128,2560]{2,1,0:T(8,128)(2,1)S(1)}, bf16[1,128,2560]{2,1,0:T(8,128)(2,1)}, u32[]{:S(2)}) copy-start(bf16[1,128,2560]{2,1,0:T(8,128)(2,1)} %param.13) | copy-start | bytes 1966084
  19.9 5.6 %copy-start.5 = (bf16[1,128,128]{2,1,0:T(8,128)(2,1)S(1)}, bf16[1,128,128]{2,1,0:T(8,128)(2,1)}, u32[]{:S(2)}) copy-start(bf16[1,128,128]{2,1,0:T(8,128)(2,1)} %param.8) | copy-start | bytes 98308
  19.9 5.6 %copy-start.7 = (bf16[1,128,128]{2,1,0:T(8,128)(2,1)S(1)}, bf16[1,128,128]{2,1,0:T(8,128)(2,1)}, u32[]{:S(2)}) copy-start(bf16[1,128,128]{2,1,0:T(8,128)(2,1)} %param.9) | copy-start | bytes 98308
  20.1 9.6 %collective-permute-start.1 = (f32[648,128]{1,0:T(8,128)S(1)}, f32[648,128]{1,0:T(8,128)S(1)}, u32[]{:S(2)}, u32[]{:S(2)}) collective-permute-start(f32[648,128]{1,0:T(8,128)S(1)} %get-tuple-element.166.refs_0_), channel_id=1, source_target_pairs={{1,3},{5,7},{9,11},{13,15},{17,19},{21,23},{25,27},{29,31},{30,28}... | collective-permute-start | bytes 995336 | tf_op jit(solution)/shard_map/ppermute | solution.py:377
  21.5 15.4 %collective-permute-start.2 = (f32[648,128]{1,0:T(8,128)S(1)}, f32[648,128]{1,0:T(8,128)S(1)}, u32[]{:S(2)}, u32[]{:S(2)}) collective-permute-start(f32[648,128]{1,0:T(8,128)S(1)} %get-tuple-element.174.refs_0_), channel_id=1, source_target_pairs={{1,3},{5,7},{9,11},{13,15},{17,19},{21,23},{25,27},{29,31},{30,28}... | collective-permute-start | bytes 995336 | tf_op jit(solution)/shard_map/ppermute | solution.py:377
  22.8 9.8 %collective-permute-start.17 = (f32[648,128]{1,0:T(8,128)S(1)}, f32[648,128]{1,0:T(8,128)S(1)}, u32[]{:S(2)}, u32[]{:S(2)}) collective-permute-start(f32[648,128]{1,0:T(8,128)S(1)} %get-tuple-element.218.refs_0_), channel_id=1, source_target_pairs={{1,3},{5,7},{9,11},{13,15},{17,19},{21,23},{25,27},{29,31},{30,28}... | collective-permute-start | bytes 995336 | tf_op jit(solution)/shard_map/ppermute | solution.py:377
  24.1 12.1 %collective-permute-start.9 = (f32[648,128]{1,0:T(8,128)S(1)}, f32[648,128]{1,0:T(8,128)S(1)}, u32[]{:S(2)}, u32[]{:S(2)}) collective-permute-start(f32[648,128]{1,0:T(8,128)S(1)} %get-tuple-element.209.refs_0_), channel_id=1, source_target_pairs={{1,3},{5,7},{9,11},{13,15},{17,19},{21,23},{25,27},{29,31},{30,28}... | collective-permute-start | bytes 995336 | tf_op jit(solution)/shard_map/ppermute | solution.py:377
  29.7 8.0 %collective-permute-start.25 = (f32[648,128]{1,0:T(8,128)S(1)}, f32[648,128]{1,0:T(8,128)S(1)}, u32[]{:S(2)}, u32[]{:S(2)}) collective-permute-start(f32[648,128]{1,0:T(8,128)S(1)} %combine.47), channel_id=1, source_target_pairs={{3,7},{11,15},{19,23},{28,24},{20,16},{12,8},{35,39},{43,47},{51,5... | collective-permute-start | bytes 995336 | tf_op jit(solution)/shard_map/ppermute | solution.py:377
  32.7 5.8 %collective-permute-start.18 = (f32[648,128]{1,0:T(8,128)S(1)}, f32[648,128]{1,0:T(8,128)S(1)}, u32[]{:S(2)}, u32[]{:S(2)}) collective-permute-start(f32[648,128]{1,0:T(8,128)S(1)} %combine.40), channel_id=1, source_target_pairs={{3,7},{11,15},{19,23},{28,24},{20,16},{12,8},{35,39},{43,47},{51,5... | collective-permute-start | bytes 995336 | tf_op jit(solution)/shard_map/ppermute | solution.py:377
  36.3 3.0 %collective-permute-start.10 = (f32[648,128]{1,0:T(8,128)S(1)}, f32[648,128]{1,0:T(8,128)S(1)}, u32[]{:S(2)}, u32[]{:S(2)}) collective-permute-start(f32[648,128]{1,0:T(8,128)S(1)} %combine.33), channel_id=1, source_target_pairs={{3,7},{11,15},{19,23},{28,24},{20,16},{12,8},{35,39},{43,47},{51,5... | collective-permute-start | bytes 995336 | tf_op jit(solution)/shard_map/ppermute | solution.py:377
  37.0 3.0 %collective-permute-start.3 = (f32[648,128]{1,0:T(8,128)S(1)}, f32[648,128]{1,0:T(8,128)S(1)}, u32[]{:S(2)}, u32[]{:S(2)}) collective-permute-start(f32[648,128]{1,0:T(8,128)S(1)} %combine.28), channel_id=1, source_target_pairs={{3,7},{11,15},{19,23},{28,24},{20,16},{12,8},{35,39},{43,47},{51,5... | collective-permute-start | bytes 995336 | tf_op jit(solution)/shard_map/ppermute | solution.py:377
  37.8 3.0 %collective-permute-start.26 = (f32[648,128]{1,0:T(8,128)S(1)}, f32[648,128]{1,0:T(8,128)S(1)}, u32[]{:S(2)}, u32[]{:S(2)}) collective-permute-start(f32[648,128]{1,0:T(8,128)S(1)} %get-tuple-element.231), channel_id=1, source_target_pairs={{7,15},{3,5},{24,16},{28,26},{39,47},{35,37},{56,48},{60,58},{71,7... | collective-permute-start | bytes 995336 | tf_op jit(solution)/shard_map/ppermute | solution.py:377
  38.6 3.0 %collective-permute-start.19 = (f32[648,128]{1,0:T(8,128)S(1)}, f32[648,128]{1,0:T(8,128)S(1)}, u32[]{:S(2)}, u32[]{:S(2)}) collective-permute-start(f32[648,128]{1,0:T(8,128)S(1)} %get-tuple-element.220), channel_id=1, source_target_pairs={{7,15},{3,5},{24,16},{28,26},{39,47},{35,37},{56,48},{60,58},{71,7... | collective-permute-start | bytes 995336 | tf_op jit(solution)/shard_map/ppermute | solution.py:377
  39.3 3.0 %collective-permute-start.11 = (f32[648,128]{1,0:T(8,128)S(1)}, f32[648,128]{1,0:T(8,128)S(1)}, u32[]{:S(2)}, u32[]{:S(2)}) collective-permute-start(f32[648,128]{1,0:T(8,128)S(1)} %get-tuple-element.211), channel_id=1, source_target_pairs={{7,15},{3,5},{24,16},{28,26},{39,47},{35,37},{56,48},{60,58},{71,7... | collective-permute-start | bytes 995336 | tf_op jit(solution)/shard_map/ppermute | solution.py:377
  40.1 3.0 %collective-permute-start.4 = (f32[648,128]{1,0:T(8,128)S(1)}, f32[648,128]{1,0:T(8,128)S(1)}, u32[]{:S(2)}, u32[]{:S(2)}) collective-permute-start(f32[648,128]{1,0:T(8,128)S(1)} %get-tuple-element.202), channel_id=1, source_target_pairs={{7,15},{3,5},{24,16},{28,26},{39,47},{35,37},{56,48},{60,58},{71,7... | collective-permute-start | bytes 995336 | tf_op jit(solution)/shard_map/ppermute | solution.py:377
  40.9 3.0 %collective-permute-start.27 = (f32[648,128]{1,0:T(8,128)S(1)}, f32[648,128]{1,0:T(8,128)S(1)}, u32[]{:S(2)}, u32[]{:S(2)}) collective-permute-start(f32[648,128]{1,0:T(8,128)S(1)} %get-tuple-element.234), channel_id=1, source_target_pairs={{15,23},{7,11},{16,8},{24,20},{47,55},{39,43},{48,40},{56,52},{79,... | collective-permute-start | bytes 995336 | tf_op jit(solution)/shard_map/ppermute | solution.py:377
  41.7 3.0 %collective-permute-start.20 = (f32[648,128]{1,0:T(8,128)S(1)}, f32[648,128]{1,0:T(8,128)S(1)}, u32[]{:S(2)}, u32[]{:S(2)}) collective-permute-start(f32[648,128]{1,0:T(8,128)S(1)} %get-tuple-element.222), channel_id=1, source_target_pairs={{15,23},{7,11},{16,8},{24,20},{47,55},{39,43},{48,40},{56,52},{79,... | collective-permute-start | bytes 995336 | tf_op jit(solution)/shard_map/ppermute | solution.py:377
  42.4 3.0 %collective-permute-start.12 = (f32[648,128]{1,0:T(8,128)S(1)}, f32[648,128]{1,0:T(8,128)S(1)}, u32[]{:S(2)}, u32[]{:S(2)}) collective-permute-start(f32[648,128]{1,0:T(8,128)S(1)} %get-tuple-element.213), channel_id=1, source_target_pairs={{15,23},{7,11},{16,8},{24,20},{47,55},{39,43},{48,40},{56,52},{79,... | collective-permute-start | bytes 995336 | tf_op jit(solution)/shard_map/ppermute | solution.py:377
  43.2 3.0 %collective-permute-start.5 = (f32[648,128]{1,0:T(8,128)S(1)}, f32[648,128]{1,0:T(8,128)S(1)}, u32[]{:S(2)}, u32[]{:S(2)}) collective-permute-start(f32[648,128]{1,0:T(8,128)S(1)} %get-tuple-element.204), channel_id=1, source_target_pairs={{15,23},{7,11},{16,8},{24,20},{47,55},{39,43},{48,40},{56,52},{79,... | collective-permute-start | bytes 995336 | tf_op jit(solution)/shard_map/ppermute | solution.py:377
  44.0 3.0 %collective-permute-start.28 = (f32[648,128]{1,0:T(8,128)S(1)}, f32[648,128]{1,0:T(8,128)S(1)}, u32[]{:S(2)}, u32[]{:S(2)}) collective-permute-start(f32[648,128]{1,0:T(8,128)S(1)} %get-tuple-element.237), channel_id=1, source_target_pairs={{23,27},{15,19},{11,13},{7,9},{8,4},{16,12},{20,18},{24,22},{55,59... | collective-permute-start | bytes 995336 | tf_op jit(solution)/shard_map/ppermute | solution.py:377
  44.7 3.7 %collective-permute-start.21 = (f32[648,128]{1,0:T(8,128)S(1)}, f32[648,128]{1,0:T(8,128)S(1)}, u32[]{:S(2)}, u32[]{:S(2)}) collective-permute-start(f32[648,128]{1,0:T(8,128)S(1)} %get-tuple-element.224), channel_id=1, source_target_pairs={{23,27},{15,19},{11,13},{7,9},{8,4},{16,12},{20,18},{24,22},{55,59... | collective-permute-start | bytes 995336 | tf_op jit(solution)/shard_map/ppermute | solution.py:377
  45.5 3.7 %collective-permute-start.13 = (f32[648,128]{1,0:T(8,128)S(1)}, f32[648,128]{1,0:T(8,128)S(1)}, u32[]{:S(2)}, u32[]{:S(2)}) collective-permute-start(f32[648,128]{1,0:T(8,128)S(1)} %get-tuple-element.215), channel_id=1, source_target_pairs={{23,27},{15,19},{11,13},{7,9},{8,4},{16,12},{20,18},{24,22},{55,59... | collective-permute-start | bytes 995336 | tf_op jit(solution)/shard_map/ppermute | solution.py:377
  46.3 3.7 %collective-permute-start.6 = (f32[648,128]{1,0:T(8,128)S(1)}, f32[648,128]{1,0:T(8,128)S(1)}, u32[]{:S(2)}, u32[]{:S(2)}) collective-permute-start(f32[648,128]{1,0:T(8,128)S(1)} %get-tuple-element.206), channel_id=1, source_target_pairs={{23,27},{15,19},{11,13},{7,9},{8,4},{16,12},{20,18},{24,22},{55,59... | collective-permute-start | bytes 995336 | tf_op jit(solution)/shard_map/ppermute | solution.py:377
  47.1 3.6 %collective-permute-start.29 = (f32[648,128]{1,0:T(8,128)S(1)}, f32[648,128]{1,0:T(8,128)S(1)}, u32[]{:S(2)}, u32[]{:S(2)}) collective-permute-start(f32[648,128]{1,0:T(8,128)S(1)} %get-tuple-element.240), channel_id=1, source_target_pairs={{15,17},{19,21},{23,25},{27,29},{16,14},{12,10},{8,6},{4,2},{47,49... | collective-permute-start | bytes 995336 | tf_op jit(solution)/shard_map/ppermute | solution.py:377
  47.8 3.6 %collective-permute-start.30 = (f32[648,128]{1,0:T(8,128)S(1)}, f32[648,128]{1,0:T(8,128)S(1)}, u32[]{:S(2)}, u32[]{:S(2)}) collective-permute-start(f32[648,128]{1,0:T(8,128)S(1)} %get-tuple-element.240), channel_id=1, source_target_pairs={{27,31},{4,0},{59,63},{36,32},{91,95},{68,64},{123,127},{100,96},{... | collective-permute-start | bytes 995336 | tf_op jit(solution)/shard_map/ppermute | solution.py:379
  48.6 55.3 %collective-permute-start.22 = (f32[648,128]{1,0:T(8,128)S(1)}, f32[648,128]{1,0:T(8,128)S(1)}, u32[]{:S(2)}, u32[]{:S(2)}) collective-permute-start(f32[648,128]{1,0:T(8,128)S(1)} %get-tuple-element.226), channel_id=1, source_target_pairs={{15,17},{19,21},{23,25},{27,29},{16,14},{12,10},{8,6},{4,2},{47,49... | collective-permute-start | bytes 995336 | tf_op jit(solution)/shard_map/ppermute | solution.py:377
  49.3 54.6 %collective-permute-start.23 = (f32[648,128]{1,0:T(8,128)S(1)}, f32[648,128]{1,0:T(8,128)S(1)}, u32[]{:S(2)}, u32[]{:S(2)}) collective-permute-start(f32[648,128]{1,0:T(8,128)S(1)} %get-tuple-element.226), channel_id=1, source_target_pairs={{27,31},{4,0},{59,63},{36,32},{91,95},{68,64},{123,127},{100,96},{... | collective-permute-start | bytes 995336 | tf_op jit(solution)/shard_map/ppermute | solution.py:379
  50.0 60.9 %collective-permute-start.14 = (f32[648,128]{1,0:T(8,128)S(1)}, f32[648,128]{1,0:T(8,128)S(1)}, u32[]{:S(2)}, u32[]{:S(2)}) collective-permute-start(f32[648,128]{1,0:T(8,128)S(1)} %get-tuple-element.217), channel_id=1, source_target_pairs={{15,17},{19,21},{23,25},{27,29},{16,14},{12,10},{8,6},{4,2},{47,49... | collective-permute-start | bytes 995336 | tf_op jit(solution)/shard_map/ppermute | solution.py:377
  50.7 60.2 %collective-permute-start.15 = (f32[648,128]{1,0:T(8,128)S(1)}, f32[648,128]{1,0:T(8,128)S(1)}, u32[]{:S(2)}, u32[]{:S(2)}) collective-permute-start(f32[648,128]{1,0:T(8,128)S(1)} %get-tuple-element.217), channel_id=1, source_target_pairs={{27,31},{4,0},{59,63},{36,32},{91,95},{68,64},{123,127},{100,96},{... | collective-permute-start | bytes 995336 | tf_op jit(solution)/shard_map/ppermute | solution.py:379
  51.5 68.1 %collective-permute-start.31 = (f32[648,128]{1,0:T(8,128)S(1)}, f32[648,128]{1,0:T(8,128)S(1)}, u32[]{:S(2)}, u32[]{:S(2)}) collective-permute-start(f32[648,128]{1,0:T(8,128)S(1)} %combine.53.rest_9_), channel_id=1, source_target_pairs={{0,1},{1,0},{2,3},{3,2},{4,5},{5,4},{6,7},{7,6},{8,9},{9,8},{10,11... | collective-permute-start | bytes 995336 | tf_op jit(solution)/shard_map/ppermute | solution.py:395
  104.0 17.1 %collective-permute-start.24 = (f32[648,128]{1,0:T(8,128)S(1)}, f32[648,128]{1,0:T(8,128)S(1)}, u32[]{:S(2)}, u32[]{:S(2)}) collective-permute-start(f32[648,128]{1,0:T(8,128)S(1)} %combine.46.rest_9_), channel_id=1, source_target_pairs={{0,1},{1,0},{2,3},{3,2},{4,5},{5,4},{6,7},{7,6},{8,9},{9,8},{10,11... | collective-permute-start | bytes 995336 | tf_op jit(solution)/shard_map/ppermute | solution.py:395
  110.9 8.8 %copy-start.8 = (f32[40]{0:T(128)S(1)}, f32[40]{0:T(128)}, u32[]{:S(2)}) copy-start(f32[40]{0:T(128)} %param.12) | copy-start | bytes 484
  111.0 11.4 %collective-permute-start.16 = (f32[648,128]{1,0:T(8,128)S(1)}, f32[648,128]{1,0:T(8,128)S(1)}, u32[]{:S(2)}, u32[]{:S(2)}) collective-permute-start(f32[648,128]{1,0:T(8,128)S(1)} %combine.39.rest_9_), channel_id=1, source_target_pairs={{0,1},{1,0},{2,3},{3,2},{4,5},{5,4},{6,7},{7,6},{8,9},{9,8},{10,11... | collective-permute-start | bytes 995336 | tf_op jit(solution)/shard_map/ppermute | solution.py:395
  118.1 5.7 %collective-permute-start.7 = (f32[648,128]{1,0:T(8,128)S(1)}, f32[648,128]{1,0:T(8,128)S(1)}, u32[]{:S(2)}, u32[]{:S(2)}) collective-permute-start(f32[648,128]{1,0:T(8,128)S(1)} %get-tuple-element.208), channel_id=1, source_target_pairs={{15,17},{19,21},{23,25},{27,29},{16,14},{12,10},{8,6},{4,2},{47,49... | collective-permute-start | bytes 995336 | tf_op jit(solution)/shard_map/ppermute | solution.py:377
  118.8 5.0 %collective-permute-start.8 = (f32[648,128]{1,0:T(8,128)S(1)}, f32[648,128]{1,0:T(8,128)S(1)}, u32[]{:S(2)}, u32[]{:S(2)}) collective-permute-start(f32[648,128]{1,0:T(8,128)S(1)} %get-tuple-element.208), channel_id=1, source_target_pairs={{27,31},{4,0},{59,63},{36,32},{91,95},{68,64},{123,127},{100,96},{... | collective-permute-start | bytes 995336 | tf_op jit(solution)/shard_map/ppermute | solution.py:379
  123.9 8.0 %collective-permute-start.32 = (f32[648,128]{1,0:T(8,128)S(1)}, f32[648,128]{1,0:T(8,128)S(1)}, u32[]{:S(2)}, u32[]{:S(2)}) collective-permute-start(f32[648,128]{1,0:T(8,128)S(1)} %combine.55.rest_9_), channel_id=1, source_target_pairs={{0,1},{1,0},{2,3},{3,2},{4,5},{5,4},{6,7},{7,6},{8,9},{9,8},{10,11... | collective-permute-start | bytes 995336 | tf_op jit(solution)/shard_map/ppermute | solution.py:395

commit v5 on v4

--- a/solution.py
+++ b/solution.py
@@ -380,7 +380,7 @@
             arrived.append(got)
         if turn == 0:
             local = within(own[-1])
-            arrived[0], local = lax.optimization_barrier((arrived[0], local))
+            arrived[-1], local = lax.optimization_barrier((arrived[-1], local))
         if turn > 0:
             arrived[0], _ = lax.optimization_barrier((arrived[0], previous))
         previous = arrived[-1]

time: 167 us -> 161 us (0.964)
  starting transfers between devices: 104 us -> 97.4 us
    ppermute x4, starting transfers between devices: 73 us -> 66.7 us  [scan_chips(): other = lax.ppermute(past[stream], 'ctx', swap)]
where the time goes in v5:
time: 161 us; the launch traced here: 160 us
  starting transfers between devices  97.4 us (60%)
  blocking collectives  30.4 us (19%)
  Pallas kernels  16.6 us (10%)
  waiting for transfers between devices  8.07 us (5%)
  local copies, waits for them, and re-layouts  5.69 us (4%)
    ppermute x4, starting transfers between devices, scan_chips(): other = lax.ppermute(past[stream], 'ctx', swap)  66.7 us
    ppermute x24, starting transfers between devices, scan_chips(): got = [lax.ppermute(send[stream], 'ctx', chip_moves(moves, chips))]  19 us
    all_to_all x1, blocking collectives, per_device(): shared = lax.all_to_all(shared, 'ctx', 0, 0, tiled=True)  17.4 us
    all_to_all x1, blocking collectives, per_device(): line_sum = jnp.sum(lax.all_to_all(shared, 'dp', 0, 0, tiled=True), axis=0)  13 us
    ppermute x1, starting transfers between devices, per_device(): pair = lax.ppermute(sends, 'ctx', swap)  8.79 us
    pallas_call x4, Pallas kernels, gradients(): pl.pallas_call(functools.partial(gradient_kernel, heads, blocks, stream),...  6.47 us
    ppermute x24, waiting for transfers between devices, scan_chips(): got = [lax.ppermute(send[stream], 'ctx', chip_moves(moves, chips))]  5.57 us
    pallas_call x2, Pallas kernels, local_part(): pl.pallas_call(functools.partial(local_kernel, heads, blocks, part), out_...  5.56 us
  transfers between devices with their start and end apart: 33, of which 4 were waited for; matrix products, arithmetic and copies ran while one was open for 0% of the time, Pallas kernels for 7%

profile of v5, /device:TPU:1, one launch (start us, length us, event | category | flops | bytes accessed | tf_op | source)
XLA Modules:
  0.0 159.6 jit_solution(553034300511192789)
XLA Ops:
  0.6 1.1 copy-done
  1.7 1.1 copy-done.2
  2.8 0.8 copy-done.4
  3.6 0.8 copy-done.6
  4.3 0.7 copy-done.9
  5.1 0.7 copy-done.10
  5.7 2.7 %summaries.1 = (f32[648,128]{1,0:T(8,128)S(1)}, f32[648,128]{1,0:T(8,128)S(1)}, f32[648,128]{1,0:T(8,128)S(1)}, f32[648,128]{1,0:T(8,128)S(1)}, f32[2592,128]{1,0:T(8,128)S(1)}) custom-call(s32[1]{0:T(128)} %bitcast.core_ref, f32[40,128]{1,0:T(8,128)S(1)} %bitcast.53, f32[1,40]{1,0:T(1,128)S(1)} %bitcast.55, bf16[128,2560]{1,0:T(8,128)(2,1)S(1)} %bitcast.20, ...), custom_call_target="tpu_custom_call" | custom-call | flops 400000000 | bytes 4000000 | tf_op jit(solution)/shard_map/summaries/pallas_call | solution.py:422
  8.4 8.8 %collective-permute-start = (f32[2592,128]{1,0:T(8,128)S(1)}, f32[2592,128]{1,0:T(8,128)S(1)}, u32[]{:S(2)}, u32[]{:S(2)}) collective-permute-start(f32[2592,128]{1,0:T(8,128)S(1)} %get-tuple-element.149), channel_id=1, source_target_pairs={{0,1},{1,0},{2,3},{3,2},{4,5},{5,4},{6,7},{7,6},{8,9},{9,8},{10,11... | collective-permute-start | bytes 3981320 | tf_op jit(solution)/shard_map/ppermute | solution.py:451
  17.2 1.4 within_slab.2
  18.6 1.2 collective-permute-done.refs_4_.rest_8_
  19.9 0.2 pair_up.1
  20.1 1.3 collective-permute-start.24
  21.4 1.3 collective-permute-start.16
  22.7 1.3 collective-permute-start.8
  24.1 1.4 collective-permute-start.1
  25.6 0.7 collective-permute-start.25
  26.3 2.7 %collective-permute-done.16.refs_1_ = f32[648,128]{1,0:T(8,128)S(1)} collective-permute-done((f32[648,128]{1,0:T(8,128)S(1)}, f32[648,128]{1,0:T(8,128)S(1)}, u32[]{:S(2)}, u32[]{:S(2)}) %collective-permute-start.16) | collective-permute-done | bytes 331808 | tf_op jit(solution)/shard_map/ppermute | solution.py:377
  29.0 0.7 collective-permute-start.17
  29.7 2.8 %collective-permute-done.8.refs_1_ = f32[648,128]{1,0:T(8,128)S(1)} collective-permute-done((f32[648,128]{1,0:T(8,128)S(1)}, f32[648,128]{1,0:T(8,128)S(1)}, u32[]{:S(2)}, u32[]{:S(2)}) %collective-permute-start.8) | collective-permute-done | bytes 331808 | tf_op jit(solution)/shard_map/ppermute | solution.py:377
  32.6 0.7 collective-permute-start.9
  33.3 4.2 %within_slab.3 = (f32[128,1920]{1,0:T(8,128)S(1)}, f32[128,128]{1,0:T(8,128)S(1)}, f32[128,128]{1,0:T(8,128)S(1)}, f32[128,128]{1,0:T(8,128)S(1)}, f32[128,128]{1,0:T(8,128)S(1)}, /*index=5*/f32[1,128]{1,0:T(1,128)S(1)}) custom-call(bf16[128,2560]{1,0:T(8,128)(2,1)S(1)} %bitcast.22, bf16[128,2560]{1,0:T(8,128)(2,1)S(1)} %bitcast.29, ...), custom_call_target="tpu_custom_call" | custom-call | flops 1000000000 | bytes 3000000 | tf_op jit(solution)/shard_map/within_slab/pallas_call | solution.py:439
  37.5 0.7 collective-permute-start.2
  38.2 0.1 combine.48
  38.3 0.7 collective-permute-start.26
  39.0 0.1 combine.41
  39.1 0.7 collective-permute-start.18
  39.8 0.1 combine.34
  39.8 0.7 collective-permute-start.10
  40.5 0.1 combine.29
  40.6 0.7 collective-permute-start.3
  41.4 0.7 collective-permute-start.27
  42.1 0.1 combine.42
  42.2 0.7 collective-permute-start.19
  42.9 0.7 collective-permute-start.11
  43.7 0.7 collective-permute-start.4
  44.5 0.7 collective-permute-start.28
  45.3 0.7 collective-permute-start.20
  46.0 0.1 combine.36
  46.0 0.7 collective-permute-start.12
  46.7 0.1 combine.31
  46.8 0.7 collective-permute-start.5
  47.5 0.1 combine.51
  47.6 0.7 collective-permute-start.29
  48.3 0.7 collective-permute-start.30
  49.0 0.1 combine.44
  49.1 0.7 collective-permute-start.21
  49.8 0.7 collective-permute-start.22
  50.5 0.1 combine.37
  50.5 0.7 collective-permute-start.13
  51.2 0.7 collective-permute-start.14
  52.0 46.0 %collective-permute-start.31 = (f32[648,128]{1,0:T(8,128)S(1)}, f32[648,128]{1,0:T(8,128)S(1)}, u32[]{:S(2)}, u32[]{:S(2)}) collective-permute-start(f32[648,128]{1,0:T(8,128)S(1)} %combine.53.rest_9_), channel_id=1, source_target_pairs={{0,1},{1,0},{2,3},{3,2},{4,5},{5,4},{6,7},{7,6},{8,9},{9,8},{10,11... | collective-permute-start | bytes 995336 | tf_op jit(solution)/shard_map/ppermute | solution.py:395
  98.2 6.9 %collective-permute-start.23 = (f32[648,128]{1,0:T(8,128)S(1)}, f32[648,128]{1,0:T(8,128)S(1)}, u32[]{:S(2)}, u32[]{:S(2)}) collective-permute-start(f32[648,128]{1,0:T(8,128)S(1)} %combine.46.rest_9_), channel_id=1, source_target_pairs={{0,1},{1,0},{2,3},{3,2},{4,5},{5,4},{6,7},{7,6},{8,9},{9,8},{10,11... | collective-permute-start | bytes 995336 | tf_op jit(solution)/shard_map/ppermute | solution.py:395
  105.3 7.0 %collective-permute-start.15 = (f32[648,128]{1,0:T(8,128)S(1)}, f32[648,128]{1,0:T(8,128)S(1)}, u32[]{:S(2)}, u32[]{:S(2)}) collective-permute-start(f32[648,128]{1,0:T(8,128)S(1)} %combine.39.rest_9_), channel_id=1, source_target_pairs={{0,1},{1,0},{2,3},{3,2},{4,5},{5,4},{6,7},{7,6},{8,9},{9,8},{10,11... | collective-permute-start | bytes 995336 | tf_op jit(solution)/shard_map/ppermute | solution.py:395
  112.3 0.7 collective-permute-start.6
  113.0 0.9 collective-permute-start.7
  113.9 1.4 gradients.4
  115.3 1.4 gradients.5
  116.6 1.4 gradients.6
  118.1 6.8 %collective-permute-start.32 = (f32[648,128]{1,0:T(8,128)S(1)}, f32[648,128]{1,0:T(8,128)S(1)}, u32[]{:S(2)}, u32[]{:S(2)}) collective-permute-start(f32[648,128]{1,0:T(8,128)S(1)} %combine.55.rest_9_), channel_id=1, source_target_pairs={{0,1},{1,0},{2,3},{3,2},{4,5},{5,4},{6,7},{7,6},{8,9},{9,8},{10,11... | collective-permute-start | bytes 995336 | tf_op jit(solution)/shard_map/ppermute | solution.py:395
  124.9 1.2 collective-permute-done.32.rest_10_
  126.2 2.4 %gradients.7 = (bf16[128,2560]{1,0:T(8,128)(2,1)}, f32[128,128]{1,0:T(8,128)}, f32[128,128]{1,0:T(8,128)}, f32[40,128]{1,0:T(8,128)}, f32[32,128]{1,0:T(8,128)S(1)}) custom-call(s32[1]{0:T(128)} %bitcast.core_ref, f32[1,40]{1,0:T(1,128)S(1)} %bitcast.52, bf16[128,2560]{1,0:T(8,128)(2,1)S(1)} %bitcast.26, bf16[128,2560]{1,0:T(8,128)(2,1)S(1)} %bitcast.33, ...), custom_call_target="tpu_custom_call" | custom-call | flops 800000000 | bytes 8000000 | tf_op jit(solution)/shard_map/gradients/pallas_call | solution.py:473
  128.5 17.4 %all_to_all.15 = f32[32,1,128]{2,1,0:T(1,128)S(1)} all-to-all(f32[32,1,128]{2,1,0:T(1,128)S(1)} %bitcast.48), channel_id=1, replica_groups=mesh['dp'=16,'ctx'=32] {'ctx'}, dimensions={0} | all-to-all | bytes 32768 | tf_op jit(solution)/shard_map/all_to_all | solution.py:486
  146.0 13.0 %all_to_all.16 = f32[16,1,128]{2,1,0:T(1,128)S(1)} all-to-all(f32[16,1,128]{2,1,0:T(1,128)S(1)} %broadcast_in_dim.22), channel_id=1, replica_groups=mesh['dp'=16,'ctx'=32] {'dp'}, dimensions={0} | all-to-all | bytes 16384 | tf_op jit(solution)/shard_map/all_to_all | solution.py:489
  159.0 0.6 fusion
  (66 shorter events, 1.1 us)
Async XLA Ops:
  0.6 1.1 copy-start
  1.7 1.1 copy-start.2
  2.8 0.8 copy-start.4
  3.6 0.8 copy-start.6
  4.3 0.7 copy-start.9
  5.1 0.7 copy-start.10
  8.4 11.5 %collective-permute-start = (f32[2592,128]{1,0:T(8,128)S(1)}, f32[2592,128]{1,0:T(8,128)S(1)}, u32[]{:S(2)}, u32[]{:S(2)}) collective-permute-start(f32[2592,128]{1,0:T(8,128)S(1)} %get-tuple-element.149), channel_id=1, source_target_pairs={{0,1},{1,0},{2,3},{3,2},{4,5},{5,4},{6,7},{7,6},{8,9},{9,8},{10,11... | collective-permute-start | bytes 3981320 | tf_op jit(solution)/shard_map/ppermute | solution.py:451
  20.1 5.5 %collective-permute-start.24 = (f32[648,128]{1,0:T(8,128)S(1)}, f32[648,128]{1,0:T(8,128)S(1)}, u32[]{:S(2)}, u32[]{:S(2)}) collective-permute-start(f32[648,128]{1,0:T(8,128)S(1)} %get-tuple-element.228.refs_0_), channel_id=1, source_target_pairs={{1,3},{5,7},{9,11},{13,15},{17,19},{21,23},{25,27},{29,31},{30,28}... | collective-permute-start | bytes 995336 | tf_op jit(solution)/shard_map/ppermute | solution.py:377
  21.4 7.6 %collective-permute-start.16 = (f32[648,128]{1,0:T(8,128)S(1)}, f32[648,128]{1,0:T(8,128)S(1)}, u32[]{:S(2)}, u32[]{:S(2)}) collective-permute-start(f32[648,128]{1,0:T(8,128)S(1)} %get-tuple-element.218.refs_0_), channel_id=1, source_target_pairs={{1,3},{5,7},{9,11},{13,15},{17,19},{21,23},{25,27},{29,31},{30,28}... | collective-permute-start | bytes 995336 | tf_op jit(solution)/shard_map/ppermute | solution.py:377
  22.7 9.8 %collective-permute-start.8 = (f32[648,128]{1,0:T(8,128)S(1)}, f32[648,128]{1,0:T(8,128)S(1)}, u32[]{:S(2)}, u32[]{:S(2)}) collective-permute-start(f32[648,128]{1,0:T(8,128)S(1)} %get-tuple-element.209.refs_0_), channel_id=1, source_target_pairs={{1,3},{5,7},{9,11},{13,15},{17,19},{21,23},{25,27},{29,31},{30,28}... | collective-permute-start | bytes 995336 | tf_op jit(solution)/shard_map/ppermute | solution.py:377
  24.0 9.2 %copy-start.1 = (bf16[1,128,2560]{2,1,0:T(8,128)(2,1)S(1)}, bf16[1,128,2560]{2,1,0:T(8,128)(2,1)}, u32[]{:S(2)}) copy-start(bf16[1,128,2560]{2,1,0:T(8,128)(2,1)} %param.7) | copy-start | bytes 1966084
  24.0 9.2 %copy-start.3 = (bf16[1,128,2560]{2,1,0:T(8,128)(2,1)S(1)}, bf16[1,128,2560]{2,1,0:T(8,128)(2,1)}, u32[]{:S(2)}) copy-start(bf16[1,128,2560]{2,1,0:T(8,128)(2,1)} %param.13) | copy-start | bytes 1966084
  24.0 9.2 %copy-start.5 = (bf16[1,128,128]{2,1,0:T(8,128)(2,1)S(1)}, bf16[1,128,128]{2,1,0:T(8,128)(2,1)}, u32[]{:S(2)}) copy-start(bf16[1,128,128]{2,1,0:T(8,128)(2,1)} %param.8) | copy-start | bytes 98308
  24.1 9.2 %copy-start.7 = (bf16[1,128,128]{2,1,0:T(8,128)(2,1)S(1)}, bf16[1,128,128]{2,1,0:T(8,128)(2,1)}, u32[]{:S(2)}) copy-start(bf16[1,128,128]{2,1,0:T(8,128)(2,1)} %param.9) | copy-start | bytes 98308
  24.1 13.4 %collective-permute-start.1 = (f32[648,128]{1,0:T(8,128)S(1)}, f32[648,128]{1,0:T(8,128)S(1)}, u32[]{:S(2)}, u32[]{:S(2)}) collective-permute-start(f32[648,128]{1,0:T(8,128)S(1)} %get-tuple-element.166.refs_0_), channel_id=1, source_target_pairs={{1,3},{5,7},{9,11},{13,15},{17,19},{21,23},{25,27},{29,31},{30,28}... | collective-permute-start | bytes 995336 | tf_op jit(solution)/shard_map/ppermute | solution.py:377
  25.6 12.6 %collective-permute-start.25 = (f32[648,128]{1,0:T(8,128)S(1)}, f32[648,128]{1,0:T(8,128)S(1)}, u32[]{:S(2)}, u32[]{:S(2)}) collective-permute-start(f32[648,128]{1,0:T(8,128)S(1)} %combine.47), channel_id=1, source_target_pairs={{3,7},{11,15},{19,23},{28,24},{20,16},{12,8},{35,39},{43,47},{51,5... | collective-permute-start | bytes 995336 | tf_op jit(solution)/shard_map/ppermute | solution.py:377
  29.0 10.0 %collective-permute-start.17 = (f32[648,128]{1,0:T(8,128)S(1)}, f32[648,128]{1,0:T(8,128)S(1)}, u32[]{:S(2)}, u32[]{:S(2)}) collective-permute-start(f32[648,128]{1,0:T(8,128)S(1)} %combine.40), channel_id=1, source_target_pairs={{3,7},{11,15},{19,23},{28,24},{20,16},{12,8},{35,39},{43,47},{51,5... | collective-permute-start | bytes 995336 | tf_op jit(solution)/shard_map/ppermute | solution.py:377
  32.6 7.2 %collective-permute-start.9 = (f32[648,128]{1,0:T(8,128)S(1)}, f32[648,128]{1,0:T(8,128)S(1)}, u32[]{:S(2)}, u32[]{:S(2)}) collective-permute-start(f32[648,128]{1,0:T(8,128)S(1)} %combine.33), channel_id=1, source_target_pairs={{3,7},{11,15},{19,23},{28,24},{20,16},{12,8},{35,39},{43,47},{51,5... | collective-permute-start | bytes 995336 | tf_op jit(solution)/shard_map/ppermute | solution.py:377
  37.5 3.0 %collective-permute-start.2 = (f32[648,128]{1,0:T(8,128)S(1)}, f32[648,128]{1,0:T(8,128)S(1)}, u32[]{:S(2)}, u32[]{:S(2)}) collective-permute-start(f32[648,128]{1,0:T(8,128)S(1)} %combine.28), channel_id=1, source_target_pairs={{3,7},{11,15},{19,23},{28,24},{20,16},{12,8},{35,39},{43,47},{51,5... | collective-permute-start | bytes 995336 | tf_op jit(solution)/shard_map/ppermute | solution.py:377
  38.3 3.0 %collective-permute-start.26 = (f32[648,128]{1,0:T(8,128)S(1)}, f32[648,128]{1,0:T(8,128)S(1)}, u32[]{:S(2)}, u32[]{:S(2)}) collective-permute-start(f32[648,128]{1,0:T(8,128)S(1)} %get-tuple-element.231), channel_id=1, source_target_pairs={{7,15},{3,5},{24,16},{28,26},{39,47},{35,37},{56,48},{60,58},{71,7... | collective-permute-start | bytes 995336 | tf_op jit(solution)/shard_map/ppermute | solution.py:377
  39.1 3.0 %collective-permute-start.18 = (f32[648,128]{1,0:T(8,128)S(1)}, f32[648,128]{1,0:T(8,128)S(1)}, u32[]{:S(2)}, u32[]{:S(2)}) collective-permute-start(f32[648,128]{1,0:T(8,128)S(1)} %get-tuple-element.220), channel_id=1, source_target_pairs={{7,15},{3,5},{24,16},{28,26},{39,47},{35,37},{56,48},{60,58},{71,7... | collective-permute-start | bytes 995336 | tf_op jit(solution)/shard_map/ppermute | solution.py:377
  39.8 3.0 %collective-permute-start.10 = (f32[648,128]{1,0:T(8,128)S(1)}, f32[648,128]{1,0:T(8,128)S(1)}, u32[]{:S(2)}, u32[]{:S(2)}) collective-permute-start(f32[648,128]{1,0:T(8,128)S(1)} %get-tuple-element.211), channel_id=1, source_target_pairs={{7,15},{3,5},{24,16},{28,26},{39,47},{35,37},{56,48},{60,58},{71,7... | collective-permute-start | bytes 995336 | tf_op jit(solution)/shard_map/ppermute | solution.py:377
  40.6 3.0 %collective-permute-start.3 = (f32[648,128]{1,0:T(8,128)S(1)}, f32[648,128]{1,0:T(8,128)S(1)}, u32[]{:S(2)}, u32[]{:S(2)}) collective-permute-start(f32[648,128]{1,0:T(8,128)S(1)} %get-tuple-element.202), channel_id=1, source_target_pairs={{7,15},{3,5},{24,16},{28,26},{39,47},{35,37},{56,48},{60,58},{71,7... | collective-permute-start | bytes 995336 | tf_op jit(solution)/shard_map/ppermute | solution.py:377
  41.4 3.0 %collective-permute-start.27 = (f32[648,128]{1,0:T(8,128)S(1)}, f32[648,128]{1,0:T(8,128)S(1)}, u32[]{:S(2)}, u32[]{:S(2)}) collective-permute-start(f32[648,128]{1,0:T(8,128)S(1)} %get-tuple-element.234), channel_id=1, source_target_pairs={{15,23},{7,11},{16,8},{24,20},{47,55},{39,43},{48,40},{56,52},{79,... | collective-permute-start | bytes 995336 | tf_op jit(solution)/shard_map/ppermute | solution.py:377
  42.2 3.0 %collective-permute-start.19 = (f32[648,128]{1,0:T(8,128)S(1)}, f32[648,128]{1,0:T(8,128)S(1)}, u32[]{:S(2)}, u32[]{:S(2)}) collective-permute-start(f32[648,128]{1,0:T(8,128)S(1)} %get-tuple-element.222), channel_id=1, source_target_pairs={{15,23},{7,11},{16,8},{24,20},{47,55},{39,43},{48,40},{56,52},{79,... | collective-permute-start | bytes 995336 | tf_op jit(solution)/shard_map/ppermute | solution.py:377
  42.9 3.0 %collective-permute-start.11 = (f32[648,128]{1,0:T(8,128)S(1)}, f32[648,128]{1,0:T(8,128)S(1)}, u32[]{:S(2)}, u32[]{:S(2)}) collective-permute-start(f32[648,128]{1,0:T(8,128)S(1)} %get-tuple-element.213), channel_id=1, source_target_pairs={{15,23},{7,11},{16,8},{24,20},{47,55},{39,43},{48,40},{56,52},{79,... | collective-permute-start | bytes 995336 | tf_op jit(solution)/shard_map/ppermute | solution.py:377
  43.7 3.0 %collective-permute-start.4 = (f32[648,128]{1,0:T(8,128)S(1)}, f32[648,128]{1,0:T(8,128)S(1)}, u32[]{:S(2)}, u32[]{:S(2)}) collective-permute-start(f32[648,128]{1,0:T(8,128)S(1)} %get-tuple-element.204), channel_id=1, source_target_pairs={{15,23},{7,11},{16,8},{24,20},{47,55},{39,43},{48,40},{56,52},{79,... | collective-permute-start | bytes 995336 | tf_op jit(solution)/shard_map/ppermute | solution.py:377
  44.5 3.0 %collective-permute-start.28 = (f32[648,128]{1,0:T(8,128)S(1)}, f32[648,128]{1,0:T(8,128)S(1)}, u32[]{:S(2)}, u32[]{:S(2)}) collective-permute-start(f32[648,128]{1,0:T(8,128)S(1)} %get-tuple-element.237), channel_id=1, source_target_pairs={{23,27},{15,19},{11,13},{7,9},{8,4},{16,12},{20,18},{24,22},{55,59... | collective-permute-start | bytes 995336 | tf_op jit(solution)/shard_map/ppermute | solution.py:377
  45.3 3.7 %collective-permute-start.20 = (f32[648,128]{1,0:T(8,128)S(1)}, f32[648,128]{1,0:T(8,128)S(1)}, u32[]{:S(2)}, u32[]{:S(2)}) collective-permute-start(f32[648,128]{1,0:T(8,128)S(1)} %get-tuple-element.224), channel_id=1, source_target_pairs={{23,27},{15,19},{11,13},{7,9},{8,4},{16,12},{20,18},{24,22},{55,59... | collective-permute-start | bytes 995336 | tf_op jit(solution)/shard_map/ppermute | solution.py:377
  46.0 3.7 %collective-permute-start.12 = (f32[648,128]{1,0:T(8,128)S(1)}, f32[648,128]{1,0:T(8,128)S(1)}, u32[]{:S(2)}, u32[]{:S(2)}) collective-permute-start(f32[648,128]{1,0:T(8,128)S(1)} %get-tuple-element.215), channel_id=1, source_target_pairs={{23,27},{15,19},{11,13},{7,9},{8,4},{16,12},{20,18},{24,22},{55,59... | collective-permute-start | bytes 995336 | tf_op jit(solution)/shard_map/ppermute | solution.py:377
  46.8 3.7 %collective-permute-start.5 = (f32[648,128]{1,0:T(8,128)S(1)}, f32[648,128]{1,0:T(8,128)S(1)}, u32[]{:S(2)}, u32[]{:S(2)}) collective-permute-start(f32[648,128]{1,0:T(8,128)S(1)} %get-tuple-element.206), channel_id=1, source_target_pairs={{23,27},{15,19},{11,13},{7,9},{8,4},{16,12},{20,18},{24,22},{55,59... | collective-permute-start | bytes 995336 | tf_op jit(solution)/shard_map/ppermute | solution.py:377
  47.6 3.6 %collective-permute-start.29 = (f32[648,128]{1,0:T(8,128)S(1)}, f32[648,128]{1,0:T(8,128)S(1)}, u32[]{:S(2)}, u32[]{:S(2)}) collective-permute-start(f32[648,128]{1,0:T(8,128)S(1)} %get-tuple-element.240), channel_id=1, source_target_pairs={{15,17},{19,21},{23,25},{27,29},{16,14},{12,10},{8,6},{4,2},{47,49... | collective-permute-start | bytes 995336 | tf_op jit(solution)/shard_map/ppermute | solution.py:377
  48.3 3.6 %collective-permute-start.30 = (f32[648,128]{1,0:T(8,128)S(1)}, f32[648,128]{1,0:T(8,128)S(1)}, u32[]{:S(2)}, u32[]{:S(2)}) collective-permute-start(f32[648,128]{1,0:T(8,128)S(1)} %get-tuple-element.240), channel_id=1, source_target_pairs={{27,31},{4,0},{59,63},{36,32},{91,95},{68,64},{123,127},{100,96},{... | collective-permute-start | bytes 995336 | tf_op jit(solution)/shard_map/ppermute | solution.py:379
  49.1 49.0 %collective-permute-start.21 = (f32[648,128]{1,0:T(8,128)S(1)}, f32[648,128]{1,0:T(8,128)S(1)}, u32[]{:S(2)}, u32[]{:S(2)}) collective-permute-start(f32[648,128]{1,0:T(8,128)S(1)} %get-tuple-element.226), channel_id=1, source_target_pairs={{15,17},{19,21},{23,25},{27,29},{16,14},{12,10},{8,6},{4,2},{47,49... | collective-permute-start | bytes 995336 | tf_op jit(solution)/shard_map/ppermute | solution.py:377
  49.8 48.3 %collective-permute-start.22 = (f32[648,128]{1,0:T(8,128)S(1)}, f32[648,128]{1,0:T(8,128)S(1)}, u32[]{:S(2)}, u32[]{:S(2)}) collective-permute-start(f32[648,128]{1,0:T(8,128)S(1)} %get-tuple-element.226), channel_id=1, source_target_pairs={{27,31},{4,0},{59,63},{36,32},{91,95},{68,64},{123,127},{100,96},{... | collective-permute-start | bytes 995336 | tf_op jit(solution)/shard_map/ppermute | solution.py:379
  50.5 54.6 %collective-permute-start.13 = (f32[648,128]{1,0:T(8,128)S(1)}, f32[648,128]{1,0:T(8,128)S(1)}, u32[]{:S(2)}, u32[]{:S(2)}) collective-permute-start(f32[648,128]{1,0:T(8,128)S(1)} %get-tuple-element.217), channel_id=1, source_target_pairs={{15,17},{19,21},{23,25},{27,29},{16,14},{12,10},{8,6},{4,2},{47,49... | collective-permute-start | bytes 995336 | tf_op jit(solution)/shard_map/ppermute | solution.py:377
  51.2 54.0 %collective-permute-start.14 = (f32[648,128]{1,0:T(8,128)S(1)}, f32[648,128]{1,0:T(8,128)S(1)}, u32[]{:S(2)}, u32[]{:S(2)}) collective-permute-start(f32[648,128]{1,0:T(8,128)S(1)} %get-tuple-element.217), channel_id=1, source_target_pairs={{27,31},{4,0},{59,63},{36,32},{91,95},{68,64},{123,127},{100,96},{... | collective-permute-start | bytes 995336 | tf_op jit(solution)/shard_map/ppermute | solution.py:379
  52.0 61.8 %collective-permute-start.31 = (f32[648,128]{1,0:T(8,128)S(1)}, f32[648,128]{1,0:T(8,128)S(1)}, u32[]{:S(2)}, u32[]{:S(2)}) collective-permute-start(f32[648,128]{1,0:T(8,128)S(1)} %combine.53.rest_9_), channel_id=1, source_target_pairs={{0,1},{1,0},{2,3},{3,2},{4,5},{5,4},{6,7},{7,6},{8,9},{9,8},{10,11... | collective-permute-start | bytes 995336 | tf_op jit(solution)/shard_map/ppermute | solution.py:395
  98.2 17.1 %collective-permute-start.23 = (f32[648,128]{1,0:T(8,128)S(1)}, f32[648,128]{1,0:T(8,128)S(1)}, u32[]{:S(2)}, u32[]{:S(2)}) collective-permute-start(f32[648,128]{1,0:T(8,128)S(1)} %combine.46.rest_9_), channel_id=1, source_target_pairs={{0,1},{1,0},{2,3},{3,2},{4,5},{5,4},{6,7},{7,6},{8,9},{9,8},{10,11... | collective-permute-start | bytes 995336 | tf_op jit(solution)/shard_map/ppermute | solution.py:395
  105.1 8.8 %copy-start.8 = (f32[40]{0:T(128)S(1)}, f32[40]{0:T(128)}, u32[]{:S(2)}) copy-start(f32[40]{0:T(128)} %param.12) | copy-start | bytes 484
  105.3 11.4 %collective-permute-start.15 = (f32[648,128]{1,0:T(8,128)S(1)}, f32[648,128]{1,0:T(8,128)S(1)}, u32[]{:S(2)}, u32[]{:S(2)}) collective-permute-start(f32[648,128]{1,0:T(8,128)S(1)} %combine.39.rest_9_), channel_id=1, source_target_pairs={{0,1},{1,0},{2,3},{3,2},{4,5},{5,4},{6,7},{7,6},{8,9},{9,8},{10,11... | collective-permute-start | bytes 995336 | tf_op jit(solution)/shard_map/ppermute | solution.py:395
  112.3 5.7 %collective-permute-start.6 = (f32[648,128]{1,0:T(8,128)S(1)}, f32[648,128]{1,0:T(8,128)S(1)}, u32[]{:S(2)}, u32[]{:S(2)}) collective-permute-start(f32[648,128]{1,0:T(8,128)S(1)} %get-tuple-element.208), channel_id=1, source_target_pairs={{15,17},{19,21},{23,25},{27,29},{16,14},{12,10},{8,6},{4,2},{47,49... | collective-permute-start | bytes 995336 | tf_op jit(solution)/shard_map/ppermute | solution.py:377
  113.0 5.0 %collective-permute-start.7 = (f32[648,128]{1,0:T(8,128)S(1)}, f32[648,128]{1,0:T(8,128)S(1)}, u32[]{:S(2)}, u32[]{:S(2)}) collective-permute-start(f32[648,128]{1,0:T(8,128)S(1)} %get-tuple-element.208), channel_id=1, source_target_pairs={{27,31},{4,0},{59,63},{36,32},{91,95},{68,64},{123,127},{100,96},{... | collective-permute-start | bytes 995336 | tf_op jit(solution)/shard_map/ppermute | solution.py:379
  118.1 8.0 %collective-permute-start.32 = (f32[648,128]{1,0:T(8,128)S(1)}, f32[648,128]{1,0:T(8,128)S(1)}, u32[]{:S(2)}, u32[]{:S(2)}) collective-permute-start(f32[648,128]{1,0:T(8,128)S(1)} %combine.55.rest_9_), channel_id=1, source_target_pairs={{0,1},{1,0},{2,3},{3,2},{4,5},{5,4},{6,7},{7,6},{8,9},{9,8},{10,11... | collective-permute-start | bytes 995336 | tf_op jit(solution)/shard_map/ppermute | solution.py:395
